TPU v7x, 128 devices: a whole 4x4x4 slice. The times are simulated.
128 devices in a mesh: expert: 32 (over x, z, core), tensor: 4 (over y).
Axes of the slice: x: 4, y: 4, z: 4, core: 2. Of those that a mesh axis runs over, the one named last changes fastest.
Arguments:
- tokens: bfloat16 [4096, 768], P('expert'), may hold values from -6 to 6
- segment_ids: int32 [32, 128], P('expert'), may hold values from 0 to 7, never falling along the last dimension, each value on 1 to 64 neighbouring positions
- expert_routes: int32 [2, 4096, 2], P(None, 'expert'), may hold values from 0 to 31, all different within a row; in each aligned block of 128 rows (0 to 127, 128 to 255, ..., all dimensions but the last counted through in order) at most 11 rows name the same one
- bucket_ids: int32 [255], replicated, may hold values from 0 to 31
- proj_qkv: bfloat16 [2, 3, 768, 768], P(None, None, None, 'tensor'), may hold values from -0.21875 to 0.21875
- proj_out: bfloat16 [2, 768, 768], P(None, 'tensor'), may hold values from -0.625 to 0.625
- bias_table: float32 [2, 32, 12], P(None, None, 'tensor'), may hold values from -4 to 4
- norm_gains: float32 [2, 2, 768], replicated, may hold values from 0.5 to 1.5
- router: bfloat16 [2, 768, 32], replicated, may hold values from -0.15625 to 0.15625
- expert_in: bfloat16 [2, 32, 768, 3072], P(None, 'expert', None, 'tensor'), may hold values from -0.21875 to 0.21875
- expert_out: bfloat16 [2, 32, 3072, 768], P(None, 'expert', 'tensor'), may hold values from -0.15625 to 0.15625
- cotangent: bfloat16 [4096, 768], P('expert'), may hold values from -6 to 6
Outputs:
- output: bfloat16 [4096, 768], P('expert')
- tokens_grad: float32 [4096, 768], P('expert')
- qkv_grad: float32 [2, 3, 768, 768], P(None, None, None, 'tensor')
- out_grad: float32 [2, 768, 768], P(None, 'tensor')
- table_grad: float32 [2, 32, 12], P(None, None, 'tensor')
- gains_grad: float32 [2, 2, 768], replicated
- router_grad: float32 [2, 768, 32], replicated
- expert_in_grad: float32 [2, 32, 768, 3072], P(None, 'expert', None, 'tensor')
- expert_out_grad: float32 [2, 32, 3072, 768], P(None, 'expert', 'tensor')
Inputs may be any that keep to these rules, and one draw needn't show every extreme that they name: `expert_routes`: in each layer, no expert is named by more than 11 tokens of one packed row, a bound that some block reaches. `segment_ids`: within a row document numbers never fall; a document holds at most 64 tokens.
All inputs are finite; a program needn't handle non-finite values.
Results may differ from a plain program's by a relative error of at most 0.02.
Values may be sent and summed in bfloat16 or wider, within the bound.
No kernel may reach another device: no remote copies, remote signals or barrier semaphores. Data moves between devices by JAX's collectives and lax.ppermute only.
A program may use at most 128 MiB of HBM per device.

v0:
```python
import jax
import jax.numpy as jnp
from jax import lax
from jax.sharding import PartitionSpec as P

epsilon = 1e-06
masked_score = -1000000000.0
highest = lax.Precision.HIGHEST


def norm_rows(values, gain_row):
    return (
        values * lax.rsqrt(jnp.mean(values * values, axis=-1, keepdims=True) + epsilon) * gain_row
    )


def slot_tables(routes_here, experts, capacity):
    labels = jnp.arange(experts, dtype=jnp.int32)
    first_hot = (routes_here[:, 0:1] == labels).astype(jnp.float32)
    second_hot = (routes_here[:, 1:2] == labels).astype(jnp.float32)
    token_order = jnp.arange(routes_here.shape[0], dtype=jnp.int32)
    before = (token_order[None, :] < token_order[:, None]).astype(jnp.float32)
    counts = jnp.dot(
        before, first_hot + second_hot, precision=highest, preferred_element_type=jnp.float32
    )
    places = jnp.arange(capacity, dtype=jnp.float32)
    tables = []
    for chosen_hot in (first_hot, second_hot):
        slot_place = jnp.sum(counts * chosen_hot, axis=1, keepdims=True)
        table_part = chosen_hot[:, :, None] * (slot_place[:, :, None] == places).astype(jnp.float32)
        tables.append(table_part.reshape(routes_here.shape[0], experts * capacity))
    return (first_hot, second_hot, jnp.stack(tables).astype(jnp.bfloat16))


def bias_rows(table_part, bucket_ids, row_count):
    position = jnp.arange(row_count, dtype=jnp.int32)
    offsets = position[:, None] - position[None, :] + row_count - 1
    picked_ids = jnp.take(bucket_ids, offsets)
    labels = jnp.arange(table_part.shape[0], dtype=jnp.int32)
    bucket_hot = (picked_ids[:, :, None] == labels).astype(jnp.float32)
    return jnp.einsum("tsb,bh->hts", bucket_hot, table_part, precision=highest)


def score_rows(queries, keys, position_bias, allowed, score_scale):
    raw = (
        jnp.einsum("thc,shc->hts", queries, keys, preferred_element_type=jnp.float32) * score_scale
        + position_bias
    )
    return jnp.where(allowed[None], raw, masked_score)


def head_total(partial_rows):
    return lax.psum(partial_rows, "tensor")


def to_owner(slot_buffer):
    return lax.all_to_all(slot_buffer, "expert", split_axis=0, concat_axis=1, tiled=True)


def send_back(partial_rows):
    summed = lax.psum(partial_rows, "tensor").astype(jnp.bfloat16)
    return lax.all_to_all(summed, "expert", split_axis=1, concat_axis=0, tiled=True)


def shards(
    tokens,
    segment_ids,
    expert_routes,
    bucket_ids,
    proj_qkv,
    proj_out,
    bias_table,
    norm_gains,
    router,
    expert_in,
    expert_out,
    cotangent,
):
    row_count, model_width = tokens.shape
    layer_count = proj_qkv.shape[0]
    heads_here = bias_table.shape[2]
    quarter = proj_qkv.shape[3]
    head_size = quarter // heads_here
    experts = router.shape[2]
    capacity = max(2, row_count * 10 // (4 * experts) + 1)
    score_scale = head_size ** (-0.5)
    position = jnp.arange(row_count, dtype=jnp.int32)
    segment_row = segment_ids[0]
    allowed = (segment_row[:, None] == segment_row[None, :]) & (
        position[None, :] <= position[:, None]
    )
    current = tokens.astype(jnp.float32)
    kept_values = []
    for layer_index in range(layer_count):
        gain_pair = norm_gains[layer_index]
        low_one = norm_rows(current, gain_pair[0]).astype(jnp.bfloat16)
        triple = jnp.einsum(
            "td,kde->kte", low_one, proj_qkv[layer_index], preferred_element_type=jnp.float32
        ).astype(jnp.bfloat16)
        triple = triple.reshape(3, row_count, heads_here, head_size)
        position_bias = bias_rows(bias_table[layer_index], bucket_ids, row_count)
        scores = score_rows(triple[0], triple[1], position_bias, allowed, score_scale)
        log_total = jax.nn.logsumexp(scores, axis=-1, keepdims=True)
        weights_low = jnp.exp(scores - log_total).astype(jnp.bfloat16)
        mixture = (
            jnp.einsum("hts,shc->thc", weights_low, triple[2], preferred_element_type=jnp.float32)
            .reshape(row_count, quarter)
            .astype(jnp.bfloat16)
        )
        attention = head_total(
            jnp.dot(mixture, proj_out[layer_index], preferred_element_type=jnp.float32)
        )
        middle = current + attention
        low_two = norm_rows(middle, gain_pair[1]).astype(jnp.bfloat16)
        logits = jnp.dot(low_two, router[layer_index], preferred_element_type=jnp.float32)
        first_hot, second_hot, tables_low = slot_tables(
            expert_routes[layer_index], experts, capacity
        )
        chosen = jnp.stack(
            [jnp.sum(logits * first_hot, axis=1), jnp.sum(logits * second_hot, axis=1)], axis=1
        )
        gates = jax.nn.softmax(chosen, axis=1)
        outgoing = jnp.einsum(
            "ktc,td->cd", tables_low, low_two, preferred_element_type=jnp.float32
        ).astype(jnp.bfloat16)
        arrived = to_owner(outgoing.reshape(experts, capacity, model_width))
        hidden_pre = jnp.einsum(
            "erd,edf->erf", arrived, expert_in[layer_index], preferred_element_type=jnp.float32
        )
        activated = jax.nn.gelu(hidden_pre).astype(jnp.bfloat16)
        partial_out = jnp.einsum(
            "erf,efd->erd", activated, expert_out[layer_index], preferred_element_type=jnp.float32
        )
        returned = send_back(partial_out).reshape(experts * capacity, model_width)
        picked = jnp.einsum("ktc,cd->ktd", tables_low, returned, preferred_element_type=jnp.float32)
        kept_values.append(
            (
                current,
                low_one,
                triple,
                log_total,
                mixture,
                middle,
                low_two,
                first_hot,
                second_hot,
                tables_low,
                gates,
                picked,
                arrived,
                hidden_pre,
                activated,
            )
        )
        current = middle + gates[:, 0:1] * picked[0] + gates[:, 1:2] * picked[1]
    gradient = cotangent.astype(jnp.float32)
    grads_qkv, grads_out, grads_table, grads_gain, grads_router, grads_in, grads_back = (
        [],
        [],
        [],
        [],
        [],
        [],
        [],
    )
    for layer_index in reversed(range(layer_count)):
        (
            layer_input,
            low_one,
            triple,
            log_total,
            mixture,
            middle,
            low_two,
            first_hot,
            second_hot,
            tables_low,
            gates,
            picked,
            arrived,
            hidden_pre,
            activated,
        ) = kept_values[layer_index]
        gain_pair = norm_gains[layer_index]
        grad_gate = jnp.stack(
            [jnp.sum(gradient * picked[0], axis=1), jnp.sum(gradient * picked[1], axis=1)], axis=1
        )
        grad_chosen = gates * (grad_gate - jnp.sum(gates * grad_gate, axis=1, keepdims=True))
        grad_logits = grad_chosen[:, 0:1] * first_hot + grad_chosen[:, 1:2] * second_hot
        router_wide = router[layer_index].astype(jnp.float32)
        grad_router = jnp.dot(
            low_two.astype(jnp.float32).T,
            grad_logits,
            precision=highest,
            preferred_element_type=jnp.float32,
        )
        grad_low_two = jnp.dot(
            grad_logits, router_wide.T, precision=highest, preferred_element_type=jnp.float32
        )
        weighted = jnp.stack([gates[:, 0:1] * gradient, gates[:, 1:2] * gradient]).astype(
            jnp.bfloat16
        )
        grad_sent = jnp.einsum(
            "ktc,ktd->cd", tables_low, weighted, preferred_element_type=jnp.float32
        ).astype(jnp.bfloat16)
        grad_arrived = to_owner(grad_sent.reshape(experts, capacity, model_width))
        grad_expert_out = jnp.einsum(
            "erf,erd->efd", activated, grad_arrived, preferred_element_type=jnp.float32
        )
        grad_activated = jnp.einsum(
            "erd,efd->erf",
            grad_arrived,
            expert_out[layer_index],
            preferred_element_type=jnp.float32,
        )
        grad_pre = jax.vjp(jax.nn.gelu, hidden_pre)[1](grad_activated)[0].astype(jnp.bfloat16)
        grad_expert_in = jnp.einsum(
            "erd,erf->edf", arrived, grad_pre, preferred_element_type=jnp.float32
        )
        grad_rows_part = jnp.einsum(
            "erf,edf->erd", grad_pre, expert_in[layer_index], preferred_element_type=jnp.float32
        )
        grad_back = send_back(grad_rows_part).reshape(experts * capacity, model_width)
        grad_low_two = grad_low_two + jnp.einsum(
            "ktc,cd->td", tables_low, grad_back, preferred_element_type=jnp.float32
        )
        grad_middle, grad_gain_two = jax.vjp(norm_rows, middle, gain_pair[1])[1](grad_low_two)
        gradient = gradient + grad_middle
        grad_attention = gradient.astype(jnp.bfloat16)
        grad_proj_out = jnp.einsum(
            "tf,td->fd", mixture, grad_attention, preferred_element_type=jnp.float32
        )
        grad_mixture = (
            jnp.einsum(
                "td,fd->tf",
                grad_attention,
                proj_out[layer_index],
                preferred_element_type=jnp.float32,
            )
            .astype(jnp.bfloat16)
            .reshape(row_count, heads_here, head_size)
        )
        position_bias, bias_pull = jax.vjp(
            lambda table_part: bias_rows(table_part, bucket_ids, row_count), bias_table[layer_index]
        )
        scores = score_rows(triple[0], triple[1], position_bias, allowed, score_scale)
        weights_full = jnp.exp(scores - log_total)
        weights_low = weights_full.astype(jnp.bfloat16)
        grad_values = jnp.einsum(
            "hts,thc->shc", weights_low, grad_mixture, preferred_element_type=jnp.float32
        )
        grad_weights = jnp.einsum(
            "thc,shc->hts", grad_mixture, triple[2], preferred_element_type=jnp.float32
        )
        grad_scores = (
            weights_full
            * (grad_weights - jnp.sum(weights_full * grad_weights, axis=-1, keepdims=True))
        ).astype(jnp.bfloat16)
        grad_table = bias_pull(grad_scores.astype(jnp.float32))[0]
        grad_queries = (
            jnp.einsum("hts,shc->thc", grad_scores, triple[1], preferred_element_type=jnp.float32)
            * score_scale
        )
        grad_keys = (
            jnp.einsum("hts,thc->shc", grad_scores, triple[0], preferred_element_type=jnp.float32)
            * score_scale
        )
        grad_triple = (
            jnp.stack([grad_queries, grad_keys, grad_values])
            .astype(jnp.bfloat16)
            .reshape(3, row_count, quarter)
        )
        grad_proj_qkv = jnp.einsum(
            "td,kte->kde", low_one, grad_triple, preferred_element_type=jnp.float32
        )
        grad_low_one = head_total(
            jnp.einsum(
                "kte,kde->td",
                grad_triple,
                proj_qkv[layer_index],
                preferred_element_type=jnp.float32,
            )
        )
        grad_input, grad_gain_one = jax.vjp(norm_rows, layer_input, gain_pair[0])[1](grad_low_one)
        gradient = gradient + grad_input
        grads_qkv.insert(0, grad_proj_qkv)
        grads_out.insert(0, grad_proj_out)
        grads_table.insert(0, grad_table)
        grads_gain.insert(0, jnp.stack([grad_gain_one, grad_gain_two]))
        grads_router.insert(0, grad_router)
        grads_in.insert(0, grad_expert_in)
        grads_back.insert(0, grad_expert_out)
    summed = lax.psum(
        (
            jnp.stack(grads_qkv),
            jnp.stack(grads_out),
            jnp.stack(grads_table),
            jnp.stack(grads_gain),
            jnp.stack(grads_router),
        ),
        "expert",
    )
    return (
        current.astype(jnp.bfloat16),
        gradient,
        summed[0],
        summed[1],
        summed[2],
        summed[3],
        summed[4],
        jnp.stack(grads_in),
        jnp.stack(grads_back),
    )


def solution(mesh):
    placed = (
        P("expert", None),
        P("expert", None),
        P(None, "expert", None),
        P(),
        P(None, None, None, "tensor"),
        P(None, "tensor", None),
        P(None, None, "tensor"),
        P(),
        P(),
        P(None, "expert", None, "tensor"),
        P(None, "expert", "tensor", None),
        P("expert", None),
    )
    return jax.shard_map(
        shards,
        mesh=mesh,
        in_specs=placed,
        out_specs=(
            P("expert", None),
            P("expert", None),
            P(None, None, None, "tensor"),
            P(None, "tensor", None),
            P(None, None, "tensor"),
            P(),
            P(),
            P(None, "expert", None, "tensor"),
            P(None, "expert", "tensor", None),
        ),
        check_vma=False,
    )
```

profile of v0, /device:TPU:1, one launch (start us, length us, event | category | flops | bytes accessed | tf_op | source)
XLA Modules:
  0.0 785.3 jit_solution(2969295934219564094)
XLA Ops:
  7.3 2.5 fusion.196
  11.2 101.4 %gather_fusion = s32[16384]{0:T(1024)S(1)} fusion(s32[255]{0:T(256)S(1)} %copy-done, s32[16384]{0:T(1024)S(1)} %bitcast_clamp_fusion), kind=kCustom, calls=%fused_computation.clone | custom fusion | bytes 196608 | tf_op jit(solution)/shard_map/jit(_take)/gather | solution.py:38
  117.6 42.9 %all-reduce.12.cloned.1.call-done = f32[128,768]{1,0:T(8,128)} async-done(((f32[128,768]{1,0:T(8,128)}), f32[128,768]{1,0:T(8,128)}) %all-reduce.12.cloned.1.call-update) | async-done | bytes 393232 | tf_op jit(solution)/shard_map/psum | solution.py:53
  164.9 10.0 %all-to-all-start = ((bf16[32,11,768]{2,1,0:T(8,128)(2,1)}), bf16[32,11,768]{2,1,0:T(8,128)(2,1)}, u32[]{:S(2)}, u32[]{:S(2)}) async-start(bf16[32,11,768]{2,1,0:T(8,128)(2,1)} %reshape.713), calls=%async_computation | async-start | bytes 1572864 | tf_op jit(solution)/shard_map/all_to_all | solution.py:57
  177.4 11.9 %all-to-all-done = bf16[32,11,768]{2,1,0:T(8,128)(2,1)} async-done(((bf16[32,11,768]{2,1,0:T(8,128)(2,1)}), bf16[32,11,768]{2,1,0:T(8,128)(2,1)}, u32[]{:S(2)}, u32[]{:S(2)}) %all-to-all-start) | async-done | bytes 540704 | tf_op jit(solution)/shard_map/all_to_all | solution.py:57
  189.2 2.2 reshape.714
  195.9 28.3 %all-reduce.21 = bf16[1,352,768]{2,1,0:T(8,128)(2,1)} all-reduce(f32[1,352,768]{2,1,0:T(8,128)} %convolution_bitcast_fusion.11), channel_id=1, replica_groups=mesh['expert'=32,'tensor'=4] {'tensor'}, use_global_device_ids=true, to_apply=%region_11.13 | all-reduce | flops 270336 | bytes 1622016 | tf_op jit(solution)/shard_map/psum | solution.py:61
  224.2 2.9 copy.126
  227.6 5.6 reduce.12
  235.3 8.6 %all-to-all-start.1 = ((bf16[32,2,4224]{2,1,0:T(2,128)(2,1)}), bf16[32,2,4224]{2,1,0:T(2,128)(2,1)}, u32[]{:S(2)}, u32[]{:S(2)}) async-start(bf16[32,2,4224]{2,1,0:T(2,128)(2,1)} %reshape.773), calls=%async_computation.1 | async-start | bytes 1081344 | tf_op jit(solution)/shard_map/all_to_all | solution.py:62
  244.3 11.4 %all-to-all-done.1 = bf16[32,2,4224]{2,1,0:T(2,128)(2,1)} async-done(((bf16[32,2,4224]{2,1,0:T(2,128)(2,1)}), bf16[32,2,4224]{2,1,0:T(2,128)(2,1)}, u32[]{:S(2)}, u32[]{:S(2)}) %all-to-all-start.1) | async-done | bytes 540704 | tf_op jit(solution)/shard_map/all_to_all | solution.py:62
  255.7 4.5 reshape.774
  266.6 35.2 %all-reduce.14.cloned.1.call-done = f32[128,768]{1,0:T(8,128)} async-done(((f32[128,768]{1,0:T(8,128)}), f32[128,768]{1,0:T(8,128)}) %all-reduce.14.cloned.1.call-update) | async-done | bytes 393232 | tf_op jit(solution)/shard_map/psum | solution.py:53
  317.8 2.1 reshape.718
  319.9 10.0 %all-to-all-start.2 = ((bf16[32,11,768]{2,1,0:T(8,128)(2,1)}), bf16[32,11,768]{2,1,0:T(8,128)(2,1)}, u32[]{:S(2)}, u32[]{:S(2)}) async-start(bf16[32,11,768]{2,1,0:T(8,128)(2,1)} %reshape.718), calls=%async_computation.2 | async-start | bytes 1572864 | tf_op jit(solution)/shard_map/all_to_all | solution.py:57
  335.4 2.1 reshape.723
  337.6 6.6 all-to-all-done.2
  344.2 4.4 all-to-all-start.4
  348.6 2.2 reshape.719
  355.3 7.4 all-to-all-done.4
  362.7 2.1 reshape.724
  364.8 2.7 fusion.41
  370.0 43.2 %all-reduce.22 = (bf16[1,352,768]{2,1,0:T(8,128)(2,1)}, bf16[1,352,768]{2,1,0:T(8,128)(2,1)}) all-reduce(f32[1,352,768]{2,1,0:T(8,128)} %convolution_bitcast_fusion.10, f32[1,352,768]{2,1,0:T(8,128)} %convolution_bitcast_fusion.9), channel_id=1, replica_groups=mesh['expert'=32,'tensor'=4] {'tensor'}, use_global_device_ids=true, to_apply=%region_23.25 | all-reduce | flops 540672 | bytes 3244032 | tf_op jit(solution)/shard_map/psum | solution.py:61
  413.2 2.9 copy.125
  416.0 5.6 reduce.13
  423.7 6.8 all-to-all-start.3
  430.5 2.9 copy.124
  433.3 5.6 reduce.14
  442.4 6.1 all-to-all-start.5
  448.8 4.5 reshape.776
  456.5 3.9 all-to-all-done.5
  460.4 4.5 reshape.778
  472.8 36.1 %all-reduce.16.cloned.1.call-done = f32[128,768]{1,0:T(8,128)} async-done(((f32[128,768]{1,0:T(8,128)}), f32[128,768]{1,0:T(8,128)}) %all-reduce.16.cloned.1.call-update) | async-done | bytes 393232 | tf_op jit(solution)/shard_map/psum | solution.py:53
  514.6 2.1 reshape.727
  516.7 9.9 %all-to-all-start.6 = ((bf16[32,11,768]{2,1,0:T(8,128)(2,1)}), bf16[32,11,768]{2,1,0:T(8,128)(2,1)}, u32[]{:S(2)}, u32[]{:S(2)}) async-start(bf16[32,11,768]{2,1,0:T(8,128)(2,1)} %reshape.727), calls=%async_computation.6 | async-start | bytes 1572864 | tf_op jit(solution)/shard_map/all_to_all | solution.py:57
  526.6 3.8 convolution_bitcast_fusion
  534.1 6.7 all-to-all-done.6
  540.8 2.2 reshape.728
  543.0 2.7 fusion.34
  548.3 28.1 %all-reduce.23 = bf16[1,352,768]{2,1,0:T(8,128)(2,1)S(1)} all-reduce(f32[1,352,768]{2,1,0:T(8,128)} %convolution_bitcast_fusion.8), channel_id=1, replica_groups=mesh['expert'=32,'tensor'=4] {'tensor'}, use_global_device_ids=true, to_apply=%region_35.37 | all-reduce | flops 270336 | bytes 1622016 | tf_op jit(solution)/shard_map/psum | solution.py:61
  577.2 3.8 reduce.15
  582.2 8.6 %all-to-all-start.7 = ((bf16[32,2,4224]{2,1,0:T(2,128)(2,1)}), bf16[32,2,4224]{2,1,0:T(2,128)(2,1)S(1)}, u32[]{:S(2)}, u32[]{:S(2)}) async-start(bf16[32,2,4224]{2,1,0:T(2,128)(2,1)} %reshape.779), calls=%async_computation.7 | async-start | bytes 1081344 | tf_op jit(solution)/shard_map/all_to_all | solution.py:62
  591.9 10.7 %all-to-all-done.7 = bf16[32,2,4224]{2,1,0:T(2,128)(2,1)S(1)} async-done(((bf16[32,2,4224]{2,1,0:T(2,128)(2,1)}), bf16[32,2,4224]{2,1,0:T(2,128)(2,1)S(1)}, u32[]{:S(2)}, u32[]{:S(2)}) %all-to-all-start.7) | async-done | bytes 540704 | tf_op jit(solution)/shard_map/all_to_all | solution.py:62
  621.1 2.5 pad_maximum_fusion
  625.2 2.5 pad_maximum_fusion.1
  628.4 15.7 %all-reduce.18.cloned.1.call-done = f32[128,768]{1,0:T(8,128)} async-done(((f32[128,768]{1,0:T(8,128)}), f32[128,768]{1,0:T(8,128)}) %all-reduce.18.cloned.1.call-update) | async-done | bytes 393232 | tf_op jit(solution)/shard_map/psum | solution.py:53
  645.3 124.6 %all-reduce = (f32[2,32,3]{1,2,0:T(4,128)S(1)}, f32[2,2,768]{2,1,0:T(2,128)}) all-reduce(f32[2,32,3]{1,2,0:T(4,128)S(1)} %pad_maximum_fusion.12, f32[2,2,768]{2,1,0:T(2,128)S(1)} %pad_maximum_fusion.11), channel_id=1, replica_groups=mesh['expert'=32,'tensor'=4] {'expert'}, use_global_device_ids=true, to_apply=%region_42.44 | all-reduce | flops 3264 | bytes 26112 | tf_op jit(solution)/shard_map/psum | solution.py:293
  772.4 4.3 copy.144
  (463 shorter events, 112.1 us)
Async XLA Ops:
  7.2 153.2 %all-reduce.12.cloned.1.call-start = ((), (), s32[]{:S(2)}) async-start(), calls=%async_computation.8 | async-start | bytes 786432 | tf_op jit(solution)/shard_map/psum | solution.py:53
  10.4 151.2 %copy-start.81 = (f32[768]{0:T(1024)}, f32[768]{0:T(1024)S(1)}, u32[]{:S(2)}) copy-start(f32[768]{0:T(1024)S(1)} %get-tuple-element.67) | copy-start | bytes 9220
  11.1 103.1 %copy-start.63 = (bf16[1,128,192]{1,2,0:T(8,128)(2,1)}, bf16[1,128,192]{1,2,0:T(8,128)(2,1)S(1)}, u32[]{:S(2)}) copy-start(bf16[1,128,192]{1,2,0:T(8,128)(2,1)S(1)} %get-tuple-element.98) | copy-start | bytes 147460
  11.1 103.1 %copy-start.65 = (bf16[1,128,192]{1,2,0:T(8,128)(2,1)}, bf16[1,128,192]{1,2,0:T(8,128)(2,1)S(1)}, u32[]{:S(2)}) copy-start(bf16[1,128,192]{1,2,0:T(8,128)(2,1)S(1)} %get-tuple-element.99) | copy-start | bytes 147460
  11.2 103.5 %copy-start.59 = (bf16[1,128,192]{1,2,0:T(8,128)(2,1)}, bf16[1,128,192]{1,2,0:T(8,128)(2,1)S(1)}, u32[]{:S(2)}) copy-start(bf16[1,128,192]{1,2,0:T(8,128)(2,1)S(1)} %get-tuple-element.100) | copy-start | bytes 147460
  11.2 101.4 %copy-start.135 = (f32[2,32,3]{1,0,2:T(2,128)S(1)}, f32[2,32,3]{1,0,2:T(2,128)}, u32[]{:S(2)}) copy-start(f32[2,32,3]{1,0,2:T(2,128)} %param.20) | copy-start | bytes 2308
  114.6 47.0 %copy-start.87 = (f32[3,128]{1,0:T(4,128)}, f32[3,128]{1,0:T(4,128)S(1)}, u32[]{:S(2)}) copy-start(f32[3,128]{1,0:T(4,128)S(1)} %log_add_fusion.1) | copy-start | bytes 4612
  116.9 44.8 %copy-start.71 = (bf16[2,768,32]{1,2,0:T(8,128)(2,1)S(1)}, bf16[2,768,32]{1,2,0:T(8,128)(2,1)}, u32[]{:S(2)}) copy-start(bf16[2,768,32]{1,2,0:T(8,128)(2,1)} %param.22) | copy-start | bytes 294916
  117.6 45.0 %copy-start.94 = (s32[128]{0:T(128)}, s32[128]{0:T(128)S(1)}, u32[]{:S(2)}) copy-start(s32[128]{0:T(128)S(1)} %get-tuple-element.116) | copy-start | bytes 1540
  117.6 45.1 %copy-start.92 = (s32[128]{0:T(128)}, s32[128]{0:T(128)S(1)}, u32[]{:S(2)}) copy-start(s32[128]{0:T(128)S(1)} %get-tuple-element.115) | copy-start | bytes 1540
  162.8 97.3 %copy-start.31 = (bf16[2,128,352]{1,2,0:T(8,128)(2,1)}, bf16[2,128,352]{1,2,0:T(8,128)(2,1)S(1)}, u32[]{:S(2)}) copy-start(bf16[2,128,352]{1,2,0:T(8,128)(2,1)S(1)} %constant_dynamic-update-slice_fusion) | copy-start | bytes 540676
  163.8 11.1 %copy-start.138 = (f32[1,32,3]{1,0,2:T(1,128)S(1)}, f32[1,32,3]{1,0,2:T(1,128)}, u32[]{:S(2)}) copy-start(f32[1,32,3]{1,0,2:T(1,128)} %get-tuple-element.101) | copy-start | bytes 1156
  164.9 12.4 %copy-start.98 = (f32[128]{0:T(128)S(1)}, f32[128]{0:T(128)}, u32[]{:S(2)}) copy-start(f32[128]{0:T(128)} %get-tuple-element.70) | copy-start | bytes 1540
  164.9 12.4 %copy-start.100 = (f32[128]{0:T(128)S(1)}, f32[128]{0:T(128)}, u32[]{:S(2)}) copy-start(f32[128]{0:T(128)} %get-tuple-element.71) | copy-start | bytes 1540
  164.9 26.4 %copy-start.2 = (bf16[2,1,768,768]{3,2,1,0:T(8,128)(2,1)S(1)}, bf16[2,1,768,768]{3,2,1,0:T(8,128)(2,1)}, u32[]{:S(2)}) copy-start(bf16[2,1,768,768]{3,2,1,0:T(8,128)(2,1)} %param.23) | copy-start | bytes 7077892
  164.9 24.3 %all-to-all-start = ((bf16[32,11,768]{2,1,0:T(8,128)(2,1)}), bf16[32,11,768]{2,1,0:T(8,128)(2,1)}, u32[]{:S(2)}, u32[]{:S(2)}) async-start(bf16[32,11,768]{2,1,0:T(8,128)(2,1)} %reshape.713), calls=%async_computation | async-start | bytes 1572864 | tf_op jit(solution)/shard_map/all_to_all | solution.py:57
  177.3 66.9 %copy-start.103 = (f32[128]{0:T(128)}, f32[128]{0:T(128)S(1)}, u32[]{:S(2)}) copy-start(f32[128]{0:T(128)S(1)} %reduce_max.39) | copy-start | bytes 1540
  235.3 20.4 %all-to-all-start.1 = ((bf16[32,2,4224]{2,1,0:T(2,128)(2,1)}), bf16[32,2,4224]{2,1,0:T(2,128)(2,1)}, u32[]{:S(2)}, u32[]{:S(2)}) async-start(bf16[32,2,4224]{2,1,0:T(2,128)(2,1)} %reshape.773), calls=%async_computation.1 | async-start | bytes 1081344 | tf_op jit(solution)/shard_map/all_to_all | solution.py:62
  243.9 58.0 %all-reduce.14.cloned.1.call-start = ((), (), s32[]{:S(2)}) async-start(), calls=%async_computation.9 | async-start | bytes 786432 | tf_op jit(solution)/shard_map/psum | solution.py:53
  244.2 17.6 %copy-start.106 = (f32[128]{0:T(128)}, f32[128]{0:T(128)S(1)}, u32[]{:S(2)}) copy-start(f32[128]{0:T(128)S(1)} %fusion.191) | copy-start | bytes 1540
  244.3 17.6 %copy-start.114 = (f32[128]{0:T(128)}, f32[128]{0:T(128)S(1)}, u32[]{:S(2)}) copy-start(f32[128]{0:T(128)S(1)} %get-tuple-element.113) | copy-start | bytes 1540
  244.3 17.6 %copy-start.116 = (f32[128]{0:T(128)}, f32[128]{0:T(128)S(1)}, u32[]{:S(2)}) copy-start(f32[128]{0:T(128)S(1)} %get-tuple-element.114) | copy-start | bytes 1540
  264.9 38.6 %copy-start.83 = (f32[768]{0:T(1024)S(1)}, f32[768]{0:T(1024)}, u32[]{:S(2)}) copy-start(f32[768]{0:T(1024)} %get-tuple-element.66) | copy-start | bytes 9220
  266.0 39.2 %copy-start.96 = (s32[128]{0:T(128)}, s32[128]{0:T(128)S(1)}, u32[]{:S(2)}) copy-start(s32[128]{0:T(128)S(1)} %get-tuple-element.112) | copy-start | bytes 1540
  319.9 10.0 %copy-start.109 = (f32[128]{0:T(128)S(1)}, f32[128]{0:T(128)}, u32[]{:S(2)}) copy-start(f32[128]{0:T(128)} %get-tuple-element.72) | copy-start | bytes 1540
  319.9 24.3 %all-to-all-start.2 = ((bf16[32,11,768]{2,1,0:T(8,128)(2,1)}), bf16[32,11,768]{2,1,0:T(8,128)(2,1)}, u32[]{:S(2)}, u32[]{:S(2)}) async-start(bf16[32,11,768]{2,1,0:T(8,128)(2,1)} %reshape.718), calls=%async_computation.2 | async-start | bytes 1572864 | tf_op jit(solution)/shard_map/all_to_all | solution.py:57
  344.2 18.5 %all-to-all-start.4 = ((bf16[32,11,768]{2,1,0:T(8,128)(2,1)}), bf16[32,11,768]{2,1,0:T(8,128)(2,1)}, u32[]{:S(2)}, u32[]{:S(2)}) async-start(bf16[32,11,768]{2,1,0:T(8,128)(2,1)} %reshape.723), calls=%async_computation.4 | async-start | bytes 1572864 | tf_op jit(solution)/shard_map/all_to_all | solution.py:57
  423.7 18.7 %all-to-all-start.3 = ((bf16[32,2,4224]{2,1,0:T(2,128)(2,1)}), bf16[32,2,4224]{2,1,0:T(2,128)(2,1)}, u32[]{:S(2)}, u32[]{:S(2)}) async-start(bf16[32,2,4224]{2,1,0:T(2,128)(2,1)} %reshape.775), calls=%async_computation.3 | async-start | bytes 1081344 | tf_op jit(solution)/shard_map/all_to_all | solution.py:62
  442.4 18.0 %all-to-all-start.5 = ((bf16[32,2,4224]{2,1,0:T(2,128)(2,1)}), bf16[32,2,4224]{2,1,0:T(2,128)(2,1)}, u32[]{:S(2)}, u32[]{:S(2)}) async-start(bf16[32,2,4224]{2,1,0:T(2,128)(2,1)} %reshape.777), calls=%async_computation.5 | async-start | bytes 1081344 | tf_op jit(solution)/shard_map/all_to_all | solution.py:62
  448.6 60.3 %all-reduce.16.cloned.1.call-start = ((), (), s32[]{:S(2)}) async-start(), calls=%async_computation.10 | async-start | bytes 786432 | tf_op jit(solution)/shard_map/psum | solution.py:53
  470.7 38.2 %copy-start.80 = (f32[768]{0:T(1024)S(1)}, f32[768]{0:T(1024)}, u32[]{:S(2)}) copy-start(f32[768]{0:T(1024)} %get-tuple-element.69) | copy-start | bytes 9220
  471.7 39.0 %copy-start.15 = (f32[128,768]{1,0:T(8,128)S(1)}, f32[128,768]{1,0:T(8,128)}, u32[]{:S(2)}) copy-start(f32[128,768]{1,0:T(8,128)} %copy-done.14) | copy-start | bytes 1179652
  516.7 24.1 %all-to-all-start.6 = ((bf16[32,11,768]{2,1,0:T(8,128)(2,1)}), bf16[32,11,768]{2,1,0:T(8,128)(2,1)}, u32[]{:S(2)}, u32[]{:S(2)}) async-start(bf16[32,11,768]{2,1,0:T(8,128)(2,1)} %reshape.727), calls=%async_computation.6 | async-start | bytes 1572864 | tf_op jit(solution)/shard_map/all_to_all | solution.py:57
  581.1 9.8 %copy-start.102 = (f32[128]{0:T(128)S(1)}, f32[128]{0:T(128)}, u32[]{:S(2)}) copy-start(f32[128]{0:T(128)} %get-tuple-element.71) | copy-start | bytes 1540
  581.1 9.8 %copy-start.105 = (f32[128]{0:T(128)S(1)}, f32[128]{0:T(128)}, u32[]{:S(2)}) copy-start(f32[128]{0:T(128)} %copy-done.103) | copy-start | bytes 1540
  581.1 9.8 %copy-start.108 = (f32[128]{0:T(128)S(1)}, f32[128]{0:T(128)}, u32[]{:S(2)}) copy-start(f32[128]{0:T(128)} %copy-done.106) | copy-start | bytes 1540
  581.1 9.8 %copy-start.22 = (bf16[128,768]{1,0:T(8,128)(2,1)S(1)}, bf16[128,768]{1,0:T(8,128)(2,1)}, u32[]{:S(2)}) copy-start(bf16[128,768]{1,0:T(8,128)(2,1)} %copy-done.21) | copy-start | bytes 589828
  581.1 9.8 %copy-start.93 = (s32[128]{0:T(128)S(1)}, s32[128]{0:T(128)}, u32[]{:S(2)}) copy-start(s32[128]{0:T(128)} %copy-done.92) | copy-start | bytes 1540
  581.1 9.8 %copy-start.95 = (s32[128]{0:T(128)S(1)}, s32[128]{0:T(128)}, u32[]{:S(2)}) copy-start(s32[128]{0:T(128)} %copy-done.94) | copy-start | bytes 1540
  581.1 10.0 %copy-start.75 = (f32[1,768,32]{1,2,0:T(8,128)S(1)}, f32[1,768,32]{1,2,0:T(8,128)}, u32[]{:S(2)}) copy-start(f32[1,768,32]{1,2,0:T(8,128)} %convolution_bitcast_fusion.16) | copy-start | bytes 294916
  582.2 20.4 %all-to-all-start.7 = ((bf16[32,2,4224]{2,1,0:T(2,128)(2,1)}), bf16[32,2,4224]{2,1,0:T(2,128)(2,1)S(1)}, u32[]{:S(2)}, u32[]{:S(2)}) async-start(bf16[32,2,4224]{2,1,0:T(2,128)(2,1)} %reshape.779), calls=%async_computation.7 | async-start | bytes 1081344 | tf_op jit(solution)/shard_map/all_to_all | solution.py:62
  590.8 53.3 %all-reduce.18.cloned.1.call-start = ((), (), s32[]{:S(2)}) async-start(), calls=%async_computation.11 | async-start | bytes 786432 | tf_op jit(solution)/shard_map/psum | solution.py:53
  591.2 11.9 %copy-start.45 = (bf16[128,352]{0,1:T(8,128)(2,1)S(1)}, bf16[128,352]{0,1:T(8,128)(2,1)}, u32[]{:S(2)}) copy-start(bf16[128,352]{0,1:T(8,128)(2,1)} %copy-done.44) | copy-start | bytes 270340
  591.9 11.5 %copy-start.74 = (bf16[2,768,32]{1,2,0:T(8,128)(2,1)S(1)}, bf16[2,768,32]{1,2,0:T(8,128)(2,1)}, u32[]{:S(2)}) copy-start(bf16[2,768,32]{1,2,0:T(8,128)(2,1)} %param.22) | copy-start | bytes 294916
  591.9 11.5 %copy-start.82 = (f32[768]{0:T(1024)S(1)}, f32[768]{0:T(1024)}, u32[]{:S(2)}) copy-start(f32[768]{0:T(1024)} %copy-done.81) | copy-start | bytes 9220
  591.9 11.5 %copy-start.127 = (f32[128]{0:T(128)S(1)}, f32[128]{0:T(128)}, u32[]{:S(2)}) copy-start(f32[128]{0:T(128)} %copy-done.126) | copy-start | bytes 1540
  608.2 164.2 %all-reduce.20.cloned.1.call-start = ((), (), s32[]{:S(2)}) async-start(), calls=%async_computation.12 | async-start | bytes 9830400 | tf_op jit(solution)/shard_map/psum | solution.py:293
  627.7 142.8 %copy-start.143 = (f32[128]{0:T(128)S(1)}, f32[128]{0:T(128)}, u32[]{:S(2)}) copy-start(f32[128]{0:T(128)} %copy-done.142) | copy-start | bytes 1540
  (113 other events, 223.5 us)
Sparse Core Ops, SparseCore 0:
  117.1 43.2 all-reduce.11
  266.0 35.7 all-reduce.13
  473.0 35.8 all-reduce.15
  608.3 35.7 all-reduce.17
  648.3 116.2 all-reduce.19
where the time goes:
time: 801 us; the launch traced here: 785 us
  blocking collectives  224 us (28%)
  waiting for transfers between devices  190 us (24%)
  local copies, waits for them, and re-layouts  185 us (23%)
  starting transfers between devices  65.3 us (8%)
  matrix products  54.9 us (7%)
  other arithmetic  50 us (6%)
  between operations  16.1 us (2%)
    psum x4, waiting for transfers between devices, head_total(): return lax.psum(partial_rows, 'tensor')  130 us
    psum x1, blocking collectives, shards(): lax.psum((jnp.stack(grads_qkv), jnp.stack(grads_out), jnp.stack(grads_tab...  125 us
    gather x1, local copies, waits for them, and re-layouts, bias_rows(): picked_ids = jnp.take(bucket_ids, offsets)  101 us
    psum x3, blocking collectives, send_back(): summed = lax.psum(partial_rows, 'tensor').astype(jnp.bfloat16)  99.6 us
    unnamed x311, local copies, waits for them, and re-layouts  46 us
    all_to_all x4, starting transfers between devices, to_owner(): lax.all_to_all(slot_buffer, 'expert', split_axis=0, concat_axis=1, tiled=...  34.2 us
    all_to_all x4, waiting for transfers between devices, to_owner(): lax.all_to_all(slot_buffer, 'expert', split_axis=0, concat_axis=1, tiled=...  32.6 us
    all_to_all x4, starting transfers between devices, send_back(): lax.all_to_all(summed, 'expert', split_axis=1, concat_axis=0, tiled=True)  30.1 us
  transfers between devices with their start and end apart: 13, of which 12 were waited for; matrix products, arithmetic and copies ran while one was open for 8% of the time, Pallas kernels for 0%

commit v1 on v0

v1 whole, which is shorter than its diff:
```python
import jax
import jax.numpy as jnp
from jax import lax
from jax.experimental import pallas as pl
from jax.experimental.pallas import tpu as pltpu
from jax.sharding import PartitionSpec as P

epsilon = 1e-06
masked_score = -1000000000.0
highest = lax.Precision.HIGHEST
f32, bf16 = jnp.float32, jnp.bfloat16

ROWS = 128
WIDTH = 768
QUARTER = 192
HERE = 3
HEAD = 64
EXPERTS = 32
MAIN = EXPERTS * 8
REST = 128
HALF = WIDTH // 2
SENT = WIDTH + HALF
SUMMED = WIDTH + 128
VMEM = 40 * 1024 * 1024


def call(body, outs, *operands, cost=0):
    return pl.pallas_call(
        body,
        out_shape=[jax.ShapeDtypeStruct(shape, dtype) for shape, dtype in outs],
        in_specs=[pl.BlockSpec(memory_space=pltpu.VMEM)] * len(operands),
        out_specs=[pl.BlockSpec(memory_space=pltpu.VMEM)] * len(outs),
        compiler_params=pltpu.CompilerParams(vmem_limit_bytes=VMEM),
        cost_estimate=pl.CostEstimate(
            flops=cost, transcendentals=0, bytes_accessed=sum(o.size * o.dtype.itemsize for o in operands)
        ),
        name=body.__name__,
    )(*operands)


def dot(left, right, left_axis=1, right_axis=0, precision=None):
    return lax.dot_general(
        left,
        right,
        (((left_axis,), (right_axis,)), ((), ())),
        precision=precision,
        preferred_element_type=f32,
    )


def iota(shape, axis):
    return lax.broadcasted_iota(jnp.int32, shape, axis)


def scale_of(values):
    return lax.rsqrt(jnp.mean(values * values, axis=-1, keepdims=True) + epsilon)


def norm_back(values, gain, upstream):
    inverse = scale_of(values)
    inner = upstream * gain
    mean = jnp.mean(inner * values, axis=-1, keepdims=True)
    back = inverse * inner - values * (inverse * inverse * inverse * mean)
    return back, jnp.sum(upstream * (values * inverse), axis=0, keepdims=True)


def head_mask(head):
    lane = iota((1, QUARTER), 1)
    return ((lane >= head * HEAD) & (lane < (head + 1) * HEAD)).astype(f32).astype(bf16)


def four(own, one, two, three):
    return (own.astype(f32) + two.astype(f32)) + (one.astype(f32) + three.astype(f32))


def column_of(row, size):
    same = iota((size, size), 0) == iota((size, size), 1)
    return jnp.sum(jnp.where(same, jnp.broadcast_to(row, (size, size)), 0.0), axis=1, keepdims=True)


def row_of(column, size):
    same = iota((size, size), 0) == iota((size, size), 1)
    return jnp.sum(jnp.where(same, jnp.broadcast_to(column, (size, size)), 0.0), axis=0, keepdims=True)


def setup(ids_ref, table_ref, segment_ref, routes_ref, bias_ref, across_ref, down_ref):
    hot = (iota((EXPERTS, 256), 0) == ids_ref[...]).astype(f32)
    by_offset = dot(table_ref[...], hot, precision=highest)
    segment = segment_ref[...].astype(f32)
    allowed = (column_of(segment, ROWS) == segment) & (iota((ROWS, ROWS), 1) <= iota((ROWS, ROWS), 0))
    for which in range(2 * HERE):
        line = jnp.broadcast_to(by_offset[which : which + 1, :], (ROWS, 256))
        placed = pltpu.roll(line, 129, axis=1, stride=1, stride_axis=0)[:, :ROWS]
        bias_ref[which] = jnp.where(allowed, placed, masked_score)
    lane = iota((ROWS, ROWS), 1)
    before = (lane < iota((ROWS, ROWS), 0)).astype(f32).astype(bf16)
    for layer in range(2):
        routes = routes_ref[layer]
        expert = [routes[:, k : k + 1].astype(f32) for k in range(2)]
        hots = [(lane.astype(f32) == expert[k]).astype(f32) for k in range(2)]
        counts = dot(before, (hots[0] + hots[1]).astype(bf16))
        columns = []
        for k in range(2):
            slot = jnp.sum(counts * hots[k], axis=1, keepdims=True)
            first = slot < 7.5
            base = expert[k] * 8.0
            columns.append(jnp.where(first, base + slot, -1.0))
            columns.append(jnp.where(first, -1.0, base + (slot - 8.0) * 2.0))
            columns.append(jnp.where(first, -1.0, base + (slot - 8.0) * 2.0 + 1.0))
        columns.extend(expert)
        across = jnp.zeros((ROWS, ROWS), f32)
        down = jnp.zeros((8, ROWS), f32)
        for place, column in enumerate(columns):
            across = jnp.where(lane == place, column, across)
            down = jnp.where(iota((8, ROWS), 0) == place, row_of(column, ROWS), down)
        across_ref[layer] = across
        down_ref[layer] = down


def one_hot(flags):
    return flags.astype(f32).astype(bf16)


def dispatch(down, rows):
    place = iota((MAIN, ROWS), 0).astype(f32)
    tables = [one_hot(place == down[n : n + 1, :]) for n in range(6)]
    if len(rows) == 1:
        pairs = [([tables[n] + tables[n + 3] for n in range(3)], rows[0])]
    else:
        pairs = [(tables[:3], rows[0]), (tables[3:], rows[1])]
    main, rest = 0.0, 0.0
    for (whole, low, high), row in pairs:
        main = main + dot(whole, row)
        rest = rest + dot(low, row[:, :HALF]) + dot(high, row[:, HALF:])
    return main.astype(bf16), rest.astype(bf16)


def pick(across, route, main, rest):
    place = iota((ROWS, MAIN), 1).astype(f32)
    whole, low, high = [
        one_hot(place == across[:, 3 * route + n : 3 * route + n + 1]) for n in range(3)
    ]
    whole_part = dot(whole, main)
    return whole_part[:, :HALF] + dot(low, rest), whole_part[:, HALF:] + dot(high, rest)


def rest_tables():
    row = iota((REST, MAIN), 0)
    target = (row & 31) * 8 + (row >> 5) * 2
    lane = iota((REST, MAIN), 1)
    real = row < 96
    return one_hot((lane == target) & real), one_hot((lane == target + 1) & real)


def unpack(packed_ref, offset, into_ref):
    low, high = rest_tables()
    rest = packed_ref[:, offset + WIDTH : offset + SENT]
    into_ref[0:MAIN, :] = packed_ref[:, offset : offset + WIDTH]
    into_ref[MAIN : MAIN + REST, 0:HALF] = dot(low, rest).astype(bf16)
    into_ref[MAIN : MAIN + REST, HALF:WIDTH] = dot(high, rest).astype(bf16)


def pack(rows, offset, into_ref):
    low, high = rest_tables()
    into_ref[:, offset : offset + WIDTH] = rows[:MAIN]
    into_ref[:, offset + WIDTH : offset + SENT] = (
        dot(low, rows[MAIN:, :HALF], 0) + dot(high, rows[MAIN:, HALF:], 0)
    ).astype(bf16)


def attend(current, gain_ref, qkv_ref, bias_ref, low_ref, triple_ref, weights_ref):
    low = (current * scale_of(current) * gain_ref[...]).astype(bf16)
    low_ref[...] = low
    for k in range(3):
        triple_ref[k] = dot(low, qkv_ref[k]).astype(bf16)
    mixture = jnp.zeros((ROWS, QUARTER), f32)
    for head in range(HERE):
        mask = head_mask(head)
        scores = dot(triple_ref[0] * mask, triple_ref[1], 1, 1) * HEAD**-0.5 + bias_ref[head]
        scores = scores - jnp.max(scores, axis=-1, keepdims=True)
        raised = jnp.exp(scores)
        weights = raised / jnp.sum(raised, axis=-1, keepdims=True)
        weights_ref[head] = weights
        mixture = mixture + dot(weights.astype(bf16), triple_ref[2] * mask)
    return mixture.astype(bf16)


def attention_first(
    tokens_ref, gain_ref, qkv_ref, bias_ref, out_ref, low_ref, triple_ref, weights_ref, mixture_ref, part_ref
):
    mixture = attend(
        tokens_ref[...].astype(f32), gain_ref, qkv_ref, bias_ref, low_ref, triple_ref, weights_ref
    )
    mixture_ref[...] = mixture
    part_ref[...] = dot(mixture, out_ref[...]).astype(bf16)


def attention_next(
    middle_ref,
    z0,
    z1,
    z2,
    z3,
    gain_ref,
    qkv_ref,
    bias_ref,
    out_ref,
    current_ref,
    low_ref,
    triple_ref,
    weights_ref,
    mixture_ref,
    part_ref,
):
    current = middle_ref[...] + four(z0[...], z1[...], z2[...], z3[...])
    current_ref[...] = current
    mixture = attend(current, gain_ref, qkv_ref, bias_ref, low_ref, triple_ref, weights_ref)
    mixture_ref[...] = mixture
    part_ref[...] = dot(mixture, out_ref[...]).astype(bf16)


def route_rows(middle, gain_ref, router_ref, across, low_ref, gates_ref):
    low = (middle * scale_of(middle) * gain_ref[...]).astype(bf16)
    low_ref[...] = low
    logits = dot(low, router_ref[...])
    lane = iota((ROWS, EXPERTS), 1).astype(f32)
    chosen = [
        jnp.sum(jnp.where(lane == across[:, 6 + k : 7 + k], logits, 0.0), axis=1, keepdims=True)
        for k in range(2)
    ]
    top = jnp.maximum(chosen[0], chosen[1])
    raised = [jnp.exp(c - top) for c in chosen]
    total = raised[0] + raised[1]
    gates = [r / total for r in raised]
    place = iota((ROWS, ROWS), 1)
    gates_ref[...] = jnp.where(place == 0, gates[0], jnp.where(place == 1, gates[1], 0.0))
    return low, gates


def route_first(
    current_ref,
    p0,
    p1,
    p2,
    p3,
    gain_ref,
    router_ref,
    across_ref,
    down_ref,
    middle_ref,
    low_ref,
    gates_ref,
    send_ref,
):
    middle = current_ref[...].astype(f32) + four(p0[...], p1[...], p2[...], p3[...])
    middle_ref[...] = middle
    low, gates = route_rows(middle, gain_ref, router_ref, across_ref[...], low_ref, gates_ref)
    main, rest = dispatch(down_ref[...], [low])
    send_ref[:, :WIDTH] = main
    send_ref[:, WIDTH:] = rest


def route_next(
    current_ref,
    p0,
    p1,
    p2,
    p3,
    gain_ref,
    router_ref,
    across_ref,
    down_ref,
    cotangent_ref,
    middle_ref,
    low_ref,
    gates_ref,
    send_ref,
):
    middle = current_ref[...].astype(f32) + four(p0[...], p1[...], p2[...], p3[...])
    middle_ref[...] = middle
    low, gates = route_rows(middle, gain_ref, router_ref, across_ref[...], low_ref, gates_ref)
    main, rest = dispatch(down_ref[...], [low])
    send_ref[:, :WIDTH] = main
    send_ref[:, WIDTH:SENT] = rest
    gradient = cotangent_ref[...].astype(f32)
    main, rest = dispatch(down_ref[...], [(gate * gradient).astype(bf16) for gate in gates])
    send_ref[:, SENT : SENT + WIDTH] = main
    send_ref[:, SENT + WIDTH :] = rest


CURVE = (2.0 / 3.141592653589793) ** 0.5


def gelu_parts(values):
    squared = values * values
    bent = jnp.tanh(CURVE * values * (1.0 + 0.044715 * squared))
    return bent, squared


def gelu(values):
    bent, _ = gelu_parts(values)
    return 0.5 * values * (1.0 + bent)


def gelu_slope(values):
    bent, squared = gelu_parts(values)
    inner = CURVE * (1.0 + 3.0 * 0.044715 * squared)
    return 0.5 * (1.0 + bent) + 0.5 * values * (1.0 - bent * bent) * inner


def expert_forward(got_ref, in_ref, out_ref, rows_ref, before_ref, active_ref, back_ref):
    unpack(got_ref, 0, rows_ref)
    before = dot(rows_ref[...], in_ref[...])
    before_ref[...] = before
    active = gelu(before).astype(bf16)
    active_ref[...] = active
    pack(dot(active, out_ref[...]).astype(bf16), 0, back_ref)


def expert_backward(got_ref, before_ref, in_ref, out_ref, grads_ref, down_ref, back_ref):
    unpack(got_ref, 0, grads_ref)
    grad_active = dot(grads_ref[...], out_ref[...], 1, 1)
    grad_before = (grad_active * gelu_slope(before_ref[...])).astype(bf16)
    down_ref[...] = grad_before
    pack(dot(grad_before, in_ref[...], 1, 1).astype(bf16), 0, back_ref)


def expert_both(got_ref, in_ref, out_ref, rows_ref, active_ref, grads_ref, down_ref, back_ref):
    unpack(got_ref, 0, rows_ref)
    unpack(got_ref, SENT, grads_ref)
    before = dot(rows_ref[...], in_ref[...])
    active = gelu(before).astype(bf16)
    active_ref[...] = active
    pack(dot(active, out_ref[...]).astype(bf16), 0, back_ref)
    grad_active = dot(grads_ref[...], out_ref[...], 1, 1)
    grad_before = (grad_active * gelu_slope(before)).astype(bf16)
    down_ref[...] = grad_before
    pack(dot(grad_before, in_ref[...], 1, 1).astype(bf16), SENT, back_ref)


def expert_grads_top(rows_ref, active_ref, grads_ref, down_ref, in_grad_ref, out_grad_ref):
    in_grad_ref[0, 0] = dot(rows_ref[...], down_ref[...], 0)
    out_grad_ref[0, 0] = dot(active_ref[...], grads_ref[...], 0)


def combine_first(got_ref, across_ref, gates_ref, part_ref, picked_ref):
    main, rest = got_ref[:, :WIDTH], got_ref[:, WIDTH:]
    across, gates = across_ref[...], gates_ref[...]
    left, right = 0.0, 0.0
    for route in range(2):
        one, two = pick(across, route, main, rest)
        picked_ref[route, :, :HALF] = one.astype(bf16)
        picked_ref[route, :, HALF:] = two.astype(bf16)
        left = left + gates[:, route : route + 1] * one
        right = right + gates[:, route : route + 1] * two
    part_ref[:, :HALF] = left.astype(bf16)
    part_ref[:, HALF:] = right.astype(bf16)


def gate_lanes(grads):
    place = iota((ROWS, 128), 1)
    both = jnp.where(place == 0, grads[0], jnp.where(place == 1, grads[1], 0.0))
    high = both.astype(bf16)
    moved = jnp.where(place == 2, grads[0], jnp.where(place == 3, grads[1], 0.0))
    low = (moved - moved.astype(bf16).astype(f32)).astype(bf16)
    return high + low


def gathered_back(got_ref, offset, across, into_ref):
    main = got_ref[:, offset : offset + WIDTH]
    rest = got_ref[:, offset + WIDTH : offset + SENT]
    left, right = pick(across, 0, main, rest)
    other_left, other_right = pick(across, 1, main, rest)
    into_ref[:, :HALF] = (left + other_left).astype(bf16)
    into_ref[:, HALF:WIDTH] = (right + other_right).astype(bf16)


def combine_next(got_ref, across_ref, gates_ref, cotangent_ref, part_ref, back_ref):
    main, rest = got_ref[:, :WIDTH], got_ref[:, WIDTH:SENT]
    across, gates = across_ref[...], gates_ref[...]
    gradient = cotangent_ref[...].astype(f32)
    left, right, grads = 0.0, 0.0, []
    for route in range(2):
        one, two = pick(across, route, main, rest)
        left = left + gates[:, route : route + 1] * one
        right = right + gates[:, route : route + 1] * two
        grads.append(
            jnp.sum(gradient[:, :HALF] * one + gradient[:, HALF:] * two, axis=1, keepdims=True)
        )
    part_ref[:, :HALF] = left.astype(bf16)
    part_ref[:, HALF:] = right.astype(bf16)
    gathered_back(got_ref, SENT, across, back_ref)
    back_ref[:, WIDTH:] = gate_lanes(grads)


def combine_back(got_ref, across_ref, lanes_ref, back_ref):
    gathered_back(got_ref, 0, across_ref[...], back_ref)
    back_ref[:, WIDTH:] = lanes_ref[...]


def attention_back(
    e0,
    e1,
    e2,
    e3,
    gates_ref,
    across_ref,
    router_ref,
    middle_ref,
    gain_ref,
    gradient_ref,
    out_ref,
    triple_ref,
    weights_ref,
    qkv_ref,
    ids_ref,
    after_ref,
    low_ref,
    back_triple_ref,
    part_ref,
    logits_ref,
    gain_grad_ref,
    table_grad_ref,
):
    total = four(e0[...], e1[...], e2[...], e3[...])
    gates = gates_ref[...]
    across = across_ref[...]
    gate = [gates[:, k : k + 1] for k in range(2)]
    grad_gate = [
        total[:, WIDTH + k : WIDTH + k + 1] + total[:, WIDTH + 2 + k : WIDTH + 3 + k] for k in range(2)
    ]
    mean = gate[0] * grad_gate[0] + gate[1] * grad_gate[1]
    lane = iota((ROWS, EXPERTS), 1).astype(f32)
    grad_logits = 0.0
    for k in range(2):
        grad_logits = grad_logits + jnp.where(
            lane == across[:, 6 + k : 7 + k], gate[k] * (grad_gate[k] - mean), 0.0
        )
    high = grad_logits.astype(bf16)
    low = (grad_logits - high.astype(f32)).astype(bf16)
    logits_ref[:, :EXPERTS] = high
    logits_ref[:, EXPERTS : 2 * EXPERTS] = low
    logits_ref[:, 2 * EXPERTS :] = jnp.zeros((ROWS, 128 - 2 * EXPERTS), bf16)
    grad_low = total[:, :WIDTH] + dot(high, router_ref[...], 1, 1) + dot(low, router_ref[...], 1, 1)
    grad_middle, gain_grad_ref[...] = norm_back(middle_ref[...], gain_ref[...], grad_low)
    after = gradient_ref[...].astype(f32) + grad_middle
    after_ref[...] = after
    low_after = after.astype(bf16)
    low_ref[...] = low_after
    grad_mixture = dot(low_after, out_ref[...], 1, 1).astype(bf16)
    queries, keys, values = triple_ref[0], triple_ref[1], triple_ref[2]
    grad_queries = jnp.zeros((ROWS, QUARTER), f32)
    grad_keys, grad_values = grad_queries, grad_queries
    diagonals = jnp.zeros((8, 256), f32)
    flip = one_hot(iota((ROWS, ROWS), 0) + iota((ROWS, ROWS), 1) == ROWS - 1)
    for head in range(HERE):
        mask = head_mask(head)
        masked_grad = grad_mixture * mask
        weights = weights_ref[head]
        grad_values = grad_values + dot(weights.astype(bf16), masked_grad, 0)
        grad_weights = dot(masked_grad, values, 1, 1)
        grad_scores = weights * (
            grad_weights - jnp.sum(weights * grad_weights, axis=-1, keepdims=True)
        )
        grad_scores = grad_scores.astype(bf16)
        grad_queries = grad_queries + dot(grad_scores, keys * mask)
        grad_keys = grad_keys + dot(grad_scores, queries * mask, 0)
        wide = jnp.concatenate([dot(flip, grad_scores), jnp.zeros((ROWS, 128), f32)], axis=1)
        turned = pltpu.roll(wide, 0, axis=1, stride=1, stride_axis=0)
        diagonals = jnp.where(
            iota((8, 256), 0) == head, jnp.sum(turned, axis=0, keepdims=True), diagonals
        )
    hot = (iota((EXPERTS, 256), 0) == ids_ref[...]).astype(f32)
    table_grad_ref[...] = dot(diagonals, hot, 1, 1, precision=highest)
    grad_input = 0.0
    for k, grad in enumerate((grad_queries * HEAD**-0.5, grad_keys * HEAD**-0.5, grad_values)):
        grad = grad.astype(bf16)
        back_triple_ref[:, k * QUARTER : (k + 1) * QUARTER] = grad
        grad_input = grad_input + dot(grad, qkv_ref[k], 1, 1)
    part_ref[...] = grad_input.astype(bf16)


def weight_grads(low_ref, back_triple_ref, mixture_ref, after_ref, low_two_ref, logits_ref, grads_ref):
    kind = grads_ref.dtype
    grads_ref[:, : 3 * QUARTER] = dot(low_ref[...], back_triple_ref[...], 0).astype(kind)
    for part in range(4):
        grads_ref[part * QUARTER : (part + 1) * QUARTER, 3 * QUARTER : WIDTH] = dot(
            mixture_ref[...], after_ref[:, part * QUARTER : (part + 1) * QUARTER], 0
        ).astype(kind)
    both = dot(low_two_ref[...], logits_ref[...], 0)
    grads_ref[:, WIDTH : WIDTH + EXPERTS] = (
        both[:, :EXPERTS] + both[:, EXPERTS : 2 * EXPERTS]
    ).astype(kind)
    grads_ref[:, WIDTH + EXPERTS :] = jnp.zeros((WIDTH, 128 - EXPERTS), kind)


def start_back(
    after_ref,
    d0,
    d1,
    d2,
    d3,
    input_ref,
    gain_ref,
    gates_ref,
    down_ref,
    picked_ref,
    gradient_ref,
    gain_grad_ref,
    lanes_ref,
    send_ref,
):
    grad_low = four(d0[...], d1[...], d2[...], d3[...])
    grad_input, gain_grad_ref[...] = norm_back(input_ref[...].astype(f32), gain_ref[...], grad_low)
    gradient = after_ref[...] + grad_input
    gradient_ref[...] = gradient
    gates = gates_ref[...]
    weighted = [(gates[:, k : k + 1] * gradient).astype(bf16) for k in range(2)]
    main, rest = dispatch(down_ref[...], weighted)
    send_ref[:, :WIDTH] = main
    send_ref[:, WIDTH:] = rest
    lanes_ref[...] = gate_lanes(
        [jnp.sum(gradient * picked_ref[k].astype(f32), axis=1, keepdims=True) for k in range(2)]
    )


def finish_back(after_ref, d0, d1, d2, d3, input_ref, gain_ref, gradient_ref, gain_grad_ref):
    grad_low = four(d0[...], d1[...], d2[...], d3[...])
    grad_input, gain_grad_ref[...] = norm_back(input_ref[...].astype(f32), gain_ref[...], grad_low)
    gradient_ref[...] = after_ref[...] + grad_input


def finish_output(middle_ref, z0, z1, z2, z3, output_ref):
    output_ref[...] = (middle_ref[...] + four(z0[...], z1[...], z2[...], z3[...])).astype(bf16)


def add_chunks(chunks_ref, g00, g01, g10, g11, t0, t1, spread_ref):
    share = WIDTH // EXPERTS
    total = chunks_ref[0:share, :].astype(f32)
    for block in range(1, EXPERTS):
        total = total + chunks_ref[block * share : (block + 1) * share, :].astype(f32)
    total = total.astype(bf16)
    row = iota((8, WIDTH), 0)
    gains = jnp.zeros((8, WIDTH), f32)
    for place, gain in enumerate((g00, g01, g10, g11)):
        gains = jnp.where(row == place, gain[...], gains)
    tables = jnp.concatenate([t0[0:4, :], t1[0:4, :]], axis=0)
    tables = jnp.concatenate([tables, jnp.zeros((8, 128 - EXPERTS), f32)], axis=1)
    small = jnp.concatenate([gains, tables], axis=1).astype(bf16)
    for block in range(EXPERTS):
        spread_ref[block * 32 : block * 32 + share, :] = total
        spread_ref[block * 32 + share : block * 32 + 32, :] = small


def place_grads(top_ref, all_ref, qkv_ref, out_ref, router_ref, gains_ref, tables_ref):
    share = WIDTH // EXPERTS
    small = jnp.zeros((8, SUMMED), f32)
    for block in range(EXPERTS):
        rows = slice(block * share, (block + 1) * share)
        chunk = all_ref[block * 32 : block * 32 + share, :].astype(f32)
        small = small + all_ref[block * 32 + share : block * 32 + 32, :].astype(f32)
        for k in range(3):
            qkv_ref[0, k, rows, :] = chunk[:, k * QUARTER : (k + 1) * QUARTER]
        part, first = divmod(block * share, QUARTER)
        out_ref[0, first : first + share, part * QUARTER : (part + 1) * QUARTER] = chunk[
            :, 3 * QUARTER : WIDTH
        ]
        router_ref[0, rows, :] = chunk[:, WIDTH : WIDTH + EXPERTS]
    for k in range(3):
        qkv_ref[1, k] = top_ref[:, k * QUARTER : (k + 1) * QUARTER]
    for part in range(4):
        out_ref[1, :, part * QUARTER : (part + 1) * QUARTER] = top_ref[
            part * QUARTER : (part + 1) * QUARTER, 3 * QUARTER : WIDTH
        ]
    router_ref[1] = top_ref[:, WIDTH : WIDTH + EXPERTS]
    gains_ref[...] = small[:, :WIDTH]
    tables_ref[...] = small[:, WIDTH:]


def around(values):
    sent = [
        lax.ppermute(values, "tensor", [(i, (i + shift) % 4) for i in range(4)]) for shift in (1, 2, 3)
    ]
    return [values, *sent]


def across_experts(values):
    return lax.all_to_all(values, "expert", 0, 0, tiled=True)


def shards(
    tokens,
    segment_ids,
    expert_routes,
    bucket_ids,
    proj_qkv,
    proj_out,
    bias_table,
    norm_gains,
    router,
    expert_in,
    expert_out,
    cotangent,
):
    ids = jnp.pad(jnp.flip(bucket_ids), (0, 1), constant_values=-1).reshape(1, 256)
    table = jnp.pad(bias_table.transpose(0, 2, 1).reshape(2 * HERE, EXPERTS), ((0, 2), (0, 0)))
    gains = norm_gains.reshape(4, 1, WIDTH)
    row = (ROWS, WIDTH)
    narrow = (ROWS, QUARTER)
    scores = (HERE, ROWS, ROWS)
    slots = (MAIN + REST, WIDTH)
    bias, across, down = call(
        setup,
        [((2 * HERE, ROWS, ROWS), f32), ((2, ROWS, ROWS), f32), ((2, 8, ROWS), f32)],
        ids,
        table,
        segment_ids,
        expert_routes,
    )
    kept = [(row, bf16), ((3, *narrow), bf16), (scores, f32), (narrow, bf16), (row, bf16)]

    low_a0, triple0, weights0, mixture0, part = call(
        attention_first, kept, tokens, gains[0], proj_qkv[0], bias[:HERE], proj_out[0]
    )
    middle0, low_b0, gates0, send = call(
        route_first,
        [(row, f32), (row, bf16), ((ROWS, ROWS), f32), ((MAIN, SENT), bf16)],
        tokens,
        *around(part),
        gains[1],
        router[0],
        across[0],
        down[0],
    )
    rows0, before0, active0, send = call(
        expert_forward,
        [(slots, bf16), (slots, f32), (slots, bf16), ((MAIN, SENT), bf16)],
        across_experts(send),
        expert_in[0, 0],
        expert_out[0, 0],
    )
    part, picked0 = call(
        combine_first,
        [(row, bf16), ((2, *row), bf16)],
        across_experts(send),
        across[0],
        gates0,
    )

    current1, low_a1, triple1, weights1, mixture1, part = call(
        attention_next,
        [(row, f32), *kept],
        middle0,
        *around(part),
        gains[2],
        proj_qkv[1],
        bias[HERE:],
        proj_out[1],
    )
    middle1, low_b1, gates1, send = call(
        route_next,
        [(row, f32), (row, bf16), ((ROWS, ROWS), f32), ((MAIN, 2 * SENT), bf16)],
        current1,
        *around(part),
        gains[3],
        router[1],
        across[1],
        down[1],
        cotangent,
    )
    rows1, active1, grads1, down1, send = call(
        expert_both,
        [(slots, bf16), (slots, bf16), (slots, bf16), (slots, bf16), ((MAIN, 2 * SENT), bf16)],
        across_experts(send),
        expert_in[1, 0],
        expert_out[1, 0],
    )
    moved, back = call(
        combine_next,
        [(row, bf16), ((ROWS, SUMMED), bf16)],
        across_experts(send),
        across[1],
        gates1,
        cotangent,
    )

    back_kept = [
        (row, f32),
        (row, bf16),
        ((ROWS, 3 * QUARTER), bf16),
        (row, bf16),
        ((ROWS, 128), bf16),
        ((1, WIDTH), f32),
        ((8, EXPERTS), f32),
    ]
    after1, low_after1, back_triple1, part, logits1, gain11, table1 = call(
        attention_back,
        back_kept,
        *around(back),
        gates1,
        across[1],
        router[1],
        middle1,
        gains[3],
        cotangent,
        proj_out[1],
        triple1,
        weights1,
        proj_qkv[1],
        ids,
    )
    parts = around(part)
    (top_grads,) = call(
        weight_grads,
        [((WIDTH, SUMMED), f32)],
        low_a1,
        back_triple1,
        mixture1,
        low_after1,
        low_b1,
        logits1,
    )
    top_grads = lax.psum(top_grads, "expert")
    (output,) = call(finish_output, [(row, bf16)], middle1, *around(moved))

    gradient0, gain10, lanes0, send = call(
        start_back,
        [(row, f32), ((1, WIDTH), f32), ((ROWS, 128), bf16), ((MAIN, SENT), bf16)],
        after1,
        *parts,
        current1,
        gains[2],
        gates0,
        down[0],
        picked0,
    )
    grads0, down0, send = call(
        expert_backward,
        [(slots, bf16), (slots, bf16), ((MAIN, SENT), bf16)],
        across_experts(send),
        before0,
        expert_in[0, 0],
        expert_out[0, 0],
    )
    (back,) = call(
        combine_back, [((ROWS, SUMMED), bf16)], across_experts(send), across[0], lanes0
    )
    after0, low_after0, back_triple0, part, logits0, gain01, table0 = call(
        attention_back,
        back_kept,
        *around(back),
        gates0,
        across[0],
        router[0],
        middle0,
        gains[1],
        gradient0,
        proj_out[0],
        triple0,
        weights0,
        proj_qkv[0],
        ids,
    )
    parts = around(part)
    (grads,) = call(
        weight_grads,
        [((WIDTH, SUMMED), bf16)],
        low_a0,
        back_triple0,
        mixture0,
        low_after0,
        low_b0,
        logits0,
    )
    tokens_grad, gain00 = call(
        finish_back,
        [(row, f32), ((1, WIDTH), f32)],
        after0,
        *parts,
        tokens,
        gains[0],
    )
    (spread,) = call(
        add_chunks,
        [((EXPERTS * 32, SUMMED), bf16)],
        across_experts(grads),
        gain00,
        gain01,
        gain10,
        gain11,
        table0,
        table1,
    )
    qkv_grad, out_grad, router_grad, gain_grads, table_grads = call(
        place_grads,
        [
            ((2, 3, WIDTH, QUARTER), f32),
            ((2, QUARTER, WIDTH), f32),
            ((2, WIDTH, EXPERTS), f32),
            ((8, WIDTH), f32),
            ((8, 128), f32),
        ],
        top_grads,
        across_experts(spread),
    )
    table_grad = table_grads.reshape(2, 4, 128)[:, :HERE, :EXPERTS].transpose(0, 2, 1)
    in_grad0 = dot(rows0, down0, 0)
    out_grad0 = dot(active0, grads0, 0)
    in_grad1 = dot(rows1, down1, 0)
    out_grad1 = dot(active1, grads1, 0)
    return (
        output,
        tokens_grad,
        qkv_grad,
        out_grad,
        table_grad,
        gain_grads[:4].reshape(2, 2, WIDTH),
        router_grad,
        jnp.stack([in_grad0, in_grad1])[:, None],
        jnp.stack([out_grad0, out_grad1])[:, None],
    )


def solution(mesh):
    placed = (
        P("expert", None),
        P("expert", None),
        P(None, "expert", None),
        P(),
        P(None, None, None, "tensor"),
        P(None, "tensor", None),
        P(None, None, "tensor"),
        P(),
        P(),
        P(None, "expert", None, "tensor"),
        P(None, "expert", "tensor", None),
        P("expert", None),
    )
    return jax.shard_map(
        shards,
        mesh=mesh,
        in_specs=placed,
        out_specs=(
            P("expert", None),
            P("expert", None),
            P(None, None, None, "tensor"),
            P(None, "tensor", None),
            P(None, None, "tensor"),
            P(),
            P(),
            P(None, "expert", None, "tensor"),
            P(None, "expert", "tensor", None),
        ),
        check_vma=False,
    )
```

time: 801 us -> 430 us (0.54); the launches traced: 785 us -> 428 us
  local copies, waits for them, and re-layouts: 185 us -> 52.6 us
  blocking collectives: 224 us -> 92.5 us
  matrix products: 54.9 us -> 3.22 us
  other arithmetic: 50 us -> 4.98 us
  starting transfers between devices: 65.3 us -> 32 us
  Pallas kernels: 0 us -> 32.8 us
    psum x4 -> x0, blocking collectives: 224 us -> none  [the longest x1 125 us: shards(): lax.psum((jnp.stack(grads_qkv), jnp.stack(grads_out), jnp.stack(grads_tab...]
    gather x1 -> x0, local copies, waits for them, and re-layouts: 101 us -> none  [bias_rows(): picked_ids = jnp.take(bucket_ids, offsets)]
    all_to_all x0 -> x5, blocking collectives: none -> 92.5 us  [across_experts(): return lax.all_to_all(values, 'expert', 0, 0, tiled=True)]
    ppermute x0 -> x24, waiting for transfers between devices: none -> 88.7 us  [around(): lax.ppermute(values, 'tensor', [(i, (i + shift) % 4) for i in range(4)])]
    dot_general x54 -> x4, matrix products: 54 us -> 3.22 us  [dot(): lax.dot_general(left, right, (((left_axis,), (right_axis,)), ((), ())), p...]
    all_to_all x8 -> x3, starting transfers between devices: 64.3 us -> 16.9 us  [across_experts(): return lax.all_to_all(values, 'expert', 0, 0, tiled=True)]
    all_to_all x8 -> x3, waiting for transfers between devices: 60 us -> 14.9 us  [across_experts(): return lax.all_to_all(values, 'expert', 0, 0, tiled=True)]
    psum x5 -> x1, waiting for transfers between devices: 130 us -> 91.5 us  [shards(): top_grads = lax.psum(top_grads, 'expert')]
  transfers between devices with their start and end apart: 13 -> 28, of which waited for: 12 -> 26; matrix products, arithmetic and copies ran while one was open for 8% -> 4% of each run, Pallas kernels for 0% -> 1%
where the time goes in v1:
time: 430 us; the launch traced here: 428 us
  waiting for transfers between devices  195 us (45%)
  blocking collectives  92.5 us (22%)
  local copies, waits for them, and re-layouts  52.6 us (12%)
  Pallas kernels  32.8 us (8%)
  starting transfers between devices  32 us (7%)
  between operations  14.9 us (3%)
  other arithmetic  4.98 us (1%)
    all_to_all x5, blocking collectives, across_experts(): return lax.all_to_all(values, 'expert', 0, 0, tiled=True)  92.5 us
    psum x1, waiting for transfers between devices, shards(): top_grads = lax.psum(top_grads, 'expert')  91.5 us
    ppermute x24, waiting for transfers between devices, around(): lax.ppermute(values, 'tensor', [(i, (i + shift) % 4) for i in range(4)])  88.7 us
    unnamed x202, local copies, waits for them, and re-layouts  41.1 us
    pallas_call x20, Pallas kernels, call(): pl.pallas_call(body, out_shape=[jax.ShapeDtypeStruct(shape, dtype) for sh...  32.8 us
    all_to_all x3, starting transfers between devices, across_experts(): return lax.all_to_all(values, 'expert', 0, 0, tiled=True)  16.9 us
    ppermute x24, starting transfers between devices, around(): lax.ppermute(values, 'tensor', [(i, (i + shift) % 4) for i in range(4)])  15.1 us
    all_to_all x3, waiting for transfers between devices, across_experts(): return lax.all_to_all(values, 'expert', 0, 0, tiled=True)  14.9 us
  transfers between devices with their start and end apart: 28, of which 26 were waited for; matrix products, arithmetic and copies ran while one was open for 4% of the time, Pallas kernels for 1%

profile of v1, /device:TPU:1, one launch (start us, length us, event | category | flops | bytes accessed | tf_op | source)
XLA Modules:
  0.0 428.2 jit_solution(4245247104260894296)
XLA Ops:
  12.9 1.8 slice_bitcast_fusion.4
  19.6 3.6 collective-permute-start.2
  26.2 4.5 %collective-permute-done.2.p3 = bf16[128,768]{1,0:T(8,128)(2,1)S(1)} collective-permute-done((bf16[128,768]{1,0:T(8,128)(2,1)S(1)}, bf16[128,768]{1,0:T(8,128)(2,1)S(1)}, u32[]{:S(2)}, u32[]{:S(2)}) %collective-permute-start.2) | collective-permute-done | bytes 196640 | tf_op jit(solution)/shard_map/ppermute | solution.py:582
  30.8 4.9 %collective-permute-done.p1 = bf16[128,768]{1,0:T(8,128)(2,1)S(1)} collective-permute-done((bf16[128,768]{1,0:T(8,128)(2,1)S(1)}, bf16[128,768]{1,0:T(8,128)(2,1)S(1)}, u32[]{:S(2)}, u32[]{:S(2)}) %collective-permute-start) | collective-permute-done | bytes 196640 | tf_op jit(solution)/shard_map/ppermute | solution.py:582
  39.1 8.5 %all-to-all-start = ((bf16[32,8,1152]{2,1,0:T(8,128)(2,1)}), bf16[32,8,1152]{2,1,0:T(8,128)(2,1)}, u32[]{:S(2)}, u32[]{:S(2)}) async-start(bf16[32,8,1152]{2,1,0:T(8,128)(2,1)} %bitcast.9), calls=%async_computation | async-start | bytes 1179648 | tf_op jit(solution)/shard_map/all_to_all | solution.py:588
  47.6 4.0 slice_bitcast_fusion
  51.6 8.3 %all-to-all-done = bf16[32,8,1152]{2,1,0:T(8,128)(2,1)} async-done(((bf16[32,8,1152]{2,1,0:T(8,128)(2,1)}), bf16[32,8,1152]{2,1,0:T(8,128)(2,1)}, u32[]{:S(2)}, u32[]{:S(2)}) %all-to-all-start) | async-done | bytes 589856 | tf_op jit(solution)/shard_map/all_to_all | solution.py:588
  59.9 2.6 expert_forward.1
  63.6 15.7 %all_to_all.88 = bf16[32,8,1152]{2,1,0:T(8,128)(2,1)S(1)} all-to-all(bf16[32,8,1152]{2,1,0:T(8,128)(2,1)S(1)} %bitcast.100), channel_id=1, replica_groups=mesh['expert'=32,'tensor'=4] {'expert'}, dimensions={0} | all-to-all | bytes 1179648 | tf_op jit(solution)/shard_map/all_to_all | solution.py:588
  82.7 2.3 copy.45
  85.0 3.2 collective-permute-done.5.z3
  89.9 4.6 %collective-permute-done.3.z1 = bf16[128,768]{1,0:T(8,128)(2,1)} collective-permute-done((bf16[128,768]{1,0:T(8,128)(2,1)}, bf16[128,768]{1,0:T(8,128)(2,1)}, u32[]{:S(2)}, u32[]{:S(2)}) %collective-permute-start.3) | collective-permute-done | bytes 196640 | tf_op jit(solution)/shard_map/ppermute | solution.py:582
  98.6 3.1 attention_next.1
  108.3 3.3 collective-permute-done.8.p3
  112.9 5.5 %collective-permute-done.6.p1 = bf16[128,768]{1,0:T(8,128)(2,1)} collective-permute-done((bf16[128,768]{1,0:T(8,128)(2,1)}, bf16[128,768]{1,0:T(8,128)(2,1)}, u32[]{:S(2)}, u32[]{:S(2)}) %collective-permute-start.6) | collective-permute-done | bytes 196640 | tf_op jit(solution)/shard_map/ppermute | solution.py:582
  122.8 2.3 route_next.1
  125.1 22.5 %all_to_all.89 = bf16[32,8,2304]{2,1,0:T(8,128)(2,1)S(1)} all-to-all(bf16[32,8,2304]{2,1,0:T(8,128)(2,1)S(1)} %bitcast.96), channel_id=1, replica_groups=mesh['expert'=32,'tensor'=4] {'expert'}, dimensions={0} | all-to-all | bytes 2359296 | tf_op jit(solution)/shard_map/all_to_all | solution.py:588
  147.6 3.1 expert_both.1
  150.8 22.8 %all_to_all.90 = bf16[32,8,2304]{2,1,0:T(8,128)(2,1)S(1)} all-to-all(bf16[32,8,2304]{2,1,0:T(8,128)(2,1)S(1)} %bitcast.97), channel_id=1, replica_groups=mesh['expert'=32,'tensor'=4] {'expert'}, dimensions={0} | all-to-all | bytes 2359296 | tf_op jit(solution)/shard_map/all_to_all | solution.py:588
  176.6 5.3 %collective-permute-done.14.e3 = bf16[128,896]{1,0:T(8,128)(2,1)S(1)} collective-permute-done((bf16[128,896]{1,0:T(8,128)(2,1)S(1)}, bf16[128,896]{1,0:T(8,128)(2,1)S(1)}, u32[]{:S(2)}, u32[]{:S(2)}) %collective-permute-start.14) | collective-permute-done | bytes 229408 | tf_op jit(solution)/shard_map/ppermute | solution.py:582
  181.9 1.9 collective-permute-done.13.e2
  183.8 5.9 %collective-permute-done.12.e1 = bf16[128,896]{1,0:T(8,128)(2,1)S(1)} collective-permute-done((bf16[128,896]{1,0:T(8,128)(2,1)S(1)}, bf16[128,896]{1,0:T(8,128)(2,1)S(1)}, u32[]{:S(2)}, u32[]{:S(2)}) %collective-permute-start.12) | collective-permute-done | bytes 229408 | tf_op jit(solution)/shard_map/ppermute | solution.py:582
  189.8 2.3 attention_back.2
  194.8 4.5 %collective-permute-done.17.d3 = bf16[128,768]{1,0:T(8,128)(2,1)S(1)} collective-permute-done((bf16[128,768]{1,0:T(8,128)(2,1)S(1)}, bf16[128,768]{1,0:T(8,128)(2,1)S(1)}, u32[]{:S(2)}, u32[]{:S(2)}) %collective-permute-start.17) | collective-permute-done | bytes 196640 | tf_op jit(solution)/shard_map/ppermute | solution.py:582
  200.4 5.6 %collective-permute-done.15.d1 = bf16[128,768]{1,0:T(8,128)(2,1)S(1)} collective-permute-done((bf16[128,768]{1,0:T(8,128)(2,1)S(1)}, bf16[128,768]{1,0:T(8,128)(2,1)S(1)}, u32[]{:S(2)}, u32[]{:S(2)}) %collective-permute-start.15) | collective-permute-done | bytes 196640 | tf_op jit(solution)/shard_map/ppermute | solution.py:582
  207.0 15.8 %all_to_all.91 = bf16[32,8,1152]{2,1,0:T(8,128)(2,1)S(1)} all-to-all(bf16[32,8,1152]{2,1,0:T(8,128)(2,1)S(1)} %bitcast.98), channel_id=1, replica_groups=mesh['expert'=32,'tensor'=4] {'expert'}, dimensions={0} | all-to-all | bytes 1179648 | tf_op jit(solution)/shard_map/all_to_all | solution.py:588
  222.9 1.9 expert_backward.1
  224.8 15.8 %all_to_all.92 = bf16[32,8,1152]{2,1,0:T(8,128)(2,1)S(1)} all-to-all(bf16[32,8,1152]{2,1,0:T(8,128)(2,1)S(1)} %bitcast.99), channel_id=1, replica_groups=mesh['expert'=32,'tensor'=4] {'expert'}, dimensions={0} | all-to-all | bytes 1179648 | tf_op jit(solution)/shard_map/all_to_all | solution.py:588
  242.5 5.9 %collective-permute-done.20.e3 = bf16[128,896]{1,0:T(8,128)(2,1)S(1)} collective-permute-done((bf16[128,896]{1,0:T(8,128)(2,1)S(1)}, bf16[128,896]{1,0:T(8,128)(2,1)S(1)}, u32[]{:S(2)}, u32[]{:S(2)}) %collective-permute-start.20) | collective-permute-done | bytes 229408 | tf_op jit(solution)/shard_map/ppermute | solution.py:582
  248.4 2.1 collective-permute-done.19.e2
  250.6 5.3 %collective-permute-done.18.e1 = bf16[128,896]{1,0:T(8,128)(2,1)S(1)} collective-permute-done((bf16[128,896]{1,0:T(8,128)(2,1)S(1)}, bf16[128,896]{1,0:T(8,128)(2,1)S(1)}, u32[]{:S(2)}, u32[]{:S(2)}) %collective-permute-start.18) | collective-permute-done | bytes 229408 | tf_op jit(solution)/shard_map/ppermute | solution.py:582
  255.9 2.3 attention_back.3
  258.3 1.8 weight_grads.3
  260.1 4.2 all-to-all-start.6
  265.8 4.7 %collective-permute-done.23.d3 = bf16[128,768]{1,0:T(8,128)(2,1)S(1)} collective-permute-done((bf16[128,768]{1,0:T(8,128)(2,1)S(1)}, bf16[128,768]{1,0:T(8,128)(2,1)S(1)}, u32[]{:S(2)}, u32[]{:S(2)}) %collective-permute-start.23) | collective-permute-done | bytes 196640 | tf_op jit(solution)/shard_map/ppermute | solution.py:582
  272.1 5.2 %collective-permute-done.21.d1 = bf16[128,768]{1,0:T(8,128)(2,1)S(1)} collective-permute-done((bf16[128,768]{1,0:T(8,128)(2,1)S(1)}, bf16[128,768]{1,0:T(8,128)(2,1)S(1)}, u32[]{:S(2)}, u32[]{:S(2)}) %collective-permute-start.21) | collective-permute-done | bytes 196640 | tf_op jit(solution)/shard_map/ppermute | solution.py:582
  278.3 6.6 %all-to-all-done.6 = bf16[32,24,896]{2,1,0:T(8,128)(2,1)S(1)} async-done(((bf16[32,24,896]{2,1,0:T(8,128)(2,1)}), bf16[32,24,896]{2,1,0:T(8,128)(2,1)S(1)}, u32[]{:S(2)}, u32[]{:S(2)}) %all-to-all-start.6) | async-done | bytes 1376288 | tf_op jit(solution)/shard_map/all_to_all | solution.py:588
  286.5 4.2 all-to-all-start.7
  292.7 2.4 weight_grads.2
  298.3 3.8 collective-permute-done.11.z3
  303.7 5.3 %collective-permute-done.9.z1 = bf16[128,768]{1,0:T(8,128)(2,1)S(1)} collective-permute-done((bf16[128,768]{1,0:T(8,128)(2,1)S(1)}, bf16[128,768]{1,0:T(8,128)(2,1)S(1)}, u32[]{:S(2)}, u32[]{:S(2)}) %collective-permute-start.9) | collective-permute-done | bytes 196640 | tf_op jit(solution)/shard_map/ppermute | solution.py:582
  311.4 2.5 maximum_bitcast_fusion
  313.9 2.5 maximum_bitcast_fusion.1
  316.4 91.5 %all-reduce.4.cloned.1.call-done.top_ref = f32[768,896]{1,0:T(8,128)} async-done(((f32[768,896]{1,0:T(8,128)}), f32[768,896]{1,0:T(8,128)}) %all-reduce.4.cloned.1.call-update) | async-done | bytes 2752528 | tf_op jit(solution)/shard_map/psum | solution.py:723
  407.9 1.8 copy-done.6
  409.7 1.7 place_grads.1
  411.4 2.2 copy-done.5
  413.6 5.6 %copy.39 = f32[2,3,768,192]{2,3,1,0:T(8,128)} copy(f32[2,3,768,192]{3,2,1,0:T(8,128)} %copy-done.5) | data formatting | bytes 7077888
  (257 shorter events, 66.2 us)
Async XLA Ops:
  19.6 11.2 %collective-permute-start.2 = (bf16[128,768]{1,0:T(8,128)(2,1)S(1)}, bf16[128,768]{1,0:T(8,128)(2,1)S(1)}, u32[]{:S(2)}, u32[]{:S(2)}) collective-permute-start(bf16[128,768]{1,0:T(8,128)(2,1)S(1)} %get-tuple-element.73.p0), channel_id=1, source_target_pairs={{0,3},{1,0},{2,1},{3,2},{4,7},{5,4},{6,5},{7,6},{8,11},{9,8},{10,9... | collective-permute-start | bytes 589832 | tf_op jit(solution)/shard_map/ppermute | solution.py:582
  23.1 7.6 %collective-permute-start.1 = (bf16[128,768]{1,0:T(8,128)(2,1)S(1)}, bf16[128,768]{1,0:T(8,128)(2,1)S(1)}, u32[]{:S(2)}, u32[]{:S(2)}) collective-permute-start(bf16[128,768]{1,0:T(8,128)(2,1)S(1)} %get-tuple-element.73.p0), channel_id=1, source_target_pairs={{0,2},{1,3},{2,0},{3,1},{4,6},{5,7},{6,4},{7,5},{8,10},{9,11},{10,... | collective-permute-start | bytes 589832 | tf_op jit(solution)/shard_map/ppermute | solution.py:582
  23.5 12.2 %collective-permute-start = (bf16[128,768]{1,0:T(8,128)(2,1)S(1)}, bf16[128,768]{1,0:T(8,128)(2,1)S(1)}, u32[]{:S(2)}, u32[]{:S(2)}) collective-permute-start(bf16[128,768]{1,0:T(8,128)(2,1)S(1)} %get-tuple-element.73.p0), channel_id=1, source_target_pairs={{0,1},{1,2},{2,3},{3,0},{4,5},{5,6},{6,7},{7,4},{8,9},{9,10},{10,1... | collective-permute-start | bytes 589832 | tf_op jit(solution)/shard_map/ppermute | solution.py:582
  39.1 20.8 %all-to-all-start = ((bf16[32,8,1152]{2,1,0:T(8,128)(2,1)}), bf16[32,8,1152]{2,1,0:T(8,128)(2,1)}, u32[]{:S(2)}, u32[]{:S(2)}) async-start(bf16[32,8,1152]{2,1,0:T(8,128)(2,1)} %bitcast.9), calls=%async_computation | async-start | bytes 1179648 | tf_op jit(solution)/shard_map/all_to_all | solution.py:588
  81.2 7.0 %collective-permute-start.5 = (bf16[128,768]{1,0:T(8,128)(2,1)}, bf16[128,768]{1,0:T(8,128)(2,1)}, u32[]{:S(2)}, u32[]{:S(2)}) collective-permute-start(bf16[128,768]{1,0:T(8,128)(2,1)} %get-tuple-element.80.z0), channel_id=1, source_target_pairs={{0,3},{1,0},{2,1},{3,2},{4,7},{5,4},{6,5},{7,6},{8,11},{9,8},{10,9... | collective-permute-start | bytes 589832 | tf_op jit(solution)/shard_map/ppermute | solution.py:582
  81.6 8.3 %collective-permute-start.4 = (bf16[128,768]{1,0:T(8,128)(2,1)}, bf16[128,768]{1,0:T(8,128)(2,1)}, u32[]{:S(2)}, u32[]{:S(2)}) collective-permute-start(bf16[128,768]{1,0:T(8,128)(2,1)} %get-tuple-element.80.z0), channel_id=1, source_target_pairs={{0,2},{1,3},{2,0},{3,1},{4,6},{5,7},{6,4},{7,5},{8,10},{9,11},{10,... | collective-permute-start | bytes 589832 | tf_op jit(solution)/shard_map/ppermute | solution.py:582
  81.9 12.6 %collective-permute-start.3 = (bf16[128,768]{1,0:T(8,128)(2,1)}, bf16[128,768]{1,0:T(8,128)(2,1)}, u32[]{:S(2)}, u32[]{:S(2)}) collective-permute-start(bf16[128,768]{1,0:T(8,128)(2,1)} %get-tuple-element.80.z0), channel_id=1, source_target_pairs={{0,1},{1,2},{2,3},{3,0},{4,5},{5,6},{6,7},{7,4},{8,9},{9,10},{10,1... | collective-permute-start | bytes 589832 | tf_op jit(solution)/shard_map/ppermute | solution.py:582
  105.2 6.3 %collective-permute-start.8 = (bf16[128,768]{1,0:T(8,128)(2,1)}, bf16[128,768]{1,0:T(8,128)(2,1)}, u32[]{:S(2)}, u32[]{:S(2)}) collective-permute-start(bf16[128,768]{1,0:T(8,128)(2,1)} %get-tuple-element.82.p0), channel_id=1, source_target_pairs={{0,3},{1,0},{2,1},{3,2},{4,7},{5,4},{6,5},{7,6},{8,11},{9,8},{10,9... | collective-permute-start | bytes 589832 | tf_op jit(solution)/shard_map/ppermute | solution.py:582
  105.6 7.4 %collective-permute-start.7 = (bf16[128,768]{1,0:T(8,128)(2,1)}, bf16[128,768]{1,0:T(8,128)(2,1)}, u32[]{:S(2)}, u32[]{:S(2)}) collective-permute-start(bf16[128,768]{1,0:T(8,128)(2,1)} %get-tuple-element.82.p0), channel_id=1, source_target_pairs={{0,2},{1,3},{2,0},{3,1},{4,6},{5,7},{6,4},{7,5},{8,10},{9,11},{10,... | collective-permute-start | bytes 589832 | tf_op jit(solution)/shard_map/ppermute | solution.py:582
  105.6 12.9 %collective-permute-start.6 = (bf16[128,768]{1,0:T(8,128)(2,1)}, bf16[128,768]{1,0:T(8,128)(2,1)}, u32[]{:S(2)}, u32[]{:S(2)}) collective-permute-start(bf16[128,768]{1,0:T(8,128)(2,1)} %get-tuple-element.82.p0), channel_id=1, source_target_pairs={{0,1},{1,2},{2,3},{3,0},{4,5},{5,6},{6,7},{7,4},{8,9},{9,10},{10,1... | collective-permute-start | bytes 589832 | tf_op jit(solution)/shard_map/ppermute | solution.py:582
  108.2 39.3 %copy-start.3 = (bf16[768,768]{1,0:T(8,128)(2,1)S(1)}, bf16[768,768]{1,0:T(8,128)(2,1)}, u32[]{:S(2)}) copy-start(bf16[768,768]{1,0:T(8,128)(2,1)} %get-tuple-element.153.out_ref) | copy-start | bytes 3538948
  108.2 39.3 %copy-start.4 = (bf16[768,768]{1,0:T(8,128)(2,1)S(1)}, bf16[768,768]{1,0:T(8,128)(2,1)}, u32[]{:S(2)}) copy-start(bf16[768,768]{1,0:T(8,128)(2,1)} %get-tuple-element.174.in_ref) | copy-start | bytes 3538948
  125.1 64.7 %copy-start.28 = (f32[128,768]{1,0:T(8,128)}, f32[128,768]{1,0:T(8,128)S(1)}, u32[]{:S(2)}) copy-start(f32[128,768]{1,0:T(8,128)S(1)} %get-tuple-element.83.middle_ref) | copy-start | bytes 1179652
  150.7 39.0 %copy-start.44 = (bf16[384,768]{1,0:T(8,128)(2,1)}, bf16[384,768]{1,0:T(8,128)(2,1)S(1)}, u32[]{:S(2)}) copy-start(bf16[384,768]{1,0:T(8,128)(2,1)S(1)} %get-tuple-element.134) | copy-start | bytes 1769476
  150.8 39.0 %copy-start.1 = (bf16[1,3,768,192]{3,2,1,0:T(8,128)(2,1)S(1)}, bf16[1,3,768,192]{3,2,1,0:T(8,128)(2,1)}, u32[]{:S(2)}) copy-start(bf16[1,3,768,192]{3,2,1,0:T(8,128)(2,1)} %copy.45) | copy-start | bytes 2654212
  150.8 39.0 %copy-start.8 = (bf16[192,768]{1,0:T(8,128)(2,1)S(1)}, bf16[192,768]{1,0:T(8,128)(2,1)}, u32[]{:S(2)}) copy-start(bf16[192,768]{1,0:T(8,128)(2,1)} %get-tuple-element.159.out_ref) | copy-start | bytes 884740
  150.8 39.0 %copy-start.14 = (bf16[1,768,32]{2,1,0:T(8,128)(2,1)S(1)}, bf16[1,768,32]{2,1,0:T(8,128)(2,1)}, u32[]{:S(2)}) copy-start(bf16[1,768,32]{2,1,0:T(8,128)(2,1)} %copy.46) | copy-start | bytes 147460
  150.8 39.0 %copy-start.67 = (bf16[3,128,192]{2,1,0:T(8,128)(2,1)S(1)}, bf16[3,128,192]{2,1,0:T(8,128)(2,1)}, u32[]{:S(2)}) copy-start(bf16[3,128,192]{2,1,0:T(8,128)(2,1)} %copy-done.66) | copy-start | bytes 442372
  150.8 39.0 %copy-start.69 = (f32[3,128,128]{2,1,0:T(8,128)S(1)}, f32[3,128,128]{2,1,0:T(8,128)}, u32[]{:S(2)}) copy-start(f32[3,128,128]{2,1,0:T(8,128)} %copy-done.68) | copy-start | bytes 589828
  150.8 39.0 %copy-start.87 = (s32[256]{0:T(256)S(1)}, s32[256]{0:T(256)}, u32[]{:S(2)}) copy-start(s32[256]{0:T(256)} %copy-done.86) | copy-start | bytes 3076
  173.6 32.4 %copy-start.27 = (f32[128,768]{1,0:T(8,128)S(1)}, f32[128,768]{1,0:T(8,128)}, u32[]{:S(2)}) copy-start(f32[128,768]{1,0:T(8,128)} %copy-done.25) | copy-start | bytes 1179652
  173.6 32.4 %copy-start.37 = (f32[128,128]{1,0:T(8,128)S(1)}, f32[128,128]{1,0:T(8,128)}, u32[]{:S(2)}) copy-start(f32[128,128]{1,0:T(8,128)} %copy-done.35) | copy-start | bytes 196612
  173.6 32.4 %copy-start.55 = (bf16[2,128,768]{2,1,0:T(8,128)(2,1)S(1)}, bf16[2,128,768]{2,1,0:T(8,128)(2,1)}, u32[]{:S(2)}) copy-start(bf16[2,128,768]{2,1,0:T(8,128)(2,1)} %copy-done.54) | copy-start | bytes 1179652
  175.1 6.8 %collective-permute-start.14 = (bf16[128,896]{1,0:T(8,128)(2,1)S(1)}, bf16[128,896]{1,0:T(8,128)(2,1)S(1)}, u32[]{:S(2)}, u32[]{:S(2)}) collective-permute-start(bf16[128,896]{1,0:T(8,128)(2,1)S(1)} %get-tuple-element.88.e0), channel_id=1, source_target_pairs={{0,3},{1,0},{2,1},{3,2},{4,7},{5,4},{6,5},{7,6},{8,11},{9,8},{10,9... | collective-permute-start | bytes 688136 | tf_op jit(solution)/shard_map/ppermute | solution.py:582
  175.8 8.0 %collective-permute-start.13 = (bf16[128,896]{1,0:T(8,128)(2,1)S(1)}, bf16[128,896]{1,0:T(8,128)(2,1)S(1)}, u32[]{:S(2)}, u32[]{:S(2)}) collective-permute-start(bf16[128,896]{1,0:T(8,128)(2,1)S(1)} %get-tuple-element.88.e0), channel_id=1, source_target_pairs={{0,2},{1,3},{2,0},{3,1},{4,6},{5,7},{6,4},{7,5},{8,10},{9,11},{10,... | collective-permute-start | bytes 688136 | tf_op jit(solution)/shard_map/ppermute | solution.py:582
  175.8 13.9 %collective-permute-start.12 = (bf16[128,896]{1,0:T(8,128)(2,1)S(1)}, bf16[128,896]{1,0:T(8,128)(2,1)S(1)}, u32[]{:S(2)}, u32[]{:S(2)}) collective-permute-start(bf16[128,896]{1,0:T(8,128)(2,1)S(1)} %get-tuple-element.88.e0), channel_id=1, source_target_pairs={{0,1},{1,2},{2,3},{3,0},{4,5},{5,6},{6,7},{7,4},{8,9},{9,10},{10,1... | collective-permute-start | bytes 688136 | tf_op jit(solution)/shard_map/ppermute | solution.py:582
  193.3 6.0 %collective-permute-start.17 = (bf16[128,768]{1,0:T(8,128)(2,1)S(1)}, bf16[128,768]{1,0:T(8,128)(2,1)S(1)}, u32[]{:S(2)}, u32[]{:S(2)}) collective-permute-start(bf16[128,768]{1,0:T(8,128)(2,1)S(1)} %get-tuple-element.92.d0), channel_id=1, source_target_pairs={{0,3},{1,0},{2,1},{3,2},{4,7},{5,4},{6,5},{7,6},{8,11},{9,8},{10,9... | collective-permute-start | bytes 589832 | tf_op jit(solution)/shard_map/ppermute | solution.py:582
  193.4 7.0 %collective-permute-start.16 = (bf16[128,768]{1,0:T(8,128)(2,1)S(1)}, bf16[128,768]{1,0:T(8,128)(2,1)S(1)}, u32[]{:S(2)}, u32[]{:S(2)}) collective-permute-start(bf16[128,768]{1,0:T(8,128)(2,1)S(1)} %get-tuple-element.92.d0), channel_id=1, source_target_pairs={{0,2},{1,3},{2,0},{3,1},{4,6},{5,7},{6,4},{7,5},{8,10},{9,11},{10,... | collective-permute-start | bytes 589832 | tf_op jit(solution)/shard_map/ppermute | solution.py:582
  193.5 12.5 %collective-permute-start.15 = (bf16[128,768]{1,0:T(8,128)(2,1)S(1)}, bf16[128,768]{1,0:T(8,128)(2,1)S(1)}, u32[]{:S(2)}, u32[]{:S(2)}) collective-permute-start(bf16[128,768]{1,0:T(8,128)(2,1)S(1)} %get-tuple-element.92.d0), channel_id=1, source_target_pairs={{0,1},{1,2},{2,3},{3,0},{4,5},{5,6},{6,7},{7,4},{8,9},{9,10},{10,1... | collective-permute-start | bytes 589832 | tf_op jit(solution)/shard_map/ppermute | solution.py:582
  222.8 33.0 %copy-start.10 = (bf16[192,768]{1,0:T(8,128)(2,1)S(1)}, bf16[192,768]{1,0:T(8,128)(2,1)}, u32[]{:S(2)}) copy-start(bf16[192,768]{1,0:T(8,128)(2,1)} %copy-done.9) | copy-start | bytes 884740
  222.8 33.0 %copy-start.12 = (bf16[1,768,32]{2,1,0:T(8,128)(2,1)S(1)}, bf16[1,768,32]{2,1,0:T(8,128)(2,1)}, u32[]{:S(2)}) copy-start(bf16[1,768,32]{2,1,0:T(8,128)(2,1)} %copy-done.11) | copy-start | bytes 147460
  222.8 33.0 %copy-start.24 = (f32[128,768]{1,0:T(8,128)S(1)}, f32[128,768]{1,0:T(8,128)}, u32[]{:S(2)}) copy-start(f32[128,768]{1,0:T(8,128)} %copy-done.22) | copy-start | bytes 1179652
  222.8 33.0 %copy-start.57 = (bf16[3,128,192]{2,1,0:T(8,128)(2,1)S(1)}, bf16[3,128,192]{2,1,0:T(8,128)(2,1)}, u32[]{:S(2)}) copy-start(bf16[3,128,192]{2,1,0:T(8,128)(2,1)} %copy-done.56) | copy-start | bytes 442372
  222.9 33.0 %copy-start.59 = (f32[3,128,128]{2,1,0:T(8,128)S(1)}, f32[3,128,128]{2,1,0:T(8,128)}, u32[]{:S(2)}) copy-start(f32[3,128,128]{2,1,0:T(8,128)} %copy-done.58) | copy-start | bytes 589828
  224.7 31.1 %copy-start.50 = (bf16[384,768]{1,0:T(8,128)(2,1)}, bf16[384,768]{1,0:T(8,128)(2,1)S(1)}, u32[]{:S(2)}) copy-start(bf16[384,768]{1,0:T(8,128)(2,1)S(1)} %get-tuple-element.132) | copy-start | bytes 1769476
  224.7 31.1 %copy-start.52 = (bf16[384,768]{1,0:T(8,128)(2,1)}, bf16[384,768]{1,0:T(8,128)(2,1)S(1)}, u32[]{:S(2)}) copy-start(bf16[384,768]{1,0:T(8,128)(2,1)S(1)} %get-tuple-element.128) | copy-start | bytes 1769476
  241.0 7.5 %collective-permute-start.20 = (bf16[128,896]{1,0:T(8,128)(2,1)S(1)}, bf16[128,896]{1,0:T(8,128)(2,1)S(1)}, u32[]{:S(2)}, u32[]{:S(2)}) collective-permute-start(bf16[128,896]{1,0:T(8,128)(2,1)S(1)} %combine_back.1.e0), channel_id=1, source_target_pairs={{0,3},{1,0},{2,1},{3,2},{4,7},{5,4},{6,5},{7,6},{8,11},{9,8},{10,9... | collective-permute-start | bytes 688136 | tf_op jit(solution)/shard_map/ppermute | solution.py:582
  241.9 8.7 %collective-permute-start.19 = (bf16[128,896]{1,0:T(8,128)(2,1)S(1)}, bf16[128,896]{1,0:T(8,128)(2,1)S(1)}, u32[]{:S(2)}, u32[]{:S(2)}) collective-permute-start(bf16[128,896]{1,0:T(8,128)(2,1)S(1)} %combine_back.1.e0), channel_id=1, source_target_pairs={{0,2},{1,3},{2,0},{3,1},{4,6},{5,7},{6,4},{7,5},{8,10},{9,11},{10,... | collective-permute-start | bytes 688136 | tf_op jit(solution)/shard_map/ppermute | solution.py:582
  241.9 14.0 %collective-permute-start.18 = (bf16[128,896]{1,0:T(8,128)(2,1)S(1)}, bf16[128,896]{1,0:T(8,128)(2,1)S(1)}, u32[]{:S(2)}, u32[]{:S(2)}) collective-permute-start(bf16[128,896]{1,0:T(8,128)(2,1)S(1)} %combine_back.1.e0), channel_id=1, source_target_pairs={{0,1},{1,2},{2,3},{3,0},{4,5},{5,6},{6,7},{7,4},{8,9},{9,10},{10,1... | collective-permute-start | bytes 688136 | tf_op jit(solution)/shard_map/ppermute | solution.py:582
  260.1 24.8 %all-to-all-start.6 = ((bf16[32,24,896]{2,1,0:T(8,128)(2,1)}), bf16[32,24,896]{2,1,0:T(8,128)(2,1)S(1)}, u32[]{:S(2)}, u32[]{:S(2)}) async-start(bf16[32,24,896]{2,1,0:T(8,128)(2,1)} %bitcast.32), calls=%async_computation.6 | async-start | bytes 2752512 | tf_op jit(solution)/shard_map/all_to_all | solution.py:588
  264.3 6.2 %collective-permute-start.23 = (bf16[128,768]{1,0:T(8,128)(2,1)S(1)}, bf16[128,768]{1,0:T(8,128)(2,1)S(1)}, u32[]{:S(2)}, u32[]{:S(2)}) collective-permute-start(bf16[128,768]{1,0:T(8,128)(2,1)S(1)} %get-tuple-element.102.d0), channel_id=1, source_target_pairs={{0,3},{1,0},{2,1},{3,2},{4,7},{5,4},{6,5},{7,6},{8,11},{9,8},{10,9... | collective-permute-start | bytes 589832 | tf_op jit(solution)/shard_map/ppermute | solution.py:582
  264.7 7.4 %collective-permute-start.22 = (bf16[128,768]{1,0:T(8,128)(2,1)S(1)}, bf16[128,768]{1,0:T(8,128)(2,1)S(1)}, u32[]{:S(2)}, u32[]{:S(2)}) collective-permute-start(bf16[128,768]{1,0:T(8,128)(2,1)S(1)} %get-tuple-element.102.d0), channel_id=1, source_target_pairs={{0,2},{1,3},{2,0},{3,1},{4,6},{5,7},{6,4},{7,5},{8,10},{9,11},{10,... | collective-permute-start | bytes 589832 | tf_op jit(solution)/shard_map/ppermute | solution.py:582
  264.7 12.5 %collective-permute-start.21 = (bf16[128,768]{1,0:T(8,128)(2,1)S(1)}, bf16[128,768]{1,0:T(8,128)(2,1)S(1)}, u32[]{:S(2)}, u32[]{:S(2)}) collective-permute-start(bf16[128,768]{1,0:T(8,128)(2,1)S(1)} %get-tuple-element.102.d0), channel_id=1, source_target_pairs={{0,1},{1,2},{2,3},{3,0},{4,5},{5,6},{6,7},{7,4},{8,9},{9,10},{10,1... | collective-permute-start | bytes 589832 | tf_op jit(solution)/shard_map/ppermute | solution.py:582
  286.5 121.4 %all-to-all-start.7 = ((bf16[32,32,896]{2,1,0:T(8,128)(2,1)}), bf16[32,32,896]{2,1,0:T(8,128)(2,1)S(1)}, u32[]{:S(2)}, u32[]{:S(2)}) async-start(bf16[32,32,896]{2,1,0:T(8,128)(2,1)} %bitcast.85), calls=%async_computation.7 | async-start | bytes 3670016 | tf_op jit(solution)/shard_map/all_to_all | solution.py:588
  290.7 117.2 %all-reduce.4.cloned.1.call-start = ((), (), s32[]{:S(2)}) async-start(), calls=%async_computation.8 | async-start | bytes 5505024 | tf_op jit(solution)/shard_map/psum | solution.py:723
  296.0 6.2 %collective-permute-start.11 = (bf16[128,768]{1,0:T(8,128)(2,1)S(1)}, bf16[128,768]{1,0:T(8,128)(2,1)S(1)}, u32[]{:S(2)}, u32[]{:S(2)}) collective-permute-start(bf16[128,768]{1,0:T(8,128)(2,1)S(1)} %copy-done.75), channel_id=1, source_target_pairs={{0,3},{1,0},{2,1},{3,2},{4,7},{5,4},{6,5},{7,6},{8,11},{9,8},{10,9... | collective-permute-start | bytes 589832 | tf_op jit(solution)/shard_map/ppermute | solution.py:582
  296.3 7.4 %collective-permute-start.10 = (bf16[128,768]{1,0:T(8,128)(2,1)S(1)}, bf16[128,768]{1,0:T(8,128)(2,1)S(1)}, u32[]{:S(2)}, u32[]{:S(2)}) collective-permute-start(bf16[128,768]{1,0:T(8,128)(2,1)S(1)} %copy-done.75), channel_id=1, source_target_pairs={{0,2},{1,3},{2,0},{3,1},{4,6},{5,7},{6,4},{7,5},{8,10},{9,11},{10,... | collective-permute-start | bytes 589832 | tf_op jit(solution)/shard_map/ppermute | solution.py:582
  296.3 12.6 %collective-permute-start.9 = (bf16[128,768]{1,0:T(8,128)(2,1)S(1)}, bf16[128,768]{1,0:T(8,128)(2,1)S(1)}, u32[]{:S(2)}, u32[]{:S(2)}) collective-permute-start(bf16[128,768]{1,0:T(8,128)(2,1)S(1)} %copy-done.75), channel_id=1, source_target_pairs={{0,1},{1,2},{2,3},{3,0},{4,5},{5,6},{6,7},{7,4},{8,9},{9,10},{10,1... | collective-permute-start | bytes 589832 | tf_op jit(solution)/shard_map/ppermute | solution.py:582
  (76 other events, 670.1 us)
Sparse Core Ops, SparseCore 0:
  295.5 112.3 all-reduce.3

commit v2 on v1

--- a/solution.py
+++ b/solution.py
@@ -21,21 +21,139 @@
 HALF = WIDTH // 2
 SENT = WIDTH + HALF
 SUMMED = WIDTH + 128
-VMEM = 40 * 1024 * 1024
-
-
-def call(body, outs, *operands, cost=0):
+LONG = ROWS + 8
+
+
+class Layer:
+    def __init__(self, array, layer):
+        self.array, self.layer = array, layer
+
+
+class Late:
+    def __init__(self, operand):
+        self.operand = operand
+
+
+class Kept:
+    def __init__(self, shape, dtype):
+        self.shape, self.dtype = shape, dtype
+
+
+class Arriving:
+    def __init__(self, source, held, done):
+        self.held, self.copy, self.here = held, pltpu.make_async_copy(source, held, done), False
+        self.copy.start()
+
+    @property
+    def shape(self):
+        return self.held.shape
+
+    def __getitem__(self, index):
+        self.wait()
+        return self.held[index]
+
+    def wait(self):
+        if not self.here:
+            self.copy.wait()
+            self.here = True
+
+
+class Leaving:
+    def __init__(self, held, target, done):
+        self.held, self.copy, self.gone = held, pltpu.make_async_copy(held, target, done), False
+
+    @property
+    def dtype(self):
+        return self.held.dtype
+
+    def __getitem__(self, index):
+        return self.held[index]
+
+    def __setitem__(self, index, value):
+        self.held[index] = value
+
+    def go(self):
+        if not self.gone:
+            self.copy.start()
+            self.gone = True
+
+
+def go(*refs):
+    for ref in refs:
+        if isinstance(ref, Leaving):
+            ref.go()
+
+
+def in_hbm(array):
+    return pltpu.with_memory_space_constraint(array, pltpu.HBM)
+
+
+def call(body, outs, *operands, limit=16):
+    late = [isinstance(o, Late) for o in operands]
+    inner = [o.operand if isinstance(o, Late) else o for o in operands]
+    arrays = [o.array if isinstance(o, Layer) else o for o in inner]
+    parts = [a.shape[1:] if isinstance(o, Layer) else a.shape for o, a in zip(inner, arrays)]
+    arrays = [in_hbm(a) if is_late else a for a, is_late in zip(arrays, late)]
+    kept = [isinstance(o, Kept) for o in outs]
+    shapes = [(o.shape, o.dtype) if isinstance(o, Kept) else o for o in outs]
+    scratch = [pltpu.VMEM(p, a.dtype) for p, a, is_late in zip(parts, arrays, late) if is_late]
+    scratch += [pltpu.VMEM(*o) for o, is_kept in zip(shapes, kept) if is_kept]
+    copies = len(scratch)
+    if copies:
+        scratch.append(pltpu.SemaphoreType.DMA((copies,)))
+
+    def kernel(*refs):
+        count = len(operands) + len(outs)
+        spare = list(refs[count:])
+        done = spare.pop() if copies else None
+        given, used = [], 0
+        for ref, operand, is_late in zip(refs, inner, late):
+            view = ref.at[operand.layer] if isinstance(operand, Layer) else ref
+            if is_late:
+                view = Arriving(view, spare[used], done.at[used])
+                used += 1
+            given.append(view)
+        taken, leaving = [], []
+        for ref, is_kept in zip(refs[len(operands) : count], kept):
+            if is_kept:
+                ref = Leaving(spare[used], ref, done.at[used])
+                leaving.append(ref)
+                used += 1
+            taken.append(ref)
+        body(*given, *taken)
+        go(*leaving)
+        for ref in leaving:
+            ref.copy.wait()
+        for view in given:
+            if isinstance(view, Arriving):
+                view.wait()
+
+    return pl.pallas_call(
+        kernel,
+        out_shape=[
+            pltpu.HBM(*o) if is_kept else jax.ShapeDtypeStruct(*o) for o, is_kept in zip(shapes, kept)
+        ],
+        in_specs=[pl.BlockSpec(memory_space=pltpu.HBM if n else pltpu.VMEM) for n in late],
+        out_specs=[pl.BlockSpec(memory_space=pltpu.HBM if n else pltpu.VMEM) for n in kept],
+        scratch_shapes=scratch,
+        compiler_params=pltpu.CompilerParams(vmem_limit_bytes=limit * 1024 * 1024),
+        name=body.__name__,
+    )(*arrays)
+
+
+def call_stacked(body, layer, operands, stacked, earlier=()):
+    whole = [pl.BlockSpec(o.shape, lambda _, n=o.ndim: (0,) * n) for o in operands]
+    part = pl.BlockSpec((1, 1, *stacked[2:]), lambda _: (layer, 0, 0, 0))
     return pl.pallas_call(
         body,
-        out_shape=[jax.ShapeDtypeStruct(shape, dtype) for shape, dtype in outs],
-        in_specs=[pl.BlockSpec(memory_space=pltpu.VMEM)] * len(operands),
-        out_specs=[pl.BlockSpec(memory_space=pltpu.VMEM)] * len(outs),
-        compiler_params=pltpu.CompilerParams(vmem_limit_bytes=VMEM),
-        cost_estimate=pl.CostEstimate(
-            flops=cost, transcendentals=0, bytes_accessed=sum(o.size * o.dtype.itemsize for o in operands)
-        ),
+        grid=(1,),
+        out_shape=[jax.ShapeDtypeStruct(stacked, f32)] * 2,
+        in_specs=whole + [pl.BlockSpec(memory_space=pl.ANY)] * len(earlier),
+        out_specs=[part] * 2,
+        input_output_aliases={len(operands) + n: n for n in range(len(earlier))},
+        compiler_params=pltpu.CompilerParams(vmem_limit_bytes=24 * 1024 * 1024),
         name=body.__name__,
-    )(*operands)
+    )(*[in_hbm(o) for o in operands], *earlier)
 
 
 def dot(left, right, left_axis=1, right_axis=0, precision=None):
@@ -83,20 +201,24 @@
     return jnp.sum(jnp.where(same, jnp.broadcast_to(column, (size, size)), 0.0), axis=0, keepdims=True)
 
 
-def setup(ids_ref, table_ref, segment_ref, routes_ref, bias_ref, across_ref, down_ref):
-    hot = (iota((EXPERTS, 256), 0) == ids_ref[...]).astype(f32)
-    by_offset = dot(table_ref[...], hot, precision=highest)
+def setup(ids_ref, table_ref, segment_ref, routes_ref, bias_ref, across_ref, down_ref, hot_ref):
+    offsets = ids_ref.shape[1]
+    hot = one_hot(iota((EXPERTS, offsets), 0) == ids_ref[...])
+    mirror = one_hot(iota((offsets, 256), 0) + iota((offsets, 256), 1) == offsets - 1)
+    hot = dot(hot, mirror)
+    hot_ref[...] = hot
     segment = segment_ref[...].astype(f32)
     allowed = (column_of(segment, ROWS) == segment) & (iota((ROWS, ROWS), 1) <= iota((ROWS, ROWS), 0))
-    for which in range(2 * HERE):
-        line = jnp.broadcast_to(by_offset[which : which + 1, :], (ROWS, 256))
-        placed = pltpu.roll(line, 129, axis=1, stride=1, stride_axis=0)[:, :ROWS]
-        bias_ref[which] = jnp.where(allowed, placed, masked_score)
     lane = iota((ROWS, ROWS), 1)
-    before = (lane < iota((ROWS, ROWS), 0)).astype(f32).astype(bf16)
+    before = one_hot(lane < iota((ROWS, ROWS), 0))
     for layer in range(2):
-        routes = routes_ref[layer]
-        expert = [routes[:, k : k + 1].astype(f32) for k in range(2)]
+        by_offset = dot(table_ref[layer], hot, precision=highest)
+        for head in range(HERE):
+            line = jnp.broadcast_to(by_offset[head : head + 1, :], (ROWS, 256))
+            placed = pltpu.roll(line, 129, axis=1, stride=1, stride_axis=0)[:, :ROWS]
+            bias_ref[layer, head] = jnp.where(allowed, placed, masked_score)
+        routes = routes_ref[layer].astype(f32)
+        expert = [column_of(routes[k : k + 1, :], ROWS) for k in range(2)]
         hots = [(lane.astype(f32) == expert[k]).astype(f32) for k in range(2)]
         counts = dot(before, (hots[0] + hots[1]).astype(bf16))
         columns = []
@@ -169,11 +291,12 @@
 
 
 def attend(current, gain_ref, qkv_ref, bias_ref, low_ref, triple_ref, weights_ref):
-    low = (current * scale_of(current) * gain_ref[...]).astype(bf16)
+    low = (current * scale_of(current) * gain_ref[0:1, :]).astype(bf16)
     low_ref[...] = low
     for k in range(3):
-        triple_ref[k] = dot(low, qkv_ref[k]).astype(bf16)
+        triple_ref[k] = dot(low, qkv_ref[k], 1, 1).astype(bf16)
     mixture = jnp.zeros((ROWS, QUARTER), f32)
+    go(low_ref, triple_ref)
     for head in range(HERE):
         mask = head_mask(head)
         scores = dot(triple_ref[0] * mask, triple_ref[1], 1, 1) * HEAD**-0.5 + bias_ref[head]
@@ -182,6 +305,7 @@
         weights = raised / jnp.sum(raised, axis=-1, keepdims=True)
         weights_ref[head] = weights
         mixture = mixture + dot(weights.astype(bf16), triple_ref[2] * mask)
+    go(weights_ref)
     return mixture.astype(bf16)
 
 
@@ -192,6 +316,7 @@
         tokens_ref[...].astype(f32), gain_ref, qkv_ref, bias_ref, low_ref, triple_ref, weights_ref
     )
     mixture_ref[...] = mixture
+    go(mixture_ref)
     part_ref[...] = dot(mixture, out_ref[...]).astype(bf16)
 
 
@@ -216,13 +341,15 @@
     current_ref[...] = current
     mixture = attend(current, gain_ref, qkv_ref, bias_ref, low_ref, triple_ref, weights_ref)
     mixture_ref[...] = mixture
+    go(mixture_ref)
     part_ref[...] = dot(mixture, out_ref[...]).astype(bf16)
 
 
 def route_rows(middle, gain_ref, router_ref, across, low_ref, gates_ref):
-    low = (middle * scale_of(middle) * gain_ref[...]).astype(bf16)
+    low = (middle * scale_of(middle) * gain_ref[1:2, :]).astype(bf16)
     low_ref[...] = low
-    logits = dot(low, router_ref[...])
+    go(low_ref)
+    logits = dot(low, router_ref[...], 1, 1)
     lane = iota((ROWS, EXPERTS), 1).astype(f32)
     chosen = [
         jnp.sum(jnp.where(lane == across[:, 6 + k : 7 + k], logits, 0.0), axis=1, keepdims=True)
@@ -254,6 +381,7 @@
 ):
     middle = current_ref[...].astype(f32) + four(p0[...], p1[...], p2[...], p3[...])
     middle_ref[...] = middle
+    go(middle_ref)
     low, gates = route_rows(middle, gain_ref, router_ref, across_ref[...], low_ref, gates_ref)
     main, rest = dispatch(down_ref[...], [low])
     send_ref[:, :WIDTH] = main
@@ -278,6 +406,7 @@
 ):
     middle = current_ref[...].astype(f32) + four(p0[...], p1[...], p2[...], p3[...])
     middle_ref[...] = middle
+    go(middle_ref)
     low, gates = route_rows(middle, gain_ref, router_ref, across_ref[...], low_ref, gates_ref)
     main, rest = dispatch(down_ref[...], [low])
     send_ref[:, :WIDTH] = main
@@ -312,35 +441,46 @@
     unpack(got_ref, 0, rows_ref)
     before = dot(rows_ref[...], in_ref[...])
     before_ref[...] = before
+    go(rows_ref, before_ref)
     active = gelu(before).astype(bf16)
     active_ref[...] = active
+    go(active_ref)
     pack(dot(active, out_ref[...]).astype(bf16), 0, back_ref)
 
 
 def expert_backward(got_ref, before_ref, in_ref, out_ref, grads_ref, down_ref, back_ref):
     unpack(got_ref, 0, grads_ref)
+    go(grads_ref)
     grad_active = dot(grads_ref[...], out_ref[...], 1, 1)
     grad_before = (grad_active * gelu_slope(before_ref[...])).astype(bf16)
     down_ref[...] = grad_before
+    go(down_ref)
     pack(dot(grad_before, in_ref[...], 1, 1).astype(bf16), 0, back_ref)
 
 
 def expert_both(got_ref, in_ref, out_ref, rows_ref, active_ref, grads_ref, down_ref, back_ref):
     unpack(got_ref, 0, rows_ref)
     unpack(got_ref, SENT, grads_ref)
+    go(rows_ref, grads_ref)
     before = dot(rows_ref[...], in_ref[...])
     active = gelu(before).astype(bf16)
     active_ref[...] = active
+    go(active_ref)
     pack(dot(active, out_ref[...]).astype(bf16), 0, back_ref)
     grad_active = dot(grads_ref[...], out_ref[...], 1, 1)
     grad_before = (grad_active * gelu_slope(before)).astype(bf16)
     down_ref[...] = grad_before
+    go(down_ref)
     pack(dot(grad_before, in_ref[...], 1, 1).astype(bf16), SENT, back_ref)
 
 
 def expert_grads_top(rows_ref, active_ref, grads_ref, down_ref, in_grad_ref, out_grad_ref):
     in_grad_ref[0, 0] = dot(rows_ref[...], down_ref[...], 0)
     out_grad_ref[0, 0] = dot(active_ref[...], grads_ref[...], 0)
+
+
+def expert_grads_low(rows_ref, active_ref, grads_ref, down_ref, _, __, in_grad_ref, out_grad_ref):
+    expert_grads_top(rows_ref, active_ref, grads_ref, down_ref, in_grad_ref, out_grad_ref)
 
 
 def combine_first(got_ref, across_ref, gates_ref, part_ref, picked_ref):
@@ -357,22 +497,24 @@
     part_ref[:, HALF:] = right.astype(bf16)
 
 
-def gate_lanes(grads):
-    place = iota((ROWS, 128), 1)
-    both = jnp.where(place == 0, grads[0], jnp.where(place == 1, grads[1], 0.0))
-    high = both.astype(bf16)
-    moved = jnp.where(place == 2, grads[0], jnp.where(place == 3, grads[1], 0.0))
-    low = (moved - moved.astype(bf16).astype(f32)).astype(bf16)
-    return high + low
-
-
-def gathered_back(got_ref, offset, across, into_ref):
+def gate_rows(grads):
+    place = iota((8, ROWS), 0)
+    rows = [row_of(grad, ROWS) for grad in grads]
+    both = jnp.where(place == 0, rows[0], jnp.where(place == 1, rows[1], 0.0))
+    moved = jnp.where(place == 2, rows[0], jnp.where(place == 3, rows[1], 0.0))
+    left = moved - moved.astype(bf16).astype(f32)
+    return (both + left).astype(bf16)
+
+
+def gathered_back(got_ref, offset, across, rows, into_ref):
     main = got_ref[:, offset : offset + WIDTH]
     rest = got_ref[:, offset + WIDTH : offset + SENT]
     left, right = pick(across, 0, main, rest)
     other_left, other_right = pick(across, 1, main, rest)
-    into_ref[:, :HALF] = (left + other_left).astype(bf16)
-    into_ref[:, HALF:WIDTH] = (right + other_right).astype(bf16)
+    into_ref[:ROWS, :HALF] = (left + other_left).astype(bf16)
+    into_ref[:ROWS, HALF:] = (right + other_right).astype(bf16)
+    into_ref[ROWS:, :ROWS] = rows
+    into_ref[ROWS:, ROWS:] = jnp.zeros((8, WIDTH - ROWS), bf16)
 
 
 def combine_next(got_ref, across_ref, gates_ref, cotangent_ref, part_ref, back_ref):
@@ -389,13 +531,11 @@
         )
     part_ref[:, :HALF] = left.astype(bf16)
     part_ref[:, HALF:] = right.astype(bf16)
-    gathered_back(got_ref, SENT, across, back_ref)
-    back_ref[:, WIDTH:] = gate_lanes(grads)
-
-
-def combine_back(got_ref, across_ref, lanes_ref, back_ref):
-    gathered_back(got_ref, 0, across_ref[...], back_ref)
-    back_ref[:, WIDTH:] = lanes_ref[...]
+    gathered_back(got_ref, SENT, across, gate_rows(grads), back_ref)
+
+
+def combine_back(got_ref, across_ref, rows_ref, back_ref):
+    gathered_back(got_ref, 0, across_ref[...], rows_ref[...], back_ref)
 
 
 def attention_back(
@@ -413,7 +553,7 @@
     triple_ref,
     weights_ref,
     qkv_ref,
-    ids_ref,
+    hot_ref,
     after_ref,
     low_ref,
     back_triple_ref,
@@ -426,9 +566,8 @@
     gates = gates_ref[...]
     across = across_ref[...]
     gate = [gates[:, k : k + 1] for k in range(2)]
-    grad_gate = [
-        total[:, WIDTH + k : WIDTH + k + 1] + total[:, WIDTH + 2 + k : WIDTH + 3 + k] for k in range(2)
-    ]
+    rows = total[ROWS:, :ROWS]
+    grad_gate = [column_of(rows[k : k + 1] + rows[k + 2 : k + 3], ROWS) for k in range(2)]
     mean = gate[0] * grad_gate[0] + gate[1] * grad_gate[1]
     lane = iota((ROWS, EXPERTS), 1).astype(f32)
     grad_logits = 0.0
@@ -441,12 +580,13 @@
     logits_ref[:, :EXPERTS] = high
     logits_ref[:, EXPERTS : 2 * EXPERTS] = low
     logits_ref[:, 2 * EXPERTS :] = jnp.zeros((ROWS, 128 - 2 * EXPERTS), bf16)
-    grad_low = total[:, :WIDTH] + dot(high, router_ref[...], 1, 1) + dot(low, router_ref[...], 1, 1)
-    grad_middle, gain_grad_ref[...] = norm_back(middle_ref[...], gain_ref[...], grad_low)
+    grad_low = total[:ROWS] + dot(high, router_ref[...]) + dot(low, router_ref[...])
+    grad_middle, gain_grad_ref[...] = norm_back(middle_ref[...], gain_ref[1:2, :], grad_low)
     after = gradient_ref[...].astype(f32) + grad_middle
     after_ref[...] = after
     low_after = after.astype(bf16)
     low_ref[...] = low_after
+    go(after_ref, low_ref, logits_ref, gain_grad_ref)
     grad_mixture = dot(low_after, out_ref[...], 1, 1).astype(bf16)
     queries, keys, values = triple_ref[0], triple_ref[1], triple_ref[2]
     grad_queries = jnp.zeros((ROWS, QUARTER), f32)
@@ -470,28 +610,29 @@
         diagonals = jnp.where(
             iota((8, 256), 0) == head, jnp.sum(turned, axis=0, keepdims=True), diagonals
         )
-    hot = (iota((EXPERTS, 256), 0) == ids_ref[...]).astype(f32)
-    table_grad_ref[...] = dot(diagonals, hot, 1, 1, precision=highest)
+    table_grad_ref[...] = dot(hot_ref[...], diagonals, 1, 1, precision=highest)
     grad_input = 0.0
     for k, grad in enumerate((grad_queries * HEAD**-0.5, grad_keys * HEAD**-0.5, grad_values)):
         grad = grad.astype(bf16)
         back_triple_ref[:, k * QUARTER : (k + 1) * QUARTER] = grad
-        grad_input = grad_input + dot(grad, qkv_ref[k], 1, 1)
+        grad_input = grad_input + dot(grad, qkv_ref[k])
+    go(back_triple_ref)
     part_ref[...] = grad_input.astype(bf16)
 
 
 def weight_grads(low_ref, back_triple_ref, mixture_ref, after_ref, low_two_ref, logits_ref, grads_ref):
     kind = grads_ref.dtype
-    grads_ref[:, : 3 * QUARTER] = dot(low_ref[...], back_triple_ref[...], 0).astype(kind)
-    for part in range(4):
-        grads_ref[part * QUARTER : (part + 1) * QUARTER, 3 * QUARTER : WIDTH] = dot(
-            mixture_ref[...], after_ref[:, part * QUARTER : (part + 1) * QUARTER], 0
-        ).astype(kind)
-    both = dot(low_two_ref[...], logits_ref[...], 0)
-    grads_ref[:, WIDTH : WIDTH + EXPERTS] = (
-        both[:, :EXPERTS] + both[:, EXPERTS : 2 * EXPERTS]
-    ).astype(kind)
-    grads_ref[:, WIDTH + EXPERTS :] = jnp.zeros((WIDTH, 128 - EXPERTS), kind)
+    qkv_rows = 3 * QUARTER
+    grads_ref[:qkv_rows, :WIDTH] = dot(back_triple_ref[...], low_ref[...], 0).astype(kind)
+    grads_ref[qkv_rows:, :WIDTH] = dot(mixture_ref[...], after_ref[...], 0).astype(kind)
+    both = dot(logits_ref[...], low_two_ref[...], 0)
+    total = both[:EXPERTS] + both[EXPERTS : 2 * EXPERTS]
+    for part in range(WIDTH // 128):
+        grads_ref[part * EXPERTS : (part + 1) * EXPERTS, WIDTH:] = total[
+            :, part * 128 : (part + 1) * 128
+        ].astype(kind)
+    used = WIDTH // 128 * EXPERTS
+    grads_ref[used:, WIDTH:] = jnp.zeros((WIDTH - used, 128), kind)
 
 
 def start_back(
@@ -507,26 +648,27 @@
     picked_ref,
     gradient_ref,
     gain_grad_ref,
-    lanes_ref,
+    rows_ref,
     send_ref,
 ):
     grad_low = four(d0[...], d1[...], d2[...], d3[...])
-    grad_input, gain_grad_ref[...] = norm_back(input_ref[...].astype(f32), gain_ref[...], grad_low)
+    grad_input, gain_grad_ref[...] = norm_back(input_ref[...].astype(f32), gain_ref[0:1, :], grad_low)
     gradient = after_ref[...] + grad_input
     gradient_ref[...] = gradient
+    go(gradient_ref, gain_grad_ref)
     gates = gates_ref[...]
     weighted = [(gates[:, k : k + 1] * gradient).astype(bf16) for k in range(2)]
     main, rest = dispatch(down_ref[...], weighted)
     send_ref[:, :WIDTH] = main
     send_ref[:, WIDTH:] = rest
-    lanes_ref[...] = gate_lanes(
+    rows_ref[...] = gate_rows(
         [jnp.sum(gradient * picked_ref[k].astype(f32), axis=1, keepdims=True) for k in range(2)]
     )
 
 
 def finish_back(after_ref, d0, d1, d2, d3, input_ref, gain_ref, gradient_ref, gain_grad_ref):
     grad_low = four(d0[...], d1[...], d2[...], d3[...])
-    grad_input, gain_grad_ref[...] = norm_back(input_ref[...].astype(f32), gain_ref[...], grad_low)
+    grad_input, gain_grad_ref[...] = norm_back(input_ref[...].astype(f32), gain_ref[0:1, :], grad_low)
     gradient_ref[...] = after_ref[...] + grad_input
 
 
@@ -534,47 +676,80 @@
     output_ref[...] = (middle_ref[...] + four(z0[...], z1[...], z2[...], z3[...])).astype(bf16)
 
 
+SHARE = WIDTH // EXPERTS
+
+
+def total_of(chunks_ref):
+    total = chunks_ref[0:SHARE, :].astype(f32)
+    for block in range(1, EXPERTS):
+        total = total + chunks_ref[block * SHARE : (block + 1) * SHARE, :].astype(f32)
+    return total.astype(bf16)
+
+
+def add_chunks_top(chunks_ref, spread_ref):
+    total = total_of(chunks_ref)
+    for block in range(EXPERTS):
+        spread_ref[block * SHARE : (block + 1) * SHARE, :] = total
+
+
 def add_chunks(chunks_ref, g00, g01, g10, g11, t0, t1, spread_ref):
-    share = WIDTH // EXPERTS
-    total = chunks_ref[0:share, :].astype(f32)
-    for block in range(1, EXPERTS):
-        total = total + chunks_ref[block * share : (block + 1) * share, :].astype(f32)
-    total = total.astype(bf16)
+    total = total_of(chunks_ref)
     row = iota((8, WIDTH), 0)
     gains = jnp.zeros((8, WIDTH), f32)
     for place, gain in enumerate((g00, g01, g10, g11)):
         gains = jnp.where(row == place, gain[...], gains)
-    tables = jnp.concatenate([t0[0:4, :], t1[0:4, :]], axis=0)
-    tables = jnp.concatenate([tables, jnp.zeros((8, 128 - EXPERTS), f32)], axis=1)
-    small = jnp.concatenate([gains, tables], axis=1).astype(bf16)
+    spread = 0.0
+    for layer, table in enumerate((t0, t1)):
+        lifted = table[...].astype(bf16)
+        rows = iota((8, EXPERTS), 0)
+        for turn in range(4):
+            chosen = one_hot(iota((8, EXPERTS), 1) == rows * 4 + turn)
+            start = turn * 32 + layer * 8
+            onto = one_hot(iota((8, 128), 1) == iota((8, 128), 0) + start)
+            spread = spread + dot(dot(chosen, lifted).astype(bf16), onto)
+    small = jnp.concatenate([gains, spread], axis=1).astype(bf16)
     for block in range(EXPERTS):
-        spread_ref[block * 32 : block * 32 + share, :] = total
-        spread_ref[block * 32 + share : block * 32 + 32, :] = small
+        spread_ref[block * 32 : block * 32 + SHARE, :] = total
+        spread_ref[block * 32 + SHARE : block * 32 + 32, :] = small
+
+
+def place_top(top_ref, qkv_ref, out_ref, router_ref):
+    for k in range(3):
+        qkv_ref[1, k] = top_ref[k * QUARTER : (k + 1) * QUARTER, :WIDTH].astype(f32)
+    out_ref[1] = top_ref[3 * QUARTER :, :WIDTH].astype(f32)
+    for part in range(WIDTH // 128):
+        router_ref[1, :, part * 128 : (part + 1) * 128] = top_ref[
+            part * EXPERTS : (part + 1) * EXPERTS, WIDTH:
+        ].astype(f32)
 
 
 def place_grads(top_ref, all_ref, qkv_ref, out_ref, router_ref, gains_ref, tables_ref):
-    share = WIDTH // EXPERTS
     small = jnp.zeros((8, SUMMED), f32)
+    place_top(top_ref, qkv_ref, out_ref, router_ref)
     for block in range(EXPERTS):
-        rows = slice(block * share, (block + 1) * share)
-        chunk = all_ref[block * 32 : block * 32 + share, :].astype(f32)
-        small = small + all_ref[block * 32 + share : block * 32 + 32, :].astype(f32)
-        for k in range(3):
-            qkv_ref[0, k, rows, :] = chunk[:, k * QUARTER : (k + 1) * QUARTER]
-        part, first = divmod(block * share, QUARTER)
-        out_ref[0, first : first + share, part * QUARTER : (part + 1) * QUARTER] = chunk[
-            :, 3 * QUARTER : WIDTH
-        ]
-        router_ref[0, rows, :] = chunk[:, WIDTH : WIDTH + EXPERTS]
-    for k in range(3):
-        qkv_ref[1, k] = top_ref[:, k * QUARTER : (k + 1) * QUARTER]
-    for part in range(4):
-        out_ref[1, :, part * QUARTER : (part + 1) * QUARTER] = top_ref[
-            part * QUARTER : (part + 1) * QUARTER, 3 * QUARTER : WIDTH
-        ]
-    router_ref[1] = top_ref[:, WIDTH : WIDTH + EXPERTS]
-    gains_ref[...] = small[:, :WIDTH]
-    tables_ref[...] = small[:, WIDTH:]
+        chunk = all_ref[block * 32 : block * 32 + SHARE, :].astype(f32)
+        small = small + all_ref[block * 32 + SHARE : block * 32 + 32, :].astype(f32)
+        which, first = divmod(block * SHARE, QUARTER)
+        if which < 3:
+            qkv_ref[0, which, first : first + SHARE, :] = chunk[:, :WIDTH]
+        else:
+            out_ref[0, first : first + SHARE, :] = chunk[:, :WIDTH]
+        for row in range(0, SHARE, 8):
+            part, inside = divmod(block * SHARE + row, EXPERTS)
+            if part < WIDTH // 128:
+                router_ref[0, inside : inside + 8, part * 128 : (part + 1) * 128] = chunk[
+                    row : row + 8, WIDTH:
+                ]
+    for layer in range(2):
+        gains_ref[layer] = small[2 * layer : 2 * layer + 2, :WIDTH]
+        lanes = small[:, WIDTH:]
+        table = 0.0
+        for turn in range(4):
+            rows = one_hot(iota((EXPERTS, 8), 0) == iota((EXPERTS, 8), 1) * 4 + turn)
+            spread = dot(rows.astype(f32), lanes, precision=highest)
+            from_lane = (iota((128, 8), 0) == iota((128, 8), 1) + turn * 32 + layer * 8).astype(f32)
+            table = table + dot(spread, from_lane, precision=highest)
+        tables_ref[layer] = table[:, :HERE]
 
 
 def around(values):
@@ -602,48 +777,67 @@
     expert_out,
     cotangent,
 ):
-    ids = jnp.pad(jnp.flip(bucket_ids), (0, 1), constant_values=-1).reshape(1, 256)
-    table = jnp.pad(bias_table.transpose(0, 2, 1).reshape(2 * HERE, EXPERTS), ((0, 2), (0, 0)))
-    gains = norm_gains.reshape(4, 1, WIDTH)
+    qkv = proj_qkv.transpose(0, 1, 3, 2)
+    router = router.transpose(0, 2, 1)
+    expert_in, expert_out = expert_in[:, 0], expert_out[:, 0]
+    gains = norm_gains
     row = (ROWS, WIDTH)
     narrow = (ROWS, QUARTER)
     scores = (HERE, ROWS, ROWS)
     slots = (MAIN + REST, WIDTH)
-    bias, across, down = call(
+    stacked = (2, 1, WIDTH, WIDTH)
+    bias, across, down, hot = call(
         setup,
-        [((2 * HERE, ROWS, ROWS), f32), ((2, ROWS, ROWS), f32), ((2, 8, ROWS), f32)],
-        ids,
-        table,
-        segment_ids,
-        expert_routes,
-    )
-    kept = [(row, bf16), ((3, *narrow), bf16), (scores, f32), (narrow, bf16), (row, bf16)]
+        [
+            ((2, HERE, ROWS, ROWS), f32),
+            ((2, ROWS, ROWS), f32),
+            ((2, 8, ROWS), f32),
+            ((EXPERTS, 256), f32),
+        ],
+        Late(bucket_ids.reshape(1, -1)),
+        Late(bias_table.transpose(0, 2, 1)),
+        Late(segment_ids),
+        Late(expert_routes.transpose(0, 2, 1)),
+    )
+    kept = [
+        Kept(row, bf16),
+        Kept((3, *narrow), bf16),
+        Kept(scores, f32),
+        Kept(narrow, bf16),
+        (row, bf16),
+    ]
 
     low_a0, triple0, weights0, mixture0, part = call(
-        attention_first, kept, tokens, gains[0], proj_qkv[0], bias[:HERE], proj_out[0]
+        attention_first,
+        kept,
+        Late(tokens),
+        Late(Layer(gains, 0)),
+        Late(Layer(qkv, 0)),
+        Layer(bias, 0),
+        Late(Layer(proj_out, 0)),
     )
     middle0, low_b0, gates0, send = call(
         route_first,
-        [(row, f32), (row, bf16), ((ROWS, ROWS), f32), ((MAIN, SENT), bf16)],
+        [Kept(row, f32), Kept(row, bf16), ((ROWS, ROWS), f32), ((MAIN, SENT), bf16)],
         tokens,
         *around(part),
-        gains[1],
-        router[0],
-        across[0],
-        down[0],
+        Layer(gains, 0),
+        Layer(router, 0),
+        Layer(across, 0),
+        Layer(down, 0),
     )
     rows0, before0, active0, send = call(
         expert_forward,
-        [(slots, bf16), (slots, f32), (slots, bf16), ((MAIN, SENT), bf16)],
+        [Kept(slots, bf16), Kept(slots, f32), Kept(slots, bf16), ((MAIN, SENT), bf16)],
         across_experts(send),
-        expert_in[0, 0],
-        expert_out[0, 0],
+        Layer(expert_in, 0),
+        Layer(expert_out, 0),
     )
     part, picked0 = call(
         combine_first,
-        [(row, bf16), ((2, *row), bf16)],
+        [(row, bf16), Kept((2, *row), bf16)],
         across_experts(send),
-        across[0],
+        Layer(across, 0),
         gates0,
     )
 
@@ -652,67 +846,71 @@
         [(row, f32), *kept],
         middle0,
         *around(part),
-        gains[2],
-        proj_qkv[1],
-        bias[HERE:],
-        proj_out[1],
+        Layer(gains, 1),
+        Layer(qkv, 1),
+        Layer(bias, 1),
+        Layer(proj_out, 1),
     )
     middle1, low_b1, gates1, send = call(
         route_next,
-        [(row, f32), (row, bf16), ((ROWS, ROWS), f32), ((MAIN, 2 * SENT), bf16)],
+        [Kept(row, f32), Kept(row, bf16), ((ROWS, ROWS), f32), ((MAIN, 2 * SENT), bf16)],
         current1,
         *around(part),
-        gains[3],
-        router[1],
-        across[1],
-        down[1],
+        Layer(gains, 1),
+        Layer(router, 1),
+        Layer(across, 1),
+        Layer(down, 1),
         cotangent,
     )
     rows1, active1, grads1, down1, send = call(
         expert_both,
-        [(slots, bf16), (slots, bf16), (slots, bf16), (slots, bf16), ((MAIN, 2 * SENT), bf16)],
+        [*[Kept(slots, bf16)] * 4, ((MAIN, 2 * SENT), bf16)],
         across_experts(send),
-        expert_in[1, 0],
-        expert_out[1, 0],
+        Layer(expert_in, 1),
+        Layer(expert_out, 1),
+    )
+    got = across_experts(send)
+    in_grads, out_grads = call_stacked(
+        expert_grads_top, 1, (rows1, active1, grads1, down1), stacked
     )
     moved, back = call(
         combine_next,
-        [(row, bf16), ((ROWS, SUMMED), bf16)],
-        across_experts(send),
-        across[1],
+        [(row, bf16), ((LONG, WIDTH), bf16)],
+        got,
+        Layer(across, 1),
         gates1,
         cotangent,
     )
 
     back_kept = [
-        (row, f32),
+        Kept(row, f32),
+        Kept(row, bf16),
+        Kept((ROWS, 3 * QUARTER), bf16),
         (row, bf16),
-        ((ROWS, 3 * QUARTER), bf16),
-        (row, bf16),
-        ((ROWS, 128), bf16),
-        ((1, WIDTH), f32),
-        ((8, EXPERTS), f32),
+        Kept((ROWS, 128), bf16),
+        Kept((1, WIDTH), f32),
+        Kept((EXPERTS, 8), f32),
     ]
     after1, low_after1, back_triple1, part, logits1, gain11, table1 = call(
         attention_back,
         back_kept,
         *around(back),
         gates1,
-        across[1],
-        router[1],
+        Layer(across, 1),
+        Layer(router, 1),
         middle1,
-        gains[3],
+        Layer(gains, 1),
         cotangent,
-        proj_out[1],
+        Layer(proj_out, 1),
         triple1,
         weights1,
-        proj_qkv[1],
-        ids,
+        Layer(qkv, 1),
+        hot,
     )
     parts = around(part)
     (top_grads,) = call(
         weight_grads,
-        [((WIDTH, SUMMED), f32)],
+        [Kept((WIDTH, SUMMED), bf16)],
         low_a1,
         back_triple1,
         mixture1,
@@ -720,51 +918,58 @@
         low_b1,
         logits1,
     )
-    top_grads = lax.psum(top_grads, "expert")
-    (output,) = call(finish_output, [(row, bf16)], middle1, *around(moved))
-
-    gradient0, gain10, lanes0, send = call(
+    top_grads = across_experts(top_grads)
+    top_grads, parts, in_grads = lax.optimization_barrier((top_grads, parts, in_grads))
+    (top_grads,) = call(add_chunks_top, [Kept((WIDTH, SUMMED), bf16)], top_grads)
+
+    gradient0, gain10, rows0b, send = call(
         start_back,
-        [(row, f32), ((1, WIDTH), f32), ((ROWS, 128), bf16), ((MAIN, SENT), bf16)],
-        after1,
+        [Kept(row, f32), Kept((1, WIDTH), f32), ((8, ROWS), bf16), ((MAIN, SENT), bf16)],
+        Late(after1),
         *parts,
-        current1,
-        gains[2],
+        Late(current1),
+        Late(Layer(gains, 1)),
         gates0,
-        down[0],
-        picked0,
+        Layer(down, 0),
+        Late(picked0),
     )
     grads0, down0, send = call(
         expert_backward,
-        [(slots, bf16), (slots, bf16), ((MAIN, SENT), bf16)],
+        [Kept(slots, bf16), Kept(slots, bf16), ((MAIN, SENT), bf16)],
         across_experts(send),
-        before0,
-        expert_in[0, 0],
-        expert_out[0, 0],
-    )
-    (back,) = call(
-        combine_back, [((ROWS, SUMMED), bf16)], across_experts(send), across[0], lanes0
-    )
+        Late(before0),
+        Late(Layer(expert_in, 0)),
+        Late(Layer(expert_out, 0)),
+    )
+    got = across_experts(send)
+    in_grads, out_grads = call_stacked(
+        expert_grads_low, 0, (rows0, active0, grads0, down0), stacked, (in_grads, out_grads)
+    )
+    (back,) = call(combine_back, [((LONG, WIDTH), bf16)], got, Layer(across, 0), rows0b)
+    backs = around(back)
+    top_grads, back = lax.optimization_barrier((top_grads, back))
+    top_grads = across_experts(top_grads)
+    top_grads, backs, in_grads = lax.optimization_barrier((top_grads, backs, in_grads))
+    (output,) = call(finish_output, [Kept(row, bf16)], middle1, *around(moved))
     after0, low_after0, back_triple0, part, logits0, gain01, table0 = call(
         attention_back,
         back_kept,
-        *around(back),
+        *backs,
         gates0,
-        across[0],
-        router[0],
+        Layer(across, 0),
+        Layer(router, 0),
         middle0,
-        gains[1],
+        Layer(gains, 0),
         gradient0,
-        proj_out[0],
+        Layer(proj_out, 0),
         triple0,
         weights0,
-        proj_qkv[0],
-        ids,
-    )
-    parts = around(part)
+        Layer(qkv, 0),
+        hot,
+    )
     (grads,) = call(
         weight_grads,
-        [((WIDTH, SUMMED), bf16)],
+        [Kept((WIDTH, SUMMED), bf16)],
         low_a0,
         back_triple0,
         mixture0,
@@ -772,52 +977,49 @@
         low_b0,
         logits0,
     )
+    parts = around(part)
     tokens_grad, gain00 = call(
         finish_back,
-        [(row, f32), ((1, WIDTH), f32)],
+        [Kept(row, f32), Kept((1, WIDTH), f32)],
         after0,
         *parts,
         tokens,
-        gains[0],
+        Layer(gains, 0),
     )
     (spread,) = call(
         add_chunks,
-        [((EXPERTS * 32, SUMMED), bf16)],
+        [Kept((EXPERTS * 32, SUMMED), bf16)],
         across_experts(grads),
-        gain00,
-        gain01,
-        gain10,
-        gain11,
-        table0,
-        table1,
-    )
-    qkv_grad, out_grad, router_grad, gain_grads, table_grads = call(
+        Late(gain00),
+        Late(gain01),
+        Late(gain10),
+        Late(gain11),
+        Late(table0),
+        Late(table1),
+    )
+    qkv_grad, out_grad, router_grad, gain_grads, table_grad = call(
         place_grads,
         [
-            ((2, 3, WIDTH, QUARTER), f32),
-            ((2, QUARTER, WIDTH), f32),
-            ((2, WIDTH, EXPERTS), f32),
-            ((8, WIDTH), f32),
-            ((8, 128), f32),
+            Kept((2, 3, QUARTER, WIDTH), f32),
+            Kept((2, QUARTER, WIDTH), f32),
+            Kept((2, EXPERTS, WIDTH), f32),
+            Kept((2, 2, WIDTH), f32),
+            Kept((2, EXPERTS, HERE), f32),
         ],
-        top_grads,
+        Late(top_grads),
         across_experts(spread),
-    )
-    table_grad = table_grads.reshape(2, 4, 128)[:, :HERE, :EXPERTS].transpose(0, 2, 1)
-    in_grad0 = dot(rows0, down0, 0)
-    out_grad0 = dot(active0, grads0, 0)
-    in_grad1 = dot(rows1, down1, 0)
-    out_grad1 = dot(active1, grads1, 0)
+        limit=24,
+    )
     return (
         output,
         tokens_grad,
-        qkv_grad,
+        qkv_grad.transpose(0, 1, 3, 2),
         out_grad,
         table_grad,
-        gain_grads[:4].reshape(2, 2, WIDTH),
-        router_grad,
-        jnp.stack([in_grad0, in_grad1])[:, None],
-        jnp.stack([out_grad0, out_grad1])[:, None],
+        gain_grads,
+        router_grad.transpose(0, 2, 1),
+        in_grads,
+        out_grads,
     )
 
 

time: 430 us -> 333 us (0.77)
  waiting for transfers between devices: 195 us -> 124 us
  local copies, waits for them, and re-layouts: 52.6 us -> 17.2 us
  Pallas kernels: 32.8 us -> 55.6 us
  between operations: 14.9 us -> 1.14 us
  other arithmetic: 4.98 us -> 0 us
  blocking collectives: 92.5 us -> 97.3 us
  starting transfers between devices: 32 us -> 36.8 us
    psum x1 -> x0, waiting for transfers between devices: 91.5 us -> none  [shards(): top_grads = lax.psum(top_grads, 'expert')]
    all_to_all x3 -> x5, waiting for transfers between devices: 14.9 us -> 40.7 us  [across_experts(): return lax.all_to_all(values, 'expert', 0, 0, tiled=True)]
    unnamed x202 -> x88, local copies, waits for them, and re-layouts: 41.1 us -> 17.2 us
    pallas_call x20 -> x23, Pallas kernels: 32.8 us -> 55.6 us  [the longest x21 46 us: call(): pl.pallas_call(kernel, out_shape=[pltpu.HBM(*o) if is_kept else jax.Shape...]
    squeeze x5 -> x0, local copies, waits for them, and re-layouts: 7.13 us -> none  [the longest x1 4.05 us: shards(): expert_out[1, 0]]
    ppermute x24, waiting for transfers between devices: 88.7 us -> 82.9 us  [around(): lax.ppermute(values, 'tensor', [(i, (i + shift) % 4) for i in range(4)])]
    unnamed x2 -> x0, other arithmetic: 4.98 us -> none
    all_to_all x5, blocking collectives: 92.5 us -> 97.3 us  [across_experts(): return lax.all_to_all(values, 'expert', 0, 0, tiled=True)]
  transfers between devices with their start and end apart: 28 -> 29, of which waited for: 26 -> 27; matrix products, arithmetic and copies ran while one was open for 4% -> 0% of each run, Pallas kernels for 1% -> 4%
where the time goes in v2:
time: 333 us; the launch traced here: 332 us
  waiting for transfers between devices  124 us (37%)
  blocking collectives  97.3 us (29%)
  Pallas kernels  55.6 us (17%)
  starting transfers between devices  36.8 us (11%)
  local copies, waits for them, and re-layouts  17.2 us (5%)
    all_to_all x5, blocking collectives, across_experts(): return lax.all_to_all(values, 'expert', 0, 0, tiled=True)  97.3 us
    ppermute x24, waiting for transfers between devices, around(): lax.ppermute(values, 'tensor', [(i, (i + shift) % 4) for i in range(4)])  82.9 us
    pallas_call x21, Pallas kernels, call(): pl.pallas_call(kernel, out_shape=[pltpu.HBM(*o) if is_kept else jax.Shape...  46 us
    all_to_all x5, waiting for transfers between devices, across_experts(): return lax.all_to_all(values, 'expert', 0, 0, tiled=True)  40.7 us
    all_to_all x5, starting transfers between devices, across_experts(): return lax.all_to_all(values, 'expert', 0, 0, tiled=True)  21.4 us
    unnamed x88, local copies, waits for them, and re-layouts  17.2 us
    ppermute x24, starting transfers between devices, around(): lax.ppermute(values, 'tensor', [(i, (i + shift) % 4) for i in range(4)])  15.4 us
    pallas_call x2, Pallas kernels, call_stacked(): pl.pallas_call(body, grid=(1,), out_shape=[jax.ShapeDtypeStruct(stacked,...  9.62 us
  transfers between devices with their start and end apart: 29, of which 27 were waited for; matrix products, arithmetic and copies ran while one was open for 0% of the time, Pallas kernels for 4%

profile of v2, /device:TPU:1, one launch (start us, length us, event | category | flops | bytes accessed | tf_op | source)
XLA Modules:
  0.0 331.6 jit_solution(5304671256462989057)
XLA Ops:
  1.9 1.8 setup.1
  3.8 3.4 %attention_first.1 = (bf16[128,768]{1,0:T(8,128)(2,1)}, bf16[3,128,192]{2,1,0:T(8,128)(2,1)}, f32[3,128,128]{2,1,0:T(8,128)}, bf16[128,192]{1,0:T(8,128)(2,1)}, bf16[128,768]{1,0:T(8,128)(2,1)S(1)}) custom-call(bf16[128,768]{1,0:T(8,128)(2,1)} %refs_5_.7, f32[2,2,768]{2,1,0:T(2,128)} %refs_6_.3, bf16[2,3,192,768]{3,2,1,0:T(8,128)(2,1)} %bitcast.31, ...), custom_call_target="tpu_custom_call" | custom-call | tf_op jit(solution)/shard_map/attention_first/pallas_call | solution.py:131
  7.2 3.6 %collective-permute-start.2 = (bf16[128,768]{1,0:T(8,128)(2,1)S(1)}, bf16[128,768]{1,0:T(8,128)(2,1)S(1)}, u32[]{:S(2)}, u32[]{:S(2)}) collective-permute-start(bf16[128,768]{1,0:T(8,128)(2,1)S(1)} %get-tuple-element.91.refs_1_), channel_id=1, source_target_pairs={{0,3},{1,0},{2,1},{3,2},{4,7},{5,4},{6,5},{7,6},{8,11},{9,8},{10,9... | collective-permute-start | bytes 589832 | tf_op jit(solution)/shard_map/ppermute | solution.py:757
  11.9 6.6 %collective-permute-done.2.refs_4_ = bf16[128,768]{1,0:T(8,128)(2,1)S(1)} collective-permute-done((bf16[128,768]{1,0:T(8,128)(2,1)S(1)}, bf16[128,768]{1,0:T(8,128)(2,1)S(1)}, u32[]{:S(2)}, u32[]{:S(2)}) %collective-permute-start.2) | collective-permute-done | bytes 196640 | tf_op jit(solution)/shard_map/ppermute | solution.py:757
  18.5 4.9 %collective-permute-done.refs_2_ = bf16[128,768]{1,0:T(8,128)(2,1)S(1)} collective-permute-done((bf16[128,768]{1,0:T(8,128)(2,1)S(1)}, bf16[128,768]{1,0:T(8,128)(2,1)S(1)}, u32[]{:S(2)}, u32[]{:S(2)}) %collective-permute-start) | collective-permute-done | bytes 196640 | tf_op jit(solution)/shard_map/ppermute | solution.py:757
  24.4 20.5 %all_to_all.112 = bf16[32,8,1152]{2,1,0:T(8,128)(2,1)S(1)} all-to-all(bf16[32,8,1152]{2,1,0:T(8,128)(2,1)S(1)} %bitcast.57), channel_id=1, replica_groups=mesh['expert'=32,'tensor'=4] {'expert'}, dimensions={0} | all-to-all | bytes 1179648 | tf_op jit(solution)/shard_map/all_to_all | solution.py:763
  44.9 2.1 expert_forward.1
  47.0 15.9 %all_to_all.113 = bf16[32,8,1152]{2,1,0:T(8,128)(2,1)S(1)} all-to-all(bf16[32,8,1152]{2,1,0:T(8,128)(2,1)S(1)} %bitcast.58), channel_id=1, replica_groups=mesh['expert'=32,'tensor'=4] {'expert'}, dimensions={0} | all-to-all | bytes 1179648 | tf_op jit(solution)/shard_map/all_to_all | solution.py:763
  65.6 5.2 %collective-permute-done.5.refs_4_ = bf16[128,768]{1,0:T(8,128)(2,1)S(1)} collective-permute-done((bf16[128,768]{1,0:T(8,128)(2,1)S(1)}, bf16[128,768]{1,0:T(8,128)(2,1)S(1)}, u32[]{:S(2)}, u32[]{:S(2)}) %collective-permute-start.5) | collective-permute-done | bytes 196640 | tf_op jit(solution)/shard_map/ppermute | solution.py:757
  70.8 1.7 collective-permute-done.4.refs_3_
  72.5 4.6 %collective-permute-done.3.refs_2_ = bf16[128,768]{1,0:T(8,128)(2,1)S(1)} collective-permute-done((bf16[128,768]{1,0:T(8,128)(2,1)S(1)}, bf16[128,768]{1,0:T(8,128)(2,1)S(1)}, u32[]{:S(2)}, u32[]{:S(2)}) %collective-permute-start.3) | collective-permute-done | bytes 196640 | tf_op jit(solution)/shard_map/ppermute | solution.py:757
  77.1 2.0 attention_next.1
  80.7 4.6 %collective-permute-done.8.refs_4_ = bf16[128,768]{1,0:T(8,128)(2,1)S(1)} collective-permute-done((bf16[128,768]{1,0:T(8,128)(2,1)S(1)}, bf16[128,768]{1,0:T(8,128)(2,1)S(1)}, u32[]{:S(2)}, u32[]{:S(2)}) %collective-permute-start.8) | collective-permute-done | bytes 196640 | tf_op jit(solution)/shard_map/ppermute | solution.py:757
  86.6 5.5 %collective-permute-done.6.refs_2_ = bf16[128,768]{1,0:T(8,128)(2,1)S(1)} collective-permute-done((bf16[128,768]{1,0:T(8,128)(2,1)S(1)}, bf16[128,768]{1,0:T(8,128)(2,1)S(1)}, u32[]{:S(2)}, u32[]{:S(2)}) %collective-permute-start.6) | collective-permute-done | bytes 196640 | tf_op jit(solution)/shard_map/ppermute | solution.py:757
  93.4 22.5 %all_to_all.114 = bf16[32,8,2304]{2,1,0:T(8,128)(2,1)S(1)} all-to-all(bf16[32,8,2304]{2,1,0:T(8,128)(2,1)S(1)} %bitcast.53), channel_id=1, replica_groups=mesh['expert'=32,'tensor'=4] {'expert'}, dimensions={0} | all-to-all | bytes 2359296 | tf_op jit(solution)/shard_map/all_to_all | solution.py:763
  115.9 3.3 expert_both.1
  119.1 22.5 %all_to_all.115 = bf16[32,8,2304]{2,1,0:T(8,128)(2,1)S(1)} all-to-all(bf16[32,8,2304]{2,1,0:T(8,128)(2,1)S(1)} %bitcast.54), channel_id=1, replica_groups=mesh['expert'=32,'tensor'=4] {'expert'}, dimensions={0} | all-to-all | bytes 2359296 | tf_op jit(solution)/shard_map/all_to_all | solution.py:763
  144.6 4.9 %collective-permute-done.14.refs_3_ = bf16[136,768]{1,0:T(8,128)(2,1)S(1)} collective-permute-done((bf16[136,768]{1,0:T(8,128)(2,1)S(1)}, bf16[136,768]{1,0:T(8,128)(2,1)S(1)}, u32[]{:S(2)}, u32[]{:S(2)}) %collective-permute-start.14) | collective-permute-done | bytes 208928 | tf_op jit(solution)/shard_map/ppermute | solution.py:757
  149.5 1.9 collective-permute-done.13.refs_2_
  151.3 5.5 %collective-permute-done.12.refs_1_ = bf16[136,768]{1,0:T(8,128)(2,1)S(1)} collective-permute-done((bf16[136,768]{1,0:T(8,128)(2,1)S(1)}, bf16[136,768]{1,0:T(8,128)(2,1)S(1)}, u32[]{:S(2)}, u32[]{:S(2)}) %collective-permute-start.12) | collective-permute-done | bytes 208928 | tf_op jit(solution)/shard_map/ppermute | solution.py:757
  156.8 2.7 attention_back.2
  162.2 1.6 weight_grads.2
  163.8 4.8 %all-to-all-start.4 = ((bf16[32,24,896]{2,1,0:T(8,128)(2,1)}), bf16[32,24,896]{2,1,0:T(8,128)(2,1)}, u32[]{:S(2)}, u32[]{:S(2)}) async-start(bf16[32,24,896]{2,1,0:T(8,128)(2,1)} %bitcast.61), calls=%async_computation.4 | async-start | bytes 2752512 | tf_op jit(solution)/shard_map/all_to_all | solution.py:763
  170.2 4.8 %expert_grads_top.1 = (f32[2,1,768,768]{3,2,1,0:T(8,128)}, f32[2,1,768,768]{3,2,1,0:T(8,128)}) custom-call(bf16[384,768]{1,0:T(8,128)(2,1)} %get-tuple-element.117.rows_ref, bf16[384,768]{1,0:T(8,128)(2,1)} %get-tuple-element.118.active_ref, bf16[384,768]{1,0:T(8,128)(2,1)} %get-tuple-element.119.grads_ref, bf16[384,768]{1,0:T(8,128)(2,1)} %get-tuple-element.120.down_ref), custom_call_target="tpu_custom_call" | custom-call | tf_op jit(solution)/shard_map/expert_grads_top/pallas_call | solution.py:147
  176.4 5.2 %collective-permute-done.15.refs_2_ = bf16[128,768]{1,0:T(8,128)(2,1)S(1)} collective-permute-done((bf16[128,768]{1,0:T(8,128)(2,1)S(1)}, bf16[128,768]{1,0:T(8,128)(2,1)S(1)}, u32[]{:S(2)}, u32[]{:S(2)}) %collective-permute-start.15) | collective-permute-done | bytes 196640 | tf_op jit(solution)/shard_map/ppermute | solution.py:757
  182.3 6.9 %all-to-all-done.4 = bf16[32,24,896]{2,1,0:T(8,128)(2,1)} async-done(((bf16[32,24,896]{2,1,0:T(8,128)(2,1)}), bf16[32,24,896]{2,1,0:T(8,128)(2,1)}, u32[]{:S(2)}, u32[]{:S(2)}) %all-to-all-start.4) | async-done | bytes 1376288 | tf_op jit(solution)/shard_map/all_to_all | solution.py:763
  190.2 2.2 start_back.1
  192.4 15.9 %all_to_all.116 = bf16[32,8,1152]{2,1,0:T(8,128)(2,1)S(1)} all-to-all(bf16[32,8,1152]{2,1,0:T(8,128)(2,1)S(1)} %bitcast.55), channel_id=1, replica_groups=mesh['expert'=32,'tensor'=4] {'expert'}, dimensions={0} | all-to-all | bytes 1179648 | tf_op jit(solution)/shard_map/all_to_all | solution.py:763
  208.3 4.8 %expert_backward.1 = (bf16[384,768]{1,0:T(8,128)(2,1)}, bf16[384,768]{1,0:T(8,128)(2,1)}, bf16[256,1152]{1,0:T(8,128)(2,1)S(1)}) custom-call(bf16[256,1152]{1,0:T(8,128)(2,1)S(1)} %bitcast.45, f32[384,768]{1,0:T(8,128)} %get-tuple-element.130.refs_1_, bf16[2,768,768]{2,1,0:T(8,128)(2,1)} %bitcast.35, bf16[2,768,768]{2,1,0:T(8,128)(2,1)} %bitcast.38), custom_call_target="tpu_custom_call" | custom-call | tf_op jit(solution)/shard_map/expert_backward/pallas_call | solution.py:131
  214.0 3.7 %all-to-all-start.6 = ((bf16[32,8,1152]{2,1,0:T(8,128)(2,1)}), bf16[32,8,1152]{2,1,0:T(8,128)(2,1)S(1)}, u32[]{:S(2)}, u32[]{:S(2)}) async-start(bf16[32,8,1152]{2,1,0:T(8,128)(2,1)} %bitcast.56), calls=%async_computation.6 | async-start | bytes 1179648 | tf_op jit(solution)/shard_map/all_to_all | solution.py:763
  217.7 2.6 add_chunks_top.1
  220.3 9.6 %all-to-all-done.6 = bf16[32,8,1152]{2,1,0:T(8,128)(2,1)S(1)} async-done(((bf16[32,8,1152]{2,1,0:T(8,128)(2,1)}), bf16[32,8,1152]{2,1,0:T(8,128)(2,1)S(1)}, u32[]{:S(2)}, u32[]{:S(2)}) %all-to-all-start.6) | async-done | bytes 589856 | tf_op jit(solution)/shard_map/all_to_all | solution.py:763
  231.1 4.5 %all-to-all-start.7 = ((bf16[32,24,896]{2,1,0:T(8,128)(2,1)}), bf16[32,24,896]{2,1,0:T(8,128)(2,1)}, u32[]{:S(2)}, u32[]{:S(2)}) async-start(bf16[32,24,896]{2,1,0:T(8,128)(2,1)} %bitcast.60), calls=%async_computation.7 | async-start | bytes 2752512 | tf_op jit(solution)/shard_map/all_to_all | solution.py:763
  237.1 4.8 %expert_grads_low.1 = (f32[2,1,768,768]{3,2,1,0:T(8,128)}, f32[2,1,768,768]{3,2,1,0:T(8,128)}) custom-call(bf16[384,768]{1,0:T(8,128)(2,1)} %get-tuple-element.134.rows_ref, bf16[384,768]{1,0:T(8,128)(2,1)} %get-tuple-element.135.active_ref, bf16[384,768]{1,0:T(8,128)(2,1)} %get-tuple-element.136.grads_ref, ...), custom_call_target="tpu_custom_call", output_to_operand_aliasing={{0}: (4, {}), {1}: (5, {})} | custom-call | tf_op jit(solution)/shard_map/expert_grads_low/pallas_call | solution.py:147
  245.0 4.4 %collective-permute-done.18.refs_1_ = bf16[136,768]{1,0:T(8,128)(2,1)S(1)} collective-permute-done((bf16[136,768]{1,0:T(8,128)(2,1)}, bf16[136,768]{1,0:T(8,128)(2,1)S(1)}, u32[]{:S(2)}, u32[]{:S(2)}) %collective-permute-start.18) | collective-permute-done | bytes 208928 | tf_op jit(solution)/shard_map/ppermute | solution.py:757
  250.1 5.7 %all-to-all-done.7 = bf16[32,24,896]{2,1,0:T(8,128)(2,1)} async-done(((bf16[32,24,896]{2,1,0:T(8,128)(2,1)}), bf16[32,24,896]{2,1,0:T(8,128)(2,1)}, u32[]{:S(2)}, u32[]{:S(2)}) %all-to-all-start.7) | async-done | bytes 1376288 | tf_op jit(solution)/shard_map/all_to_all | solution.py:763
  260.5 3.7 %attention_back.3 = (f32[128,768]{1,0:T(8,128)}, bf16[128,768]{1,0:T(8,128)(2,1)}, bf16[128,576]{1,0:T(8,128)(2,1)}, bf16[128,768]{1,0:T(8,128)(2,1)S(1)}, bf16[...) custom-call(bf16[136,768]{1,0:T(8,128)(2,1)} %combine_back.1.refs_0_, bf16[136,768]{1,0:T(8,128)(2,1)S(1)} %copy-done.20, ...), custom_call_target="tpu_custom_call" | custom-call | tf_op jit(solution)/shard_map/attention_back/pallas_call | solution.py:131
  266.9 1.6 weight_grads.3
  268.6 4.2 %all-to-all-start.8 = ((bf16[32,24,896]{2,1,0:T(8,128)(2,1)}), bf16[32,24,896]{2,1,0:T(8,128)(2,1)S(1)}, u32[]{:S(2)}, u32[]{:S(2)}) async-start(bf16[32,24,896]{2,1,0:T(8,128)(2,1)} %bitcast.62), calls=%async_computation.8 | async-start | bytes 2752512 | tf_op jit(solution)/shard_map/all_to_all | solution.py:763
  274.3 4.7 %collective-permute-done.23.refs_4_ = bf16[128,768]{1,0:T(8,128)(2,1)S(1)} collective-permute-done((bf16[128,768]{1,0:T(8,128)(2,1)S(1)}, bf16[128,768]{1,0:T(8,128)(2,1)S(1)}, u32[]{:S(2)}, u32[]{:S(2)}) %collective-permute-start.23) | collective-permute-done | bytes 196640 | tf_op jit(solution)/shard_map/ppermute | solution.py:757
  280.6 5.2 %collective-permute-done.21.refs_2_ = bf16[128,768]{1,0:T(8,128)(2,1)S(1)} collective-permute-done((bf16[128,768]{1,0:T(8,128)(2,1)S(1)}, bf16[128,768]{1,0:T(8,128)(2,1)S(1)}, u32[]{:S(2)}, u32[]{:S(2)}) %collective-permute-start.21) | collective-permute-done | bytes 196640 | tf_op jit(solution)/shard_map/ppermute | solution.py:757
  286.8 6.6 %all-to-all-done.8 = bf16[32,24,896]{2,1,0:T(8,128)(2,1)S(1)} async-done(((bf16[32,24,896]{2,1,0:T(8,128)(2,1)}), bf16[32,24,896]{2,1,0:T(8,128)(2,1)S(1)}, u32[]{:S(2)}, u32[]{:S(2)}) %all-to-all-start.8) | async-done | bytes 1376288 | tf_op jit(solution)/shard_map/all_to_all | solution.py:763
  293.4 2.5 add_chunks.1
  295.9 4.2 %all-to-all-start.9 = ((bf16[32,32,896]{2,1,0:T(8,128)(2,1)}), bf16[32,32,896]{2,1,0:T(8,128)(2,1)S(1)}, u32[]{:S(2)}, u32[]{:S(2)}) async-start(bf16[32,32,896]{2,1,0:T(8,128)(2,1)} %bitcast.59), calls=%async_computation.9 | async-start | bytes 3670016 | tf_op jit(solution)/shard_map/all_to_all | solution.py:763
  301.7 4.7 %collective-permute-done.11.refs_4_ = bf16[128,768]{1,0:T(8,128)(2,1)S(1)} collective-permute-done((bf16[128,768]{1,0:T(8,128)(2,1)S(1)}, bf16[128,768]{1,0:T(8,128)(2,1)S(1)}, u32[]{:S(2)}, u32[]{:S(2)}) %collective-permute-start.11) | collective-permute-done | bytes 196640 | tf_op jit(solution)/shard_map/ppermute | solution.py:757
  307.9 5.2 %collective-permute-done.9.refs_2_ = bf16[128,768]{1,0:T(8,128)(2,1)S(1)} collective-permute-done((bf16[128,768]{1,0:T(8,128)(2,1)S(1)}, bf16[128,768]{1,0:T(8,128)(2,1)S(1)}, u32[]{:S(2)}, u32[]{:S(2)}) %collective-permute-start.9) | collective-permute-done | bytes 196640 | tf_op jit(solution)/shard_map/ppermute | solution.py:757
  313.9 11.8 %all-to-all-done.9 = bf16[32,32,896]{2,1,0:T(8,128)(2,1)S(1)} async-done(((bf16[32,32,896]{2,1,0:T(8,128)(2,1)}), bf16[32,32,896]{2,1,0:T(8,128)(2,1)S(1)}, u32[]{:S(2)}, u32[]{:S(2)}) %all-to-all-start.9) | async-done | bytes 1835040 | tf_op jit(solution)/shard_map/all_to_all | solution.py:763
  325.7 4.5 %place_grads.1 = (f32[2,3,192,768]{3,2,1,0:T(8,128)}, f32[2,192,768]{2,1,0:T(8,128)}, f32[2,32,768]{2,1,0:T(8,128)}, f32[2,2,768]{2,1,0:T(2,128)}, f32[2,32,3]{2,1,0:T(8,128)}) custom-call(bf16[768,896]{1,0:T(8,128)(2,1)} %bitcast.22.refs_0_, bf16[1024,896]{1,0:T(8,128)(2,1)S(1)} %bitcast.41), custom_call_target="tpu_custom_call" | custom-call | tf_op jit(solution)/shard_map/place_grads/pallas_call | solution.py:131
  (126 shorter events, 44.5 us)
Async XLA Ops:
  3.8 19.6 %copy-start.5 = (bf16[128,768]{1,0:T(8,128)(2,1)S(1)}, bf16[128,768]{1,0:T(8,128)(2,1)}, u32[]{:S(2)}) copy-start(bf16[128,768]{1,0:T(8,128)(2,1)} %refs_5_.7) | copy-start | bytes 589828
  3.8 19.6 %copy-start.11 = (bf16[2,768,32]{1,2,0:T(8,128)(2,1)S(1)}, bf16[2,768,32]{1,2,0:T(8,128)(2,1)}, u32[]{:S(2)}) copy-start(bf16[2,768,32]{1,2,0:T(8,128)(2,1)} %param.20) | copy-start | bytes 294916
  3.8 19.6 %copy-start.12 = (f32[2,2,768]{2,1,0:T(2,128)S(1)}, f32[2,2,768]{2,1,0:T(2,128)}, u32[]{:S(2)}) copy-start(f32[2,2,768]{2,1,0:T(2,128)} %refs_6_.3) | copy-start | bytes 36868
  3.8 41.1 %copy-start.2 = (bf16[2,1,768,768]{3,2,1,0:T(8,128)(2,1)S(1)}, bf16[2,1,768,768]{3,2,1,0:T(8,128)(2,1)}, u32[]{:S(2)}) copy-start(bf16[2,1,768,768]{3,2,1,0:T(8,128)(2,1)} %param.22) | copy-start | bytes 7077892
  7.2 37.7 %copy-start.1 = (bf16[2,1,768,768]{3,2,1,0:T(8,128)(2,1)S(1)}, bf16[2,1,768,768]{3,2,1,0:T(8,128)(2,1)}, u32[]{:S(2)}) copy-start(bf16[2,1,768,768]{3,2,1,0:T(8,128)(2,1)} %param.21) | copy-start | bytes 7077892
  7.2 11.3 %collective-permute-start.2 = (bf16[128,768]{1,0:T(8,128)(2,1)S(1)}, bf16[128,768]{1,0:T(8,128)(2,1)S(1)}, u32[]{:S(2)}, u32[]{:S(2)}) collective-permute-start(bf16[128,768]{1,0:T(8,128)(2,1)S(1)} %get-tuple-element.91.refs_1_), channel_id=1, source_target_pairs={{0,3},{1,0},{2,1},{3,2},{4,7},{5,4},{6,5},{7,6},{8,11},{9,8},{10,9... | collective-permute-start | bytes 589832 | tf_op jit(solution)/shard_map/ppermute | solution.py:757
  10.8 7.6 %collective-permute-start.1 = (bf16[128,768]{1,0:T(8,128)(2,1)S(1)}, bf16[128,768]{1,0:T(8,128)(2,1)S(1)}, u32[]{:S(2)}, u32[]{:S(2)}) collective-permute-start(bf16[128,768]{1,0:T(8,128)(2,1)S(1)} %get-tuple-element.91.refs_1_), channel_id=1, source_target_pairs={{0,2},{1,3},{2,0},{3,1},{4,6},{5,7},{6,4},{7,5},{8,10},{9,11},{10,... | collective-permute-start | bytes 589832 | tf_op jit(solution)/shard_map/ppermute | solution.py:757
  11.2 12.2 %collective-permute-start = (bf16[128,768]{1,0:T(8,128)(2,1)S(1)}, bf16[128,768]{1,0:T(8,128)(2,1)S(1)}, u32[]{:S(2)}, u32[]{:S(2)}) collective-permute-start(bf16[128,768]{1,0:T(8,128)(2,1)S(1)} %get-tuple-element.91.refs_1_), channel_id=1, source_target_pairs={{0,1},{1,2},{2,3},{3,0},{4,5},{5,6},{6,7},{7,4},{8,9},{9,10},{10,1... | collective-permute-start | bytes 589832 | tf_op jit(solution)/shard_map/ppermute | solution.py:757
  44.9 32.2 %copy-start.3 = (bf16[2,192,768]{2,1,0:T(8,128)(2,1)S(1)}, bf16[2,192,768]{2,1,0:T(8,128)(2,1)}, u32[]{:S(2)}) copy-start(bf16[2,192,768]{2,1,0:T(8,128)(2,1)} %refs_10_.3) | copy-start | bytes 1769476
  44.9 32.2 %copy-start.9 = (f32[128,768]{1,0:T(8,128)S(1)}, f32[128,768]{1,0:T(8,128)}, u32[]{:S(2)}) copy-start(f32[128,768]{1,0:T(8,128)} %get-tuple-element.94.refs_0_.refs_7_) | copy-start | bytes 1179652
  47.0 30.1 %copy-start = (bf16[2,3,768,192]{2,3,1,0:T(8,128)(2,1)S(1)}, bf16[2,3,768,192]{2,3,1,0:T(8,128)(2,1)}, u32[]{:S(2)}) copy-start(bf16[2,3,768,192]{2,3,1,0:T(8,128)(2,1)} %param.16) | copy-start | bytes 5308420
  64.1 6.8 %collective-permute-start.5 = (bf16[128,768]{1,0:T(8,128)(2,1)S(1)}, bf16[128,768]{1,0:T(8,128)(2,1)S(1)}, u32[]{:S(2)}, u32[]{:S(2)}) collective-permute-start(bf16[128,768]{1,0:T(8,128)(2,1)S(1)} %get-tuple-element.98.refs_1_), channel_id=1, source_target_pairs={{0,3},{1,0},{2,1},{3,2},{4,7},{5,4},{6,5},{7,6},{8,11},{9,8},{10,9... | collective-permute-start | bytes 589832 | tf_op jit(solution)/shard_map/ppermute | solution.py:757
  64.5 8.0 %collective-permute-start.4 = (bf16[128,768]{1,0:T(8,128)(2,1)S(1)}, bf16[128,768]{1,0:T(8,128)(2,1)S(1)}, u32[]{:S(2)}, u32[]{:S(2)}) collective-permute-start(bf16[128,768]{1,0:T(8,128)(2,1)S(1)} %get-tuple-element.98.refs_1_), channel_id=1, source_target_pairs={{0,2},{1,3},{2,0},{3,1},{4,6},{5,7},{6,4},{7,5},{8,10},{9,11},{10,... | collective-permute-start | bytes 589832 | tf_op jit(solution)/shard_map/ppermute | solution.py:757
  64.8 12.3 %collective-permute-start.3 = (bf16[128,768]{1,0:T(8,128)(2,1)S(1)}, bf16[128,768]{1,0:T(8,128)(2,1)S(1)}, u32[]{:S(2)}, u32[]{:S(2)}) collective-permute-start(bf16[128,768]{1,0:T(8,128)(2,1)S(1)} %get-tuple-element.98.refs_1_), channel_id=1, source_target_pairs={{0,1},{1,2},{2,3},{3,0},{4,5},{5,6},{6,7},{7,4},{8,9},{9,10},{10,1... | collective-permute-start | bytes 589832 | tf_op jit(solution)/shard_map/ppermute | solution.py:757
  77.1 15.1 %copy-start.4 = (bf16[128,768]{1,0:T(8,128)(2,1)S(1)}, bf16[128,768]{1,0:T(8,128)(2,1)}, u32[]{:S(2)}) copy-start(bf16[128,768]{1,0:T(8,128)(2,1)} %refs_9_.3) | copy-start | bytes 589828
  79.1 36.7 %copy-start.8 = (f32[128,768]{1,0:T(8,128)}, f32[128,768]{1,0:T(8,128)S(1)}, u32[]{:S(2)}) copy-start(f32[128,768]{1,0:T(8,128)S(1)} %get-tuple-element.99.refs_0_.refs_5_) | copy-start | bytes 1179652
  79.1 6.1 %collective-permute-start.8 = (bf16[128,768]{1,0:T(8,128)(2,1)S(1)}, bf16[128,768]{1,0:T(8,128)(2,1)S(1)}, u32[]{:S(2)}, u32[]{:S(2)}) collective-permute-start(bf16[128,768]{1,0:T(8,128)(2,1)S(1)} %get-tuple-element.100.refs_1_), channel_id=1, source_target_pairs={{0,3},{1,0},{2,1},{3,2},{4,7},{5,4},{6,5},{7,6},{8,11},{9,8},{10,9... | collective-permute-start | bytes 589832 | tf_op jit(solution)/shard_map/ppermute | solution.py:757
  79.6 7.0 %collective-permute-start.7 = (bf16[128,768]{1,0:T(8,128)(2,1)S(1)}, bf16[128,768]{1,0:T(8,128)(2,1)S(1)}, u32[]{:S(2)}, u32[]{:S(2)}) collective-permute-start(bf16[128,768]{1,0:T(8,128)(2,1)S(1)} %get-tuple-element.100.refs_1_), channel_id=1, source_target_pairs={{0,2},{1,3},{2,0},{3,1},{4,6},{5,7},{6,4},{7,5},{8,10},{9,11},{10,... | collective-permute-start | bytes 589832 | tf_op jit(solution)/shard_map/ppermute | solution.py:757
  79.6 12.5 %collective-permute-start.6 = (bf16[128,768]{1,0:T(8,128)(2,1)S(1)}, bf16[128,768]{1,0:T(8,128)(2,1)S(1)}, u32[]{:S(2)}, u32[]{:S(2)}) collective-permute-start(bf16[128,768]{1,0:T(8,128)(2,1)S(1)} %get-tuple-element.100.refs_1_), channel_id=1, source_target_pairs={{0,1},{1,2},{2,3},{3,0},{4,5},{5,6},{6,7},{7,4},{8,9},{9,10},{10,1... | collective-permute-start | bytes 589832 | tf_op jit(solution)/shard_map/ppermute | solution.py:757
  141.6 15.2 %copy-start.6 = (f32[128,768]{1,0:T(8,128)S(1)}, f32[128,768]{1,0:T(8,128)}, u32[]{:S(2)}) copy-start(f32[128,768]{1,0:T(8,128)} %get-tuple-element.101.refs_0_.refs_7_) | copy-start | bytes 1179652
  141.6 15.2 %copy-start.21 = (bf16[3,128,192]{2,1,0:T(8,128)(2,1)S(1)}, bf16[3,128,192]{2,1,0:T(8,128)(2,1)}, u32[]{:S(2)}) copy-start(bf16[3,128,192]{2,1,0:T(8,128)(2,1)} %get-tuple-element.108.refs_11_) | copy-start | bytes 442372
  141.7 15.2 %copy-start.22 = (f32[3,128,128]{2,1,0:T(8,128)S(1)}, f32[3,128,128]{2,1,0:T(8,128)}, u32[]{:S(2)}) copy-start(f32[3,128,128]{2,1,0:T(8,128)} %get-tuple-element.109.refs_12_) | copy-start | bytes 589828
  143.1 6.4 %collective-permute-start.14 = (bf16[136,768]{1,0:T(8,128)(2,1)S(1)}, bf16[136,768]{1,0:T(8,128)(2,1)S(1)}, u32[]{:S(2)}, u32[]{:S(2)}) collective-permute-start(bf16[136,768]{1,0:T(8,128)(2,1)S(1)} %get-tuple-element.107.refs_0_), channel_id=1, source_target_pairs={{0,3},{1,0},{2,1},{3,2},{4,7},{5,4},{6,5},{7,6},{8,11},{9,8},{10,9... | collective-permute-start | bytes 626696 | tf_op jit(solution)/shard_map/ppermute | solution.py:757
  143.7 7.6 %collective-permute-start.13 = (bf16[136,768]{1,0:T(8,128)(2,1)S(1)}, bf16[136,768]{1,0:T(8,128)(2,1)S(1)}, u32[]{:S(2)}, u32[]{:S(2)}) collective-permute-start(bf16[136,768]{1,0:T(8,128)(2,1)S(1)} %get-tuple-element.107.refs_0_), channel_id=1, source_target_pairs={{0,2},{1,3},{2,0},{3,1},{4,6},{5,7},{6,4},{7,5},{8,10},{9,11},{10,... | collective-permute-start | bytes 626696 | tf_op jit(solution)/shard_map/ppermute | solution.py:757
  143.7 13.1 %collective-permute-start.12 = (bf16[136,768]{1,0:T(8,128)(2,1)S(1)}, bf16[136,768]{1,0:T(8,128)(2,1)S(1)}, u32[]{:S(2)}, u32[]{:S(2)}) collective-permute-start(bf16[136,768]{1,0:T(8,128)(2,1)S(1)} %get-tuple-element.107.refs_0_), channel_id=1, source_target_pairs={{0,1},{1,2},{2,3},{3,0},{4,5},{5,6},{6,7},{7,4},{8,9},{9,10},{10,1... | collective-permute-start | bytes 626696 | tf_op jit(solution)/shard_map/ppermute | solution.py:757
  163.8 25.4 %all-to-all-start.4 = ((bf16[32,24,896]{2,1,0:T(8,128)(2,1)}), bf16[32,24,896]{2,1,0:T(8,128)(2,1)}, u32[]{:S(2)}, u32[]{:S(2)}) async-start(bf16[32,24,896]{2,1,0:T(8,128)(2,1)} %bitcast.61), calls=%async_computation.4 | async-start | bytes 2752512 | tf_op jit(solution)/shard_map/all_to_all | solution.py:763
  168.6 6.3 %collective-permute-start.17 = (bf16[128,768]{1,0:T(8,128)(2,1)S(1)}, bf16[128,768]{1,0:T(8,128)(2,1)S(1)}, u32[]{:S(2)}, u32[]{:S(2)}) collective-permute-start(bf16[128,768]{1,0:T(8,128)(2,1)S(1)} %get-tuple-element.124.refs_1_), channel_id=1, source_target_pairs={{0,3},{1,0},{2,1},{3,2},{4,7},{5,4},{6,5},{7,6},{8,11},{9,8},{10,9... | collective-permute-start | bytes 589832 | tf_op jit(solution)/shard_map/ppermute | solution.py:757
  169.0 7.4 %collective-permute-start.16 = (bf16[128,768]{1,0:T(8,128)(2,1)S(1)}, bf16[128,768]{1,0:T(8,128)(2,1)S(1)}, u32[]{:S(2)}, u32[]{:S(2)}) collective-permute-start(bf16[128,768]{1,0:T(8,128)(2,1)S(1)} %get-tuple-element.124.refs_1_), channel_id=1, source_target_pairs={{0,2},{1,3},{2,0},{3,1},{4,6},{5,7},{6,4},{7,5},{8,10},{9,11},{10,... | collective-permute-start | bytes 589832 | tf_op jit(solution)/shard_map/ppermute | solution.py:757
  169.0 12.6 %collective-permute-start.15 = (bf16[128,768]{1,0:T(8,128)(2,1)S(1)}, bf16[128,768]{1,0:T(8,128)(2,1)S(1)}, u32[]{:S(2)}, u32[]{:S(2)}) collective-permute-start(bf16[128,768]{1,0:T(8,128)(2,1)S(1)} %get-tuple-element.124.refs_1_), channel_id=1, source_target_pairs={{0,1},{1,2},{2,3},{3,0},{4,5},{5,6},{6,7},{7,4},{8,9},{9,10},{10,1... | collective-permute-start | bytes 589832 | tf_op jit(solution)/shard_map/ppermute | solution.py:757
  214.0 16.0 %all-to-all-start.6 = ((bf16[32,8,1152]{2,1,0:T(8,128)(2,1)}), bf16[32,8,1152]{2,1,0:T(8,128)(2,1)S(1)}, u32[]{:S(2)}, u32[]{:S(2)}) async-start(bf16[32,8,1152]{2,1,0:T(8,128)(2,1)} %bitcast.56), calls=%async_computation.6 | async-start | bytes 1179648 | tf_op jit(solution)/shard_map/all_to_all | solution.py:763
  231.1 24.7 %all-to-all-start.7 = ((bf16[32,24,896]{2,1,0:T(8,128)(2,1)}), bf16[32,24,896]{2,1,0:T(8,128)(2,1)}, u32[]{:S(2)}, u32[]{:S(2)}) async-start(bf16[32,24,896]{2,1,0:T(8,128)(2,1)} %bitcast.60), calls=%async_computation.7 | async-start | bytes 2752512 | tf_op jit(solution)/shard_map/all_to_all | solution.py:763
  235.6 7.2 %collective-permute-start.20 = (bf16[136,768]{1,0:T(8,128)(2,1)}, bf16[136,768]{1,0:T(8,128)(2,1)S(1)}, u32[]{:S(2)}, u32[]{:S(2)}) collective-permute-start(bf16[136,768]{1,0:T(8,128)(2,1)} %combine_back.1.refs_0_), channel_id=1, source_target_pairs={{0,3},{1,0},{2,1},{3,2},{4,7},{5,4},{6,5},{7,6},{8,11},{9,8},{10,9... | collective-permute-start | bytes 626696 | tf_op jit(solution)/shard_map/ppermute | solution.py:757
  236.0 8.4 %collective-permute-start.19 = (bf16[136,768]{1,0:T(8,128)(2,1)}, bf16[136,768]{1,0:T(8,128)(2,1)S(1)}, u32[]{:S(2)}, u32[]{:S(2)}) collective-permute-start(bf16[136,768]{1,0:T(8,128)(2,1)} %combine_back.1.refs_0_), channel_id=1, source_target_pairs={{0,2},{1,3},{2,0},{3,1},{4,6},{5,7},{6,4},{7,5},{8,10},{9,11},{10,... | collective-permute-start | bytes 626696 | tf_op jit(solution)/shard_map/ppermute | solution.py:757
  236.0 13.4 %collective-permute-start.18 = (bf16[136,768]{1,0:T(8,128)(2,1)}, bf16[136,768]{1,0:T(8,128)(2,1)S(1)}, u32[]{:S(2)}, u32[]{:S(2)}) collective-permute-start(bf16[136,768]{1,0:T(8,128)(2,1)} %combine_back.1.refs_0_), channel_id=1, source_target_pairs={{0,1},{1,2},{2,3},{3,0},{4,5},{5,6},{6,7},{7,4},{8,9},{9,10},{10,1... | collective-permute-start | bytes 626696 | tf_op jit(solution)/shard_map/ppermute | solution.py:757
  237.1 18.7 %copy-start.10 = (f32[128,768]{1,0:T(8,128)S(1)}, f32[128,768]{1,0:T(8,128)}, u32[]{:S(2)}) copy-start(f32[128,768]{1,0:T(8,128)} %get-tuple-element.94.refs_0_.refs_7_) | copy-start | bytes 1179652
  237.1 18.7 %copy-start.13 = (f32[2,2,768]{2,1,0:T(2,128)S(1)}, f32[2,2,768]{2,1,0:T(2,128)}, u32[]{:S(2)}) copy-start(f32[2,2,768]{2,1,0:T(2,128)} %refs_6_.3) | copy-start | bytes 36868
  264.2 4.3 %copy-start.31 = (bf16[128,768]{1,0:T(8,128)(2,1)}, bf16[128,768]{1,0:T(8,128)(2,1)S(1)}, u32[]{:S(2)}) copy-start(bf16[128,768]{1,0:T(8,128)(2,1)S(1)} %get-tuple-element.149.refs_1_) | copy-start | bytes 589828
  268.6 17.2 %copy-start.15 = (f32[128,768]{1,0:T(8,128)S(1)}, f32[128,768]{1,0:T(8,128)}, u32[]{:S(2)}) copy-start(f32[128,768]{1,0:T(8,128)} %get-tuple-element.148.refs_0_) | copy-start | bytes 1179652
  268.6 24.8 %all-to-all-start.8 = ((bf16[32,24,896]{2,1,0:T(8,128)(2,1)}), bf16[32,24,896]{2,1,0:T(8,128)(2,1)S(1)}, u32[]{:S(2)}, u32[]{:S(2)}) async-start(bf16[32,24,896]{2,1,0:T(8,128)(2,1)} %bitcast.62), calls=%async_computation.8 | async-start | bytes 2752512 | tf_op jit(solution)/shard_map/all_to_all | solution.py:763
  272.8 6.2 %collective-permute-start.23 = (bf16[128,768]{1,0:T(8,128)(2,1)S(1)}, bf16[128,768]{1,0:T(8,128)(2,1)S(1)}, u32[]{:S(2)}, u32[]{:S(2)}) collective-permute-start(bf16[128,768]{1,0:T(8,128)(2,1)S(1)} %copy-done.32), channel_id=1, source_target_pairs={{0,3},{1,0},{2,1},{3,2},{4,7},{5,4},{6,5},{7,6},{8,11},{9,8},{10,9... | collective-permute-start | bytes 589832 | tf_op jit(solution)/shard_map/ppermute | solution.py:757
  273.2 7.4 %collective-permute-start.22 = (bf16[128,768]{1,0:T(8,128)(2,1)S(1)}, bf16[128,768]{1,0:T(8,128)(2,1)S(1)}, u32[]{:S(2)}, u32[]{:S(2)}) collective-permute-start(bf16[128,768]{1,0:T(8,128)(2,1)S(1)} %copy-done.32), channel_id=1, source_target_pairs={{0,2},{1,3},{2,0},{3,1},{4,6},{5,7},{6,4},{7,5},{8,10},{9,11},{10,... | collective-permute-start | bytes 589832 | tf_op jit(solution)/shard_map/ppermute | solution.py:757
  273.2 12.5 %collective-permute-start.21 = (bf16[128,768]{1,0:T(8,128)(2,1)S(1)}, bf16[128,768]{1,0:T(8,128)(2,1)S(1)}, u32[]{:S(2)}, u32[]{:S(2)}) collective-permute-start(bf16[128,768]{1,0:T(8,128)(2,1)S(1)} %copy-done.32), channel_id=1, source_target_pairs={{0,1},{1,2},{2,3},{3,0},{4,5},{5,6},{6,7},{7,4},{8,9},{9,10},{10,1... | collective-permute-start | bytes 589832 | tf_op jit(solution)/shard_map/ppermute | solution.py:757
  295.9 4.3 %copy-start.30 = (bf16[128,768]{1,0:T(8,128)(2,1)S(1)}, bf16[128,768]{1,0:T(8,128)(2,1)}, u32[]{:S(2)}) copy-start(bf16[128,768]{1,0:T(8,128)(2,1)} %copy-done.29) | copy-start | bytes 589828
  295.9 17.2 %copy-start.7 = (f32[128,768]{1,0:T(8,128)S(1)}, f32[128,768]{1,0:T(8,128)}, u32[]{:S(2)}) copy-start(f32[128,768]{1,0:T(8,128)} %get-tuple-element.101.refs_0_.refs_7_) | copy-start | bytes 1179652
  295.9 29.8 %all-to-all-start.9 = ((bf16[32,32,896]{2,1,0:T(8,128)(2,1)}), bf16[32,32,896]{2,1,0:T(8,128)(2,1)S(1)}, u32[]{:S(2)}, u32[]{:S(2)}) async-start(bf16[32,32,896]{2,1,0:T(8,128)(2,1)} %bitcast.59), calls=%async_computation.9 | async-start | bytes 3670016 | tf_op jit(solution)/shard_map/all_to_all | solution.py:763
  300.1 6.2 %collective-permute-start.11 = (bf16[128,768]{1,0:T(8,128)(2,1)S(1)}, bf16[128,768]{1,0:T(8,128)(2,1)S(1)}, u32[]{:S(2)}, u32[]{:S(2)}) collective-permute-start(bf16[128,768]{1,0:T(8,128)(2,1)S(1)} %copy-done.30), channel_id=1, source_target_pairs={{0,3},{1,0},{2,1},{3,2},{4,7},{5,4},{6,5},{7,6},{8,11},{9,8},{10,9... | collective-permute-start | bytes 589832 | tf_op jit(solution)/shard_map/ppermute | solution.py:757
  300.5 7.4 %collective-permute-start.10 = (bf16[128,768]{1,0:T(8,128)(2,1)S(1)}, bf16[128,768]{1,0:T(8,128)(2,1)S(1)}, u32[]{:S(2)}, u32[]{:S(2)}) collective-permute-start(bf16[128,768]{1,0:T(8,128)(2,1)S(1)} %copy-done.30), channel_id=1, source_target_pairs={{0,2},{1,3},{2,0},{3,1},{4,6},{5,7},{6,4},{7,5},{8,10},{9,11},{10,... | collective-permute-start | bytes 589832 | tf_op jit(solution)/shard_map/ppermute | solution.py:757
  300.5 12.5 %collective-permute-start.9 = (bf16[128,768]{1,0:T(8,128)(2,1)S(1)}, bf16[128,768]{1,0:T(8,128)(2,1)S(1)}, u32[]{:S(2)}, u32[]{:S(2)}) collective-permute-start(bf16[128,768]{1,0:T(8,128)(2,1)S(1)} %copy-done.30), channel_id=1, source_target_pairs={{0,1},{1,2},{2,3},{3,0},{4,5},{5,6},{6,7},{7,4},{8,9},{9,10},{10,1... | collective-permute-start | bytes 589832 | tf_op jit(solution)/shard_map/ppermute | solution.py:757
  (24 other events, 38.2 us)

commit v3 on v2

--- a/solution.py
+++ b/solution.py
@@ -88,7 +88,7 @@
     return pltpu.with_memory_space_constraint(array, pltpu.HBM)
 
 
-def call(body, outs, *operands, limit=16):
+def call(body, outs, *operands, held=(), limit=16):
     late = [isinstance(o, Late) for o in operands]
     inner = [o.operand if isinstance(o, Late) else o for o in operands]
     arrays = [o.array if isinstance(o, Layer) else o for o in inner]
@@ -99,6 +99,7 @@
     scratch = [pltpu.VMEM(p, a.dtype) for p, a, is_late in zip(parts, arrays, late) if is_late]
     scratch += [pltpu.VMEM(*o) for o, is_kept in zip(shapes, kept) if is_kept]
     copies = len(scratch)
+    scratch += [pltpu.VMEM(*h) for h in held]
     if copies:
         scratch.append(pltpu.SemaphoreType.DMA((copies,)))
 
@@ -120,7 +121,7 @@
                 leaving.append(ref)
                 used += 1
             taken.append(ref)
-        body(*given, *taken)
+        body(*given, *taken, *spare[used:])
         go(*leaving)
         for ref in leaving:
             ref.copy.wait()
@@ -147,13 +148,13 @@
     return pl.pallas_call(
         body,
         grid=(1,),
-        out_shape=[jax.ShapeDtypeStruct(stacked, f32)] * 2,
-        in_specs=whole + [pl.BlockSpec(memory_space=pl.ANY)] * len(earlier),
+        out_shape=[pltpu.HBM(stacked, f32)] * 2,
+        in_specs=whole + [pl.BlockSpec(memory_space=pltpu.HBM)] * len(earlier),
         out_specs=[part] * 2,
         input_output_aliases={len(operands) + n: n for n in range(len(earlier))},
         compiler_params=pltpu.CompilerParams(vmem_limit_bytes=24 * 1024 * 1024),
         name=body.__name__,
-    )(*[in_hbm(o) for o in operands], *earlier)
+    )(*[in_hbm(o) for o in (*operands, *earlier)])
 
 
 def dot(left, right, left_axis=1, right_axis=0, precision=None):
@@ -207,12 +208,13 @@
     mirror = one_hot(iota((offsets, 256), 0) + iota((offsets, 256), 1) == offsets - 1)
     hot = dot(hot, mirror)
     hot_ref[...] = hot
+    tables = table_ref[...]
     segment = segment_ref[...].astype(f32)
     allowed = (column_of(segment, ROWS) == segment) & (iota((ROWS, ROWS), 1) <= iota((ROWS, ROWS), 0))
     lane = iota((ROWS, ROWS), 1)
     before = one_hot(lane < iota((ROWS, ROWS), 0))
     for layer in range(2):
-        by_offset = dot(table_ref[layer], hot, precision=highest)
+        by_offset = dot(tables[:, layer, :], hot, precision=highest)
         for head in range(HERE):
             line = jnp.broadcast_to(by_offset[head : head + 1, :], (ROWS, 256))
             placed = pltpu.roll(line, 129, axis=1, stride=1, stride_axis=0)[:, :ROWS]
@@ -339,6 +341,7 @@
 ):
     current = middle_ref[...] + four(z0[...], z1[...], z2[...], z3[...])
     current_ref[...] = current
+    go(current_ref)
     mixture = attend(current, gain_ref, qkv_ref, bias_ref, low_ref, triple_ref, weights_ref)
     mixture_ref[...] = mixture
     go(mixture_ref)
@@ -610,7 +613,7 @@
         diagonals = jnp.where(
             iota((8, 256), 0) == head, jnp.sum(turned, axis=0, keepdims=True), diagonals
         )
-    table_grad_ref[...] = dot(hot_ref[...], diagonals, 1, 1, precision=highest)
+    table_grad_ref[...] = dot(diagonals, hot_ref[...], 1, 1, precision=highest)
     grad_input = 0.0
     for k, grad in enumerate((grad_queries * HEAD**-0.5, grad_keys * HEAD**-0.5, grad_values)):
         grad = grad.astype(bf16)
@@ -620,19 +623,73 @@
     part_ref[...] = grad_input.astype(bf16)
 
 
-def weight_grads(low_ref, back_triple_ref, mixture_ref, after_ref, low_two_ref, logits_ref, grads_ref):
+SHARE = WIDTH // EXPERTS
+GROUPS = WIDTH // 128
+
+
+def router_places():
+    row, column = iota((WIDTH, GROUPS * EXPERTS), 0), iota((WIDTH, GROUPS * EXPERTS), 1)
+    return one_hot(row == (column & (EXPERTS - 1)) * SHARE + (column >> 5))
+
+
+def folded(line):
+    place = iota((8, 128), 0)
+    rows = jnp.zeros((8, 128), f32)
+    for part in range(GROUPS):
+        rows = jnp.where(place == part, line[:, part * 128 : (part + 1) * 128], rows)
+    return rows
+
+
+def unfolded(rows):
+    return jnp.concatenate([rows[part : part + 1, :] for part in range(GROUPS)], axis=1)
+
+
+def fill_grads(low, back_triple, mixture, after, low_two, logits, gains, table, grads_ref):
     kind = grads_ref.dtype
     qkv_rows = 3 * QUARTER
-    grads_ref[:qkv_rows, :WIDTH] = dot(back_triple_ref[...], low_ref[...], 0).astype(kind)
-    grads_ref[qkv_rows:, :WIDTH] = dot(mixture_ref[...], after_ref[...], 0).astype(kind)
-    both = dot(logits_ref[...], low_two_ref[...], 0)
+    grads_ref[:qkv_rows, :WIDTH] = dot(back_triple, low, 0).astype(kind)
+    grads_ref[qkv_rows:, :WIDTH] = dot(mixture, after, 0).astype(kind)
+    both = dot(logits, low_two, 0)
     total = both[:EXPERTS] + both[EXPERTS : 2 * EXPERTS]
-    for part in range(WIDTH // 128):
-        grads_ref[part * EXPERTS : (part + 1) * EXPERTS, WIDTH:] = total[
-            :, part * 128 : (part + 1) * 128
-        ].astype(kind)
-    used = WIDTH // 128 * EXPERTS
-    grads_ref[used:, WIDTH:] = jnp.zeros((WIDTH - used, 128), kind)
+    parts = jnp.concatenate([total[:, r * 128 : (r + 1) * 128] for r in range(GROUPS)], axis=0)
+    places = router_places()
+    high = parts.astype(bf16)
+    rest = (parts - high.astype(f32)).astype(bf16)
+    grads_ref[:, WIDTH:] = (dot(places, high) + dot(places, rest)).astype(kind)
+    for chunk, gain in enumerate(gains):
+        start = chunk * SHARE + 8
+        grads_ref[start : start + 8, WIDTH:] = folded(gain).astype(kind)
+    start = 2 * SHARE + 8
+    grads_ref[start : start + 8, WIDTH : WIDTH + EXPERTS] = table.astype(kind)
+
+
+def weight_grads(
+    low_ref, back_triple_ref, mixture_ref, after_ref, low_two_ref, logits_ref, gain, table, grads_ref
+):
+    operands = (low_ref, back_triple_ref, mixture_ref, after_ref, low_two_ref, logits_ref)
+    fill_grads(*[ref[...] for ref in operands], [gain[...]], table[...], grads_ref)
+
+
+def attention_back_low(*refs):
+    operands, (low_ref, mixture_ref, low_two_ref, gain10_ref) = refs[:15], refs[15:19]
+    after_ref, part_ref, grads_ref, held_low, held_triple, held_logits, held_gain, held_table = refs[19:]
+    attention_back(
+        *operands,
+        after_ref,
+        held_low,
+        held_triple,
+        part_ref,
+        held_logits,
+        held_gain,
+        held_table,
+    )
+    operands = (low_ref, held_triple, mixture_ref, held_low, low_two_ref, held_logits)
+    fill_grads(
+        *[ref[...] for ref in operands],
+        [held_gain[...], gain10_ref[...]],
+        held_table[...],
+        grads_ref,
+    )
 
 
 def start_back(
@@ -676,80 +733,138 @@
     output_ref[...] = (middle_ref[...] + four(z0[...], z1[...], z2[...], z3[...])).astype(bf16)
 
 
-SHARE = WIDTH // EXPERTS
-
-
-def total_of(chunks_ref):
+def add_chunks(chunks_ref, gain00_ref, spread_ref):
     total = chunks_ref[0:SHARE, :].astype(f32)
     for block in range(1, EXPERTS):
         total = total + chunks_ref[block * SHARE : (block + 1) * SHARE, :].astype(f32)
-    return total.astype(bf16)
-
-
-def add_chunks_top(chunks_ref, spread_ref):
-    total = total_of(chunks_ref)
+    total = total.astype(bf16)
+    gain = folded(gain00_ref[...]).astype(bf16)
     for block in range(EXPERTS):
-        spread_ref[block * SHARE : (block + 1) * SHARE, :] = total
-
-
-def add_chunks(chunks_ref, g00, g01, g10, g11, t0, t1, spread_ref):
-    total = total_of(chunks_ref)
-    row = iota((8, WIDTH), 0)
-    gains = jnp.zeros((8, WIDTH), f32)
-    for place, gain in enumerate((g00, g01, g10, g11)):
-        gains = jnp.where(row == place, gain[...], gains)
-    spread = 0.0
-    for layer, table in enumerate((t0, t1)):
-        lifted = table[...].astype(bf16)
-        rows = iota((8, EXPERTS), 0)
-        for turn in range(4):
-            chosen = one_hot(iota((8, EXPERTS), 1) == rows * 4 + turn)
-            start = turn * 32 + layer * 8
-            onto = one_hot(iota((8, 128), 1) == iota((8, 128), 0) + start)
-            spread = spread + dot(dot(chosen, lifted).astype(bf16), onto)
-    small = jnp.concatenate([gains, spread], axis=1).astype(bf16)
-    for block in range(EXPERTS):
-        spread_ref[block * 32 : block * 32 + SHARE, :] = total
-        spread_ref[block * 32 + SHARE : block * 32 + 32, :] = small
-
-
-def place_top(top_ref, qkv_ref, out_ref, router_ref):
-    for k in range(3):
-        qkv_ref[1, k] = top_ref[k * QUARTER : (k + 1) * QUARTER, :WIDTH].astype(f32)
-    out_ref[1] = top_ref[3 * QUARTER :, :WIDTH].astype(f32)
-    for part in range(WIDTH // 128):
-        router_ref[1, :, part * 128 : (part + 1) * 128] = top_ref[
-            part * EXPERTS : (part + 1) * EXPERTS, WIDTH:
-        ].astype(f32)
-
-
-def place_grads(top_ref, all_ref, qkv_ref, out_ref, router_ref, gains_ref, tables_ref):
-    small = jnp.zeros((8, SUMMED), f32)
-    place_top(top_ref, qkv_ref, out_ref, router_ref)
-    for block in range(EXPERTS):
-        chunk = all_ref[block * 32 : block * 32 + SHARE, :].astype(f32)
-        small = small + all_ref[block * 32 + SHARE : block * 32 + 32, :].astype(f32)
-        which, first = divmod(block * SHARE, QUARTER)
-        if which < 3:
-            qkv_ref[0, which, first : first + SHARE, :] = chunk[:, :WIDTH]
-        else:
-            out_ref[0, first : first + SHARE, :] = chunk[:, :WIDTH]
-        for row in range(0, SHARE, 8):
-            part, inside = divmod(block * SHARE + row, EXPERTS)
-            if part < WIDTH // 128:
-                router_ref[0, inside : inside + 8, part * 128 : (part + 1) * 128] = chunk[
-                    row : row + 8, WIDTH:
-                ]
-    for layer in range(2):
-        gains_ref[layer] = small[2 * layer : 2 * layer + 2, :WIDTH]
-        lanes = small[:, WIDTH:]
-        table = 0.0
-        for turn in range(4):
-            rows = one_hot(iota((EXPERTS, 8), 0) == iota((EXPERTS, 8), 1) * 4 + turn)
-            spread = dot(rows.astype(f32), lanes, precision=highest)
-            from_lane = (iota((128, 8), 0) == iota((128, 8), 1) + turn * 32 + layer * 8).astype(f32)
-            table = table + dot(spread, from_lane, precision=highest)
-        tables_ref[layer] = table[:, :HERE]
+        start = block * SHARE
+        spread_ref[start : start + SHARE, :] = total
+        spread_ref[start + 16 : start + SHARE, WIDTH:] = gain
+
+
+def router_rows(small):
+    places = router_places()
+    high = small.astype(bf16)
+    parts = dot(places, high, 0) + dot(places, (small - high.astype(f32)).astype(bf16), 0)
+    return jnp.concatenate(
+        [parts[r * EXPERTS : (r + 1) * EXPERTS] for r in range(GROUPS)], axis=1
+    )
+
+
+def place_top(
+    grads_ref, qkv_ref, out_ref, router_ref, gain_ref, table_ref, wide, small, rows, done
+):
+    fetch = pltpu.make_async_copy(grads_ref.at[:, WIDTH:], small, done.at[0])
+    fetch.start()
+    arriving, leaving = [], []
+    for k in range(4):
+        source = grads_ref.at[k * QUARTER : (k + 1) * QUARTER, :WIDTH]
+        target = qkv_ref.at[1, k] if k < 3 else out_ref.at[1]
+        arriving.append(pltpu.make_async_copy(source, wide.at[k], done.at[1 + k]))
+        leaving.append(pltpu.make_async_copy(wide.at[k], target, done.at[5 + k]))
+        arriving[-1].start()
+    fetch.wait()
+    lanes = small[...]
+    rows[...] = router_rows(lanes)
+    leaving.append(pltpu.make_async_copy(rows, router_ref.at[1], done.at[9]))
+    leaving[-1].start()
+    gain_ref[...] = unfolded(lanes[8:16])
+    table_ref[...] = lanes[2 * SHARE + 8 : 2 * SHARE + 16]
+    for k in range(4):
+        arriving[k].wait()
+        leaving[k].start()
+    for copy in leaving:
+        copy.wait()
+
+
+def place_low(
+    grads_ref,
+    gain_ref,
+    table_ref,
+    _,
+    __,
+    ___,
+    qkv_ref,
+    out_ref,
+    router_ref,
+    gains_ref,
+    tables_ref,
+    wide,
+    rows,
+    done,
+):
+    copies = []
+    for k in range(4):
+        wide[k] = grads_ref[k * QUARTER : (k + 1) * QUARTER, :WIDTH].astype(f32)
+        target = qkv_ref.at[0, k] if k < 3 else out_ref.at[0]
+        copies.append(pltpu.make_async_copy(wide.at[k], target, done.at[k]))
+        copies[-1].start()
+    small = grads_ref[:, WIDTH:].astype(f32)
+    rows[...] = router_rows(small)
+    copies.append(pltpu.make_async_copy(rows, router_ref.at[0], done.at[4]))
+    copies[-1].start()
+    first = small[16:SHARE]
+    for block in range(1, EXPERTS):
+        first = first + small[block * SHARE + 16 : (block + 1) * SHARE]
+    gains_ref[0, 0:1, :] = unfolded(first)
+    gains_ref[0, 1:2, :] = unfolded(small[8:16])
+    gains_ref[1, 0:1, :] = unfolded(small[SHARE + 8 : SHARE + 16])
+    gains_ref[1, 1:2, :] = gain_ref[...]
+    table = small[2 * SHARE + 8 : 2 * SHARE + 16]
+    for head in range(HERE):
+        tables_ref[head, 0:1, :] = table[head : head + 1, :EXPERTS]
+        tables_ref[head, 1:2, :] = table_ref[head : head + 1, :EXPERTS]
+    for copy in copies:
+        copy.wait()
+
+
+def place(top_grads, low_grads):
+    stacks = [
+        pltpu.HBM((2, 3, QUARTER, WIDTH), f32),
+        pltpu.HBM((2, QUARTER, WIDTH), f32),
+        pltpu.HBM((2, EXPERTS, WIDTH), f32),
+    ]
+    hbm, vmem = pl.BlockSpec(memory_space=pltpu.HBM), pl.BlockSpec(memory_space=pltpu.VMEM)
+    params = pltpu.CompilerParams(vmem_limit_bytes=16 * 1024 * 1024)
+    *stacked, gain, table = pl.pallas_call(
+        place_top,
+        out_shape=[
+            *stacks,
+            jax.ShapeDtypeStruct((1, WIDTH), f32),
+            jax.ShapeDtypeStruct((8, 128), f32),
+        ],
+        in_specs=[hbm],
+        out_specs=[hbm] * 3 + [vmem] * 2,
+        scratch_shapes=[
+            pltpu.VMEM((4, QUARTER, WIDTH), f32),
+            pltpu.VMEM((WIDTH, 128), f32),
+            pltpu.VMEM((EXPERTS, WIDTH), f32),
+            pltpu.SemaphoreType.DMA((10,)),
+        ],
+        compiler_params=params,
+        name="place_top",
+    )(in_hbm(top_grads))
+    return pl.pallas_call(
+        place_low,
+        out_shape=[
+            *stacks,
+            jax.ShapeDtypeStruct((2, 2, WIDTH), f32),
+            jax.ShapeDtypeStruct((HERE, 2, EXPERTS), f32),
+        ],
+        in_specs=[vmem] * 3 + [hbm] * 3,
+        out_specs=[hbm] * 3 + [vmem] * 2,
+        scratch_shapes=[
+            pltpu.VMEM((4, QUARTER, WIDTH), f32),
+            pltpu.VMEM((EXPERTS, WIDTH), f32),
+            pltpu.SemaphoreType.DMA((5,)),
+        ],
+        input_output_aliases={3: 0, 4: 1, 5: 2},
+        compiler_params=params,
+        name="place_low",
+    )(low_grads, gain, table, *[in_hbm(s) for s in stacked])
 
 
 def around(values):
@@ -795,7 +910,7 @@
             ((EXPERTS, 256), f32),
         ],
         Late(bucket_ids.reshape(1, -1)),
-        Late(bias_table.transpose(0, 2, 1)),
+        Late(bias_table.transpose(2, 0, 1)),
         Late(segment_ids),
         Late(expert_routes.transpose(0, 2, 1)),
     )
@@ -822,7 +937,7 @@
         tokens,
         *around(part),
         Layer(gains, 0),
-        Layer(router, 0),
+        Late(Layer(router, 0)),
         Layer(across, 0),
         Layer(down, 0),
     )
@@ -843,21 +958,21 @@
 
     current1, low_a1, triple1, weights1, mixture1, part = call(
         attention_next,
-        [(row, f32), *kept],
-        middle0,
+        [Kept(row, f32), *kept],
+        Late(middle0),
         *around(part),
         Layer(gains, 1),
-        Layer(qkv, 1),
-        Layer(bias, 1),
-        Layer(proj_out, 1),
+        Late(Layer(qkv, 1)),
+        Late(Layer(bias, 1)),
+        Late(Layer(proj_out, 1)),
     )
     middle1, low_b1, gates1, send = call(
         route_next,
         [Kept(row, f32), Kept(row, bf16), ((ROWS, ROWS), f32), ((MAIN, 2 * SENT), bf16)],
-        current1,
+        Late(current1),
         *around(part),
         Layer(gains, 1),
-        Layer(router, 1),
+        Late(Layer(router, 1)),
         Layer(across, 1),
         Layer(down, 1),
         cotangent,
@@ -889,7 +1004,7 @@
         (row, bf16),
         Kept((ROWS, 128), bf16),
         Kept((1, WIDTH), f32),
-        Kept((EXPERTS, 8), f32),
+        Kept((8, EXPERTS), f32),
     ]
     after1, low_after1, back_triple1, part, logits1, gain11, table1 = call(
         attention_back,
@@ -897,125 +1012,125 @@
         *around(back),
         gates1,
         Layer(across, 1),
-        Layer(router, 1),
+        Late(Layer(router, 1)),
         middle1,
         Layer(gains, 1),
         cotangent,
-        Layer(proj_out, 1),
+        Late(Layer(proj_out, 1)),
         triple1,
         weights1,
-        Layer(qkv, 1),
+        Late(Layer(qkv, 1)),
         hot,
     )
     parts = around(part)
     (top_grads,) = call(
         weight_grads,
-        [Kept((WIDTH, SUMMED), bf16)],
-        low_a1,
-        back_triple1,
-        mixture1,
-        low_after1,
-        low_b1,
-        logits1,
-    )
-    top_grads = across_experts(top_grads)
-    top_grads, parts, in_grads = lax.optimization_barrier((top_grads, parts, in_grads))
-    (top_grads,) = call(add_chunks_top, [Kept((WIDTH, SUMMED), bf16)], top_grads)
-
-    gradient0, gain10, rows0b, send = call(
-        start_back,
-        [Kept(row, f32), Kept((1, WIDTH), f32), ((8, ROWS), bf16), ((MAIN, SENT), bf16)],
-        Late(after1),
-        *parts,
-        Late(current1),
-        Late(Layer(gains, 1)),
-        gates0,
-        Layer(down, 0),
-        Late(picked0),
-    )
-    grads0, down0, send = call(
-        expert_backward,
-        [Kept(slots, bf16), Kept(slots, bf16), ((MAIN, SENT), bf16)],
-        across_experts(send),
-        Late(before0),
-        Late(Layer(expert_in, 0)),
-        Late(Layer(expert_out, 0)),
-    )
-    got = across_experts(send)
-    in_grads, out_grads = call_stacked(
-        expert_grads_low, 0, (rows0, active0, grads0, down0), stacked, (in_grads, out_grads)
-    )
-    (back,) = call(combine_back, [((LONG, WIDTH), bf16)], got, Layer(across, 0), rows0b)
-    backs = around(back)
-    top_grads, back = lax.optimization_barrier((top_grads, back))
-    top_grads = across_experts(top_grads)
-    top_grads, backs, in_grads = lax.optimization_barrier((top_grads, backs, in_grads))
+        [Kept((WIDTH, SUMMED), f32)],
+        Late(low_a1),
+        Late(back_triple1),
+        Late(mixture1),
+        Late(low_after1),
+        Late(low_b1),
+        Late(logits1),
+        Late(gain11),
+        Late(table1),
+    )
+    top_grads = lax.psum(top_grads, "expert")
+    parts, in_grads = lax.optimization_barrier((parts, in_grads))
+
+    def low_layer(_, carried):
+        in_grads, out_grads, after, _ = carried
+        gradient0, gain10, rows0b, send = call(
+            start_back,
+            [Kept(row, f32), Kept((1, WIDTH), f32), ((8, ROWS), bf16), ((MAIN, SENT), bf16)],
+            Late(after),
+            *parts,
+            Late(current1),
+            Late(Layer(gains, 1)),
+            gates0,
+            Layer(down, 0),
+            Late(picked0),
+        )
+        grads0, down0, send = call(
+            expert_backward,
+            [Kept(slots, bf16), Kept(slots, bf16), ((MAIN, SENT), bf16)],
+            across_experts(send),
+            Late(before0),
+            Late(Layer(expert_in, 0)),
+            Late(Layer(expert_out, 0)),
+        )
+        got = across_experts(send)
+        in_grads, out_grads = call_stacked(
+            expert_grads_low, 0, (rows0, active0, grads0, down0), stacked, (in_grads, out_grads)
+        )
+        (back,) = call(combine_back, [((LONG, WIDTH), bf16)], got, Layer(across, 0), rows0b)
+        backs = around(back)
+        backs, in_grads = lax.optimization_barrier((backs, in_grads))
+        after0, part, grads = call(
+            attention_back_low,
+            [Kept(row, f32), (row, bf16), Kept((WIDTH, SUMMED), bf16)],
+            *backs,
+            gates0,
+            Layer(across, 0),
+            Layer(router, 0),
+            Late(middle0),
+            Layer(gains, 0),
+            Late(gradient0),
+            Layer(proj_out, 0),
+            Late(triple0),
+            Late(weights0),
+            Layer(qkv, 0),
+            Late(hot),
+            Late(low_a0),
+            Late(mixture0),
+            Late(low_b0),
+            Late(gain10),
+            held=[
+                (row, bf16),
+                ((ROWS, 3 * QUARTER), bf16),
+                ((ROWS, 128), bf16),
+                ((1, WIDTH), f32),
+                ((8, EXPERTS), f32),
+            ],
+        )
+        low_parts = around(part)
+        tokens_grad, gain00 = call(
+            finish_back,
+            [Kept(row, f32), Kept((1, WIDTH), f32)],
+            after0,
+            *low_parts,
+            tokens,
+            Layer(gains, 0),
+        )
+        (spread,) = call(
+            add_chunks,
+            [Kept((WIDTH, SUMMED), bf16)],
+            across_experts(grads),
+            Late(gain00),
+        )
+        return in_grads, out_grads, tokens_grad, spread
+
+    once = jnp.minimum(jnp.maximum(bucket_ids[0], 0) + 1, 1)
+    in_grads, out_grads, tokens_grad, spread = lax.fori_loop(
+        0,
+        once,
+        low_layer,
+        (
+            in_grads,
+            out_grads,
+            after1,
+            jnp.zeros((WIDTH, SUMMED), bf16),
+        ),
+    )
+    low_grads = across_experts(spread)
     (output,) = call(finish_output, [Kept(row, bf16)], middle1, *around(moved))
-    after0, low_after0, back_triple0, part, logits0, gain01, table0 = call(
-        attention_back,
-        back_kept,
-        *backs,
-        gates0,
-        Layer(across, 0),
-        Layer(router, 0),
-        middle0,
-        Layer(gains, 0),
-        gradient0,
-        Layer(proj_out, 0),
-        triple0,
-        weights0,
-        Layer(qkv, 0),
-        hot,
-    )
-    (grads,) = call(
-        weight_grads,
-        [Kept((WIDTH, SUMMED), bf16)],
-        low_a0,
-        back_triple0,
-        mixture0,
-        low_after0,
-        low_b0,
-        logits0,
-    )
-    parts = around(part)
-    tokens_grad, gain00 = call(
-        finish_back,
-        [Kept(row, f32), Kept((1, WIDTH), f32)],
-        after0,
-        *parts,
-        tokens,
-        Layer(gains, 0),
-    )
-    (spread,) = call(
-        add_chunks,
-        [Kept((EXPERTS * 32, SUMMED), bf16)],
-        across_experts(grads),
-        Late(gain00),
-        Late(gain01),
-        Late(gain10),
-        Late(gain11),
-        Late(table0),
-        Late(table1),
-    )
-    qkv_grad, out_grad, router_grad, gain_grads, table_grad = call(
-        place_grads,
-        [
-            Kept((2, 3, QUARTER, WIDTH), f32),
-            Kept((2, QUARTER, WIDTH), f32),
-            Kept((2, EXPERTS, WIDTH), f32),
-            Kept((2, 2, WIDTH), f32),
-            Kept((2, EXPERTS, HERE), f32),
-        ],
-        Late(top_grads),
-        across_experts(spread),
-        limit=24,
-    )
+    qkv_grad, out_grad, router_grad, gain_grads, table_grad = place(top_grads, low_grads)
     return (
         output,
         tokens_grad,
         qkv_grad.transpose(0, 1, 3, 2),
         out_grad,
-        table_grad,
+        table_grad.transpose(1, 2, 0),
         gain_grads,
         router_grad.transpose(0, 2, 1),
         in_grads,

time: 333 us -> 313 us (0.940)
  waiting for transfers between devices: 124 us -> 68.7 us
  blocking collectives: 97.3 us -> 118 us
  local copies, waits for them, and re-layouts: 17.2 us -> 1.82 us
  between operations: 1.14 us -> 15 us
  Pallas kernels: 55.6 us -> 63.3 us
  starting transfers between devices: 36.8 us -> 43.8 us
    all_to_all x5 -> x2, waiting for transfers between devices: 40.7 us -> 7.82 us  [across_experts(): return lax.all_to_all(values, 'expert', 0, 0, tiled=True)]
    ppermute x24, waiting for transfers between devices: 82.9 us -> 54.4 us  [around(): lax.ppermute(values, 'tensor', [(i, (i + shift) % 4) for i in range(4)])]
    all_to_all x5 -> x6, blocking collectives: 97.3 us -> 118 us  [across_experts(): return lax.all_to_all(values, 'expert', 0, 0, tiled=True)]
    ppermute x24, starting transfers between devices: 15.4 us -> 34.7 us  [around(): lax.ppermute(values, 'tensor', [(i, (i + shift) % 4) for i in range(4)])]
    unnamed x88 -> x20, local copies, waits for them, and re-layouts: 17.2 us -> 0.06 us
    all_to_all x5 -> x2, starting transfers between devices: 21.4 us -> 9.02 us  [across_experts(): return lax.all_to_all(values, 'expert', 0, 0, tiled=True)]
    psum x0 -> x1, waiting for transfers between devices: none -> 6.43 us  [shards(): top_grads = lax.psum(top_grads, 'expert')]
    pallas_call x2 -> x4, Pallas kernels: 9.62 us -> 14.9 us  [the longest x2 9.59 us: call_stacked(): pl.pallas_call(body, grid=(1,), out_shape=[pltpu.HBM(stacked, f32)] * 2,...]
  transfers between devices with their start and end apart: 29 -> 27, of which waited for: 27 -> 16; matrix products, arithmetic and copies ran while one was open for 0% -> 1% of each run, Pallas kernels for 4% -> 11%
where the time goes in v3:
time: 313 us; the launch traced here: 311 us
  blocking collectives  118 us (38%)
  waiting for transfers between devices  68.7 us (22%)
  Pallas kernels  63.3 us (20%)
  starting transfers between devices  43.8 us (14%)
  between operations  15 us (5%)
    all_to_all x6, blocking collectives, across_experts(): return lax.all_to_all(values, 'expert', 0, 0, tiled=True)  118 us
    ppermute x24, waiting for transfers between devices, around(): lax.ppermute(values, 'tensor', [(i, (i + shift) % 4) for i in range(4)])  54.4 us
    pallas_call x18, Pallas kernels, call(): pl.pallas_call(kernel, out_shape=[pltpu.HBM(*o) if is_kept else jax.Shape...  48.4 us
    ppermute x24, starting transfers between devices, around(): lax.ppermute(values, 'tensor', [(i, (i + shift) % 4) for i in range(4)])  34.7 us
    pallas_call x2, Pallas kernels, call_stacked(): pl.pallas_call(body, grid=(1,), out_shape=[pltpu.HBM(stacked, f32)] * 2,...  9.59 us
    all_to_all x2, starting transfers between devices, across_experts(): return lax.all_to_all(values, 'expert', 0, 0, tiled=True)  9.02 us
    all_to_all x2, waiting for transfers between devices, across_experts(): return lax.all_to_all(values, 'expert', 0, 0, tiled=True)  7.82 us
    psum x1, waiting for transfers between devices, shards(): top_grads = lax.psum(top_grads, 'expert')  6.43 us
  transfers between devices with their start and end apart: 27, of which 16 were waited for; matrix products, arithmetic and copies ran while one was open for 1% of the time, Pallas kernels for 11%

profile of v3, /device:TPU:1, one launch (start us, length us, event | category | flops | bytes accessed | tf_op | source)
XLA Modules:
  0.0 311.1 jit_solution(12567177265399276827)
XLA Ops:
  9.4 3.4 %attention_first.1 = (bf16[128,768]{1,0:T(8,128)(2,1)}, bf16[3,128,192]{2,1,0:T(8,128)(2,1)}, f32[3,128,128]{2,1,0:T(8,128)}, bf16[128,192]{1,0:T(8,128)(2,1)}, bf16[128,768]{1,0:T(8,128)(2,1)S(1)}) custom-call(bf16[128,768]{1,0:T(8,128)(2,1)} %refs_0_.3, f32[2,2,768]{2,1,0:T(2,128)} %refs_8_.3, bf16[2,3,192,768]{3,2,1,0:T(8,128)(2,1)} %bitcast.6.refs_2_.refs_6_.refs_13_, ...), custom_call_target="tpu_custom_call" | custom-call | tf_op jit(solution)/shard_map/attention_first/pallas_call | solution.py:132
  12.7 2.2 collective-permute-start.6
  14.9 2.6 collective-permute-start.7
  18.6 2.2 collective-permute-done.6.refs_2_
  20.9 5.2 %collective-permute-done.7.refs_3_ = bf16[128,768]{1,0:T(8,128)(2,1)S(1)} collective-permute-done((bf16[128,768]{1,0:T(8,128)(2,1)S(1)}, bf16[128,768]{1,0:T(8,128)(2,1)S(1)}, u32[]{:S(2)}, u32[]{:S(2)}) %collective-permute-start.7) | collective-permute-done | bytes 196640 | tf_op jit(solution)/shard_map/ppermute | solution.py:872
  28.1 21.5 %all_to_all.85 = bf16[32,8,1152]{2,1,0:T(8,128)(2,1)S(1)} all-to-all(bf16[32,8,1152]{2,1,0:T(8,128)(2,1)S(1)} %bitcast.51), channel_id=1, replica_groups=mesh['expert'=32,'tensor'=4] {'expert'}, dimensions={0} | all-to-all | bytes 1179648 | tf_op jit(solution)/shard_map/all_to_all | solution.py:878
  49.7 2.1 expert_forward.1
  51.8 15.8 %all_to_all.86 = bf16[32,8,1152]{2,1,0:T(8,128)(2,1)S(1)} all-to-all(bf16[32,8,1152]{2,1,0:T(8,128)(2,1)S(1)} %bitcast.52), channel_id=1, replica_groups=mesh['expert'=32,'tensor'=4] {'expert'}, dimensions={0} | all-to-all | bytes 1179648 | tf_op jit(solution)/shard_map/all_to_all | solution.py:878
  67.5 2.1 combine_first.1
  70.7 2.1 collective-permute-start.10
  74.1 3.5 %collective-permute-done.9.refs_2_ = bf16[128,768]{1,0:T(8,128)(2,1)S(1)} collective-permute-done((bf16[128,768]{1,0:T(8,128)(2,1)S(1)}, bf16[128,768]{1,0:T(8,128)(2,1)S(1)}, u32[]{:S(2)}, u32[]{:S(2)}) %collective-permute-start.9) | collective-permute-done | bytes 196640 | tf_op jit(solution)/shard_map/ppermute | solution.py:872
  77.6 4.6 %collective-permute-done.10.refs_3_ = bf16[128,768]{1,0:T(8,128)(2,1)S(1)} collective-permute-done((bf16[128,768]{1,0:T(8,128)(2,1)S(1)}, bf16[128,768]{1,0:T(8,128)(2,1)S(1)}, u32[]{:S(2)}, u32[]{:S(2)}) %collective-permute-start.10) | collective-permute-done | bytes 196640 | tf_op jit(solution)/shard_map/ppermute | solution.py:872
  82.2 3.4 %attention_next.1 = (f32[128,768]{1,0:T(8,128)}, bf16[128,768]{1,0:T(8,128)(2,1)}, bf16[3,128,192]{2,1,0:T(8,128)(2,1)}, f32[3,128,128]{2,1,0:T(8,128)}, bf16[12...) custom-call(f32[128,768]{1,0:T(8,128)} %get-tuple-element.633.refs_0_, bf16[128,768]{1,0:T(8,128)(2,1)S(1)} %get-tuple-element.261.refs_1_, ...), custom_call_target="tpu_custom_call" | custom-call | tf_op jit(solution)/shard_map/attention_next/pallas_call | solution.py:132
  87.2 2.3 collective-permute-start.13
  90.1 2.5 collective-permute-done.12.refs_2_
  92.6 5.8 %collective-permute-done.13.refs_3_ = bf16[128,768]{1,0:T(8,128)(2,1)S(1)} collective-permute-done((bf16[128,768]{1,0:T(8,128)(2,1)S(1)}, bf16[128,768]{1,0:T(8,128)(2,1)S(1)}, u32[]{:S(2)}, u32[]{:S(2)}) %collective-permute-start.13) | collective-permute-done | bytes 196640 | tf_op jit(solution)/shard_map/ppermute | solution.py:872
  98.3 2.2 route_next.1
  100.5 23.4 %all_to_all.87 = bf16[32,8,2304]{2,1,0:T(8,128)(2,1)S(1)} all-to-all(bf16[32,8,2304]{2,1,0:T(8,128)(2,1)S(1)} %bitcast.49), channel_id=1, replica_groups=mesh['expert'=32,'tensor'=4] {'expert'}, dimensions={0} | all-to-all | bytes 2359296 | tf_op jit(solution)/shard_map/all_to_all | solution.py:878
  123.9 3.3 %expert_both.1 = (bf16[384,768]{1,0:T(8,128)(2,1)}, bf16[384,768]{1,0:T(8,128)(2,1)}, bf16[384,768]{1,0:T(8,128)(2,1)}, bf16[384,768]{1,0:T(8,128)(2,1)}, bf16[256,2304]{1,0:T(8,128)(2,1)S(1)}) custom-call(bf16[256,2304]{1,0:T(8,128)(2,1)S(1)} %bitcast.46, bf16[2,768,768]{2,1,0:T(8,128)(2,1)S(1)} %bitcast.55, bf16[2,768,768]{2,1,0:T(8,128)(2,1)S(1)} %bitcast.58), custom_call_target="tpu_custom_call" | custom-call | tf_op jit(solution)/shard_map/expert_both/pallas_call | solution.py:132
  127.3 22.6 %all_to_all.88 = bf16[32,8,2304]{2,1,0:T(8,128)(2,1)S(1)} all-to-all(bf16[32,8,2304]{2,1,0:T(8,128)(2,1)S(1)} %bitcast.50), channel_id=1, replica_groups=mesh['expert'=32,'tensor'=4] {'expert'}, dimensions={0} | all-to-all | bytes 2359296 | tf_op jit(solution)/shard_map/all_to_all | solution.py:878
  151.6 2.3 collective-permute-start.19
  154.3 4.0 %collective-permute-done.18.refs_1_ = bf16[136,768]{1,0:T(8,128)(2,1)S(1)} collective-permute-done((bf16[136,768]{1,0:T(8,128)(2,1)S(1)}, bf16[136,768]{1,0:T(8,128)(2,1)S(1)}, u32[]{:S(2)}, u32[]{:S(2)}) %collective-permute-start.18) | collective-permute-done | bytes 208928 | tf_op jit(solution)/shard_map/ppermute | solution.py:872
  158.3 4.9 %collective-permute-done.19.refs_2_ = bf16[136,768]{1,0:T(8,128)(2,1)S(1)} collective-permute-done((bf16[136,768]{1,0:T(8,128)(2,1)S(1)}, bf16[136,768]{1,0:T(8,128)(2,1)S(1)}, u32[]{:S(2)}, u32[]{:S(2)}) %collective-permute-start.19) | collective-permute-done | bytes 208928 | tf_op jit(solution)/shard_map/ppermute | solution.py:872
  163.2 4.5 %attention_back.1 = (f32[128,768]{1,0:T(8,128)}, bf16[128,768]{1,0:T(8,128)(2,1)}, bf16[128,576]{1,0:T(8,128)(2,1)}, bf16[128,768]{1,0:T(8,128)(2,1)S(1)}, bf16[...) custom-call(bf16[136,768]{1,0:T(8,128)(2,1)S(1)} %get-tuple-element.269.refs_0_, ...), custom_call_target="tpu_custom_call" | custom-call | tf_op jit(solution)/shard_map/attention_back/pallas_call | solution.py:132
  169.6 2.7 collective-permute-start.22
  172.3 3.8 %weight_grads.1 = f32[768,896]{1,0:T(8,128)} custom-call(bf16[128,768]{1,0:T(8,128)(2,1)} %get-tuple-element.297.refs_0_, bf16[128,576]{1,0:T(8,128)(2,1)} %get-tuple-element.298.refs_1_, bf16[128,192]{1,0:T(8,128)(2,1)} %get-tuple-element.299.refs_2_, bf16[128,768]{1,0:T(8,128)(2,1)} %get-tuple-element.300.refs_3_, ...), custom_call_target="tpu_custom_call" | custom-call | tf_op jit(solution)/shard_map/weight_grads/pallas_call | solution.py:132
  177.3 4.8 %expert_grads_top.1 = (f32[2,1,768,768]{3,2,1,0:T(8,128)}, f32[2,1,768,768]{3,2,1,0:T(8,128)}) custom-call(bf16[384,768]{1,0:T(8,128)(2,1)} %get-tuple-element.274.rows_ref, bf16[384,768]{1,0:T(8,128)(2,1)} %get-tuple-element.275.active_ref, bf16[384,768]{1,0:T(8,128)(2,1)} %get-tuple-element.276.grads_ref, bf16[384,768]{1,0:T(8,128)(2,1)} %get-tuple-element.277.down_ref), custom_call_target="tpu_custom_call" | custom-call | tf_op jit(solution)/shard_map/expert_grads_top/pallas_call | solution.py:148
  183.3 91.4 %while.16 = (s32[]{:T(128)}, f32[2,1,768,768]{3,2,1,0:T(8,128)}, f32[2,1,768,768]{3,2,1,0:T(8,128)}, f32[128,768]{1,0:T(8,128)}, bf16[768,896]{1,0:T(8,128)(2,1)...) while((s32[]{:T(128)}, f32[2,1,768,768]{3,2,1,0:T(8,128)}, ...), condition=%wide.region_1.0_spmd, body=%wide.region_0.0_spmd.sunk | while | flops 2 | bytes 19268428 | solution.py:1114
  183.3 3.1 %start_back.1 = (f32[128,768]{1,0:T(8,128)}, f32[1,768]{1,0:T(1,128)}, bf16[8,128]{1,0:T(8,128)(2,1)S(1)}, bf16[256,1152]{1,0:T(8,128)(2,1)S(1)}) custom-call(f32[128,768]{1,0:T(8,128)} %get-tuple-element.647.refs_0_, bf16[128,768]{1,0:T(8,128)(2,1)S(1)} %get-tuple-element.683.refs_1_, bf16[128,768]{1,0:T(8,128)(2,1)S(1)} %get-tuple-element.684.refs_2_, ...), custom_call_target="tpu_custom_call" | custom-call | tf_op jit(solution)/shard_map/while/body/start_back/pallas_call | solution.py:132
  186.5 17.8 %all_to_all.89 = bf16[32,8,1152]{2,1,0:T(8,128)(2,1)S(1)} all-to-all(bf16[32,8,1152]{2,1,0:T(8,128)(2,1)S(1)} %bitcast.42), channel_id=1, replica_groups=mesh['expert'=32,'tensor'=4] {'expert'}, dimensions={0} | all-to-all | bytes 1179648 | tf_op jit(solution)/shard_map/while/body/all_to_all | solution.py:878
  204.2 4.9 %expert_backward.1 = (bf16[384,768]{1,0:T(8,128)(2,1)}, bf16[384,768]{1,0:T(8,128)(2,1)}, bf16[256,1152]{1,0:T(8,128)(2,1)S(1)}) custom-call(bf16[256,1152]{1,0:T(8,128)(2,1)S(1)} %bitcast.40, f32[384,768]{1,0:T(8,128)} %get-tuple-element.692.refs_1_, bf16[2,768,768]{2,1,0:T(8,128)(2,1)} %get-tuple-element.693.refs_2_, ...), custom_call_target="tpu_custom_call" | custom-call | tf_op jit(solution)/shard_map/while/body/expert_backward/pallas_call | solution.py:132
  209.1 17.3 %all_to_all.90 = bf16[32,8,1152]{2,1,0:T(8,128)(2,1)S(1)} all-to-all(bf16[32,8,1152]{2,1,0:T(8,128)(2,1)S(1)} %bitcast.43), channel_id=1, replica_groups=mesh['expert'=32,'tensor'=4] {'expert'}, dimensions={0} | all-to-all | bytes 1179648 | tf_op jit(solution)/shard_map/while/body/all_to_all | solution.py:878
  228.4 2.5 collective-permute-start.2
  230.9 4.8 %expert_grads_low.1 = (f32[2,1,768,768]{3,2,1,0:T(8,128)}, f32[2,1,768,768]{3,2,1,0:T(8,128)}) custom-call(bf16[384,768]{1,0:T(8,128)(2,1)} %get-tuple-element.696.rows_ref, bf16[384,768]{1,0:T(8,128)(2,1)} %get-tuple-element.697.active_ref, bf16[384,768]{1,0:T(8,128)(2,1)} %get-tuple-element.595.grads_ref, ...), custom_call_target="tpu_custom_call", output_to_operand_aliasing={{0}: (4, {}), {1}: (5, {})} | custom-call | tf_op jit(solution)/shard_map/while/body/expert_grads_low/pallas_call | solution.py:148
  235.7 4.0 %collective-permute-done.refs_1_ = bf16[136,768]{1,0:T(8,128)(2,1)S(1)} collective-permute-done((bf16[136,768]{1,0:T(8,128)(2,1)S(1)}, bf16[136,768]{1,0:T(8,128)(2,1)S(1)}, u32[]{:S(2)}, u32[]{:S(2)}) %collective-permute-start) | collective-permute-done | bytes 208928 | tf_op jit(solution)/shard_map/while/body/ppermute | solution.py:872
  240.1 6.7 %attention_back_low.1 = (f32[128,768]{1,0:T(8,128)}, bf16[128,768]{1,0:T(8,128)(2,1)S(1)}, bf16[768,896]{1,0:T(8,128)(2,1)}) custom-call(bf16[136,768]{1,0:T(8,128)(2,1)S(1)} %combine_back.1.refs_0_, bf16[136,768]{1,0:T(8,128)(2,1)S(1)} %collective-permute-done.refs_1_, bf16[136,768]{1,0:T(8,128)(2,1)S(1)} %collective-permute-done.1.refs_2_, ...), custom_call_target="tpu_custom_call" | custom-call | tf_op jit(solution)/shard_map/while/body/attention_back_low/pallas_call | solution.py:132
  246.7 4.5 %all-to-all-start.2 = ((bf16[32,24,896]{2,1,0:T(8,128)(2,1)}), bf16[32,24,896]{2,1,0:T(8,128)(2,1)S(1)}, u32[]{:S(2)}, u32[]{:S(2)}) async-start(bf16[32,24,896]{2,1,0:T(8,128)(2,1)} %bitcast.59), calls=%async_computation.2 | async-start | bytes 2752512 | tf_op jit(solution)/shard_map/while/body/all_to_all | solution.py:878
  252.5 2.4 collective-permute-start.4
  255.3 3.4 %collective-permute-done.3.refs_2_ = bf16[128,768]{1,0:T(8,128)(2,1)S(1)} collective-permute-done((bf16[128,768]{1,0:T(8,128)(2,1)S(1)}, bf16[128,768]{1,0:T(8,128)(2,1)S(1)}, u32[]{:S(2)}, u32[]{:S(2)}) %collective-permute-start.3) | collective-permute-done | bytes 196640 | tf_op jit(solution)/shard_map/while/body/ppermute | solution.py:872
  258.7 5.1 %collective-permute-done.4.refs_3_ = bf16[128,768]{1,0:T(8,128)(2,1)S(1)} collective-permute-done((bf16[128,768]{1,0:T(8,128)(2,1)S(1)}, bf16[128,768]{1,0:T(8,128)(2,1)S(1)}, u32[]{:S(2)}, u32[]{:S(2)}) %collective-permute-start.4) | collective-permute-done | bytes 196640 | tf_op jit(solution)/shard_map/while/body/ppermute | solution.py:872
  264.9 7.8 %all-to-all-done.2 = bf16[32,24,896]{2,1,0:T(8,128)(2,1)S(1)} async-done(((bf16[32,24,896]{2,1,0:T(8,128)(2,1)}), bf16[32,24,896]{2,1,0:T(8,128)(2,1)S(1)}, u32[]{:S(2)}, u32[]{:S(2)}) %all-to-all-start.2) | async-done | bytes 1376288 | tf_op jit(solution)/shard_map/while/body/all_to_all | solution.py:878
  274.7 4.5 %all-to-all-start.7 = ((bf16[32,24,896]{2,1,0:T(8,128)(2,1)}), bf16[32,24,896]{2,1,0:T(8,128)(2,1)S(1)}, u32[]{:S(2)}, u32[]{:S(2)}) async-start(bf16[32,24,896]{2,1,0:T(8,128)(2,1)} %bitcast.60), calls=%async_computation.7 | async-start | bytes 2752512 | tf_op jit(solution)/shard_map/all_to_all | solution.py:878
  280.3 2.3 collective-permute-start.16
  283.0 3.8 %collective-permute-done.15.refs_2_ = bf16[128,768]{1,0:T(8,128)(2,1)S(1)} collective-permute-done((bf16[128,768]{1,0:T(8,128)(2,1)S(1)}, bf16[128,768]{1,0:T(8,128)(2,1)S(1)}, u32[]{:S(2)}, u32[]{:S(2)}) %collective-permute-start.15) | collective-permute-done | bytes 196640 | tf_op jit(solution)/shard_map/ppermute | solution.py:872
  286.8 4.9 %collective-permute-done.16.refs_3_ = bf16[128,768]{1,0:T(8,128)(2,1)S(1)} collective-permute-done((bf16[128,768]{1,0:T(8,128)(2,1)S(1)}, bf16[128,768]{1,0:T(8,128)(2,1)S(1)}, u32[]{:S(2)}, u32[]{:S(2)}) %collective-permute-start.16) | collective-permute-done | bytes 196640 | tf_op jit(solution)/shard_map/ppermute | solution.py:872
  292.5 6.4 %all-reduce.2.cloned.1.call-done.grads_ref = f32[768,896]{1,0:T(8,128)} async-done(((f32[768,896]{1,0:T(8,128)}), f32[768,896]{1,0:T(8,128)}) %all-reduce.2.cloned.1.call-update) | async-done | bytes 2752528 | tf_op jit(solution)/shard_map/psum | solution.py:1038
  298.9 2.9 place_top.1
  301.8 2.4 place_low.1
  (78 shorter events, 24.6 us)
Async XLA Ops:
  7.2 18.9 %copy-start.8 = (bf16[128,768]{1,0:T(8,128)(2,1)S(1)}, bf16[128,768]{1,0:T(8,128)(2,1)}, u32[]{:S(2)}) copy-start(bf16[128,768]{1,0:T(8,128)(2,1)} %refs_0_.3) | copy-start | bytes 589828
  7.2 18.9 %copy-start.9 = (f32[2,2,768]{2,1,0:T(2,128)S(1)}, f32[2,2,768]{2,1,0:T(2,128)}, u32[]{:S(2)}) copy-start(f32[2,2,768]{2,1,0:T(2,128)} %refs_8_.3) | copy-start | bytes 36868
  7.2 291.7 %all-reduce.2.cloned.1.call-start = ((), (), s32[]{:S(2)}) async-start(), calls=%async_computation.8 | async-start | bytes 5505024 | tf_op jit(solution)/shard_map/psum | solution.py:1038
  9.3 40.3 %copy-start.3 = (f32[2,3,128,128]{3,2,1,0:T(8,128)}, f32[2,3,128,128]{3,2,1,0:T(8,128)S(1)}, u32[]{:S(2)}) copy-start(f32[2,3,128,128]{3,2,1,0:T(8,128)S(1)} %get-tuple-element.253.refs_3_.refs_7_) | copy-start | bytes 1179652
  9.3 40.3 %copy-start.6 = (bf16[2,1,768,768]{3,2,1,0:T(8,128)(2,1)S(1)}, bf16[2,1,768,768]{3,2,1,0:T(8,128)(2,1)}, u32[]{:S(2)}) copy-start(bf16[2,1,768,768]{3,2,1,0:T(8,128)(2,1)} %param.23) | copy-start | bytes 7077892
  9.3 40.3 %copy-start.7 = (bf16[2,1,768,768]{3,2,1,0:T(8,128)(2,1)S(1)}, bf16[2,1,768,768]{3,2,1,0:T(8,128)(2,1)}, u32[]{:S(2)}) copy-start(bf16[2,1,768,768]{3,2,1,0:T(8,128)(2,1)} %param.24) | copy-start | bytes 7077892
  12.7 8.1 %collective-permute-start.6 = (bf16[128,768]{1,0:T(8,128)(2,1)S(1)}, bf16[128,768]{1,0:T(8,128)(2,1)S(1)}, u32[]{:S(2)}, u32[]{:S(2)}) collective-permute-start(bf16[128,768]{1,0:T(8,128)(2,1)S(1)} %get-tuple-element.254.refs_1_), channel_id=1, source_target_pairs={{0,1},{1,2},{2,3},{3,0},{4,5},{5,6},{6,7},{7,4},{8,9},{9,10},{10,1... | collective-permute-start | bytes 589832 | tf_op jit(solution)/shard_map/ppermute | solution.py:872
  14.9 11.1 %collective-permute-start.7 = (bf16[128,768]{1,0:T(8,128)(2,1)S(1)}, bf16[128,768]{1,0:T(8,128)(2,1)S(1)}, u32[]{:S(2)}, u32[]{:S(2)}) collective-permute-start(bf16[128,768]{1,0:T(8,128)(2,1)S(1)} %get-tuple-element.254.refs_1_), channel_id=1, source_target_pairs={{0,2},{1,3},{2,0},{3,1},{4,6},{5,7},{6,4},{7,5},{8,10},{9,11},{10,... | collective-permute-start | bytes 589832 | tf_op jit(solution)/shard_map/ppermute | solution.py:872
  17.6 8.5 %collective-permute-start.8 = (bf16[128,768]{1,0:T(8,128)(2,1)S(1)}, bf16[128,768]{1,0:T(8,128)(2,1)S(1)}, u32[]{:S(2)}, u32[]{:S(2)}) collective-permute-start(bf16[128,768]{1,0:T(8,128)(2,1)S(1)} %get-tuple-element.254.refs_1_), channel_id=1, source_target_pairs={{0,3},{1,0},{2,1},{3,2},{4,7},{5,4},{6,5},{7,6},{8,11},{9,8},{10,9... | collective-permute-start | bytes 589832 | tf_op jit(solution)/shard_map/ppermute | solution.py:872
  67.5 30.8 %copy-start.1 = (bf16[128,768]{1,0:T(8,128)(2,1)S(1)}, bf16[128,768]{1,0:T(8,128)(2,1)}, u32[]{:S(2)}) copy-start(bf16[128,768]{1,0:T(8,128)(2,1)} %refs_9_.3) | copy-start | bytes 589828
  69.6 8.0 %collective-permute-start.9 = (bf16[128,768]{1,0:T(8,128)(2,1)S(1)}, bf16[128,768]{1,0:T(8,128)(2,1)S(1)}, u32[]{:S(2)}, u32[]{:S(2)}) collective-permute-start(bf16[128,768]{1,0:T(8,128)(2,1)S(1)} %get-tuple-element.261.refs_1_), channel_id=1, source_target_pairs={{0,1},{1,2},{2,3},{3,0},{4,5},{5,6},{6,7},{7,4},{8,9},{9,10},{10,1... | collective-permute-start | bytes 589832 | tf_op jit(solution)/shard_map/ppermute | solution.py:872
  70.7 11.5 %collective-permute-start.10 = (bf16[128,768]{1,0:T(8,128)(2,1)S(1)}, bf16[128,768]{1,0:T(8,128)(2,1)S(1)}, u32[]{:S(2)}, u32[]{:S(2)}) collective-permute-start(bf16[128,768]{1,0:T(8,128)(2,1)S(1)} %get-tuple-element.261.refs_1_), channel_id=1, source_target_pairs={{0,2},{1,3},{2,0},{3,1},{4,6},{5,7},{6,4},{7,5},{8,10},{9,11},{10,... | collective-permute-start | bytes 589832 | tf_op jit(solution)/shard_map/ppermute | solution.py:872
  72.8 9.5 %collective-permute-start.11 = (bf16[128,768]{1,0:T(8,128)(2,1)S(1)}, bf16[128,768]{1,0:T(8,128)(2,1)S(1)}, u32[]{:S(2)}, u32[]{:S(2)}) collective-permute-start(bf16[128,768]{1,0:T(8,128)(2,1)S(1)} %get-tuple-element.261.refs_1_), channel_id=1, source_target_pairs={{0,3},{1,0},{2,1},{3,2},{4,7},{5,4},{6,5},{7,6},{8,11},{9,8},{10,9... | collective-permute-start | bytes 589832 | tf_op jit(solution)/shard_map/ppermute | solution.py:872
  85.6 6.9 %collective-permute-start.12 = (bf16[128,768]{1,0:T(8,128)(2,1)S(1)}, bf16[128,768]{1,0:T(8,128)(2,1)S(1)}, u32[]{:S(2)}, u32[]{:S(2)}) collective-permute-start(bf16[128,768]{1,0:T(8,128)(2,1)S(1)} %get-tuple-element.263.refs_1_), channel_id=1, source_target_pairs={{0,1},{1,2},{2,3},{3,0},{4,5},{5,6},{6,7},{7,4},{8,9},{9,10},{10,1... | collective-permute-start | bytes 589832 | tf_op jit(solution)/shard_map/ppermute | solution.py:872
  87.2 11.1 %collective-permute-start.13 = (bf16[128,768]{1,0:T(8,128)(2,1)S(1)}, bf16[128,768]{1,0:T(8,128)(2,1)S(1)}, u32[]{:S(2)}, u32[]{:S(2)}) collective-permute-start(bf16[128,768]{1,0:T(8,128)(2,1)S(1)} %get-tuple-element.263.refs_1_), channel_id=1, source_target_pairs={{0,2},{1,3},{2,0},{3,1},{4,6},{5,7},{6,4},{7,5},{8,10},{9,11},{10,... | collective-permute-start | bytes 589832 | tf_op jit(solution)/shard_map/ppermute | solution.py:872
  89.6 8.8 %collective-permute-start.14 = (bf16[128,768]{1,0:T(8,128)(2,1)S(1)}, bf16[128,768]{1,0:T(8,128)(2,1)S(1)}, u32[]{:S(2)}, u32[]{:S(2)}) collective-permute-start(bf16[128,768]{1,0:T(8,128)(2,1)S(1)} %get-tuple-element.263.refs_1_), channel_id=1, source_target_pairs={{0,3},{1,0},{2,1},{3,2},{4,7},{5,4},{6,5},{7,6},{8,11},{9,8},{10,9... | collective-permute-start | bytes 589832 | tf_op jit(solution)/shard_map/ppermute | solution.py:872
  127.2 36.0 %copy-start.2 = (f32[128,768]{1,0:T(8,128)S(1)}, f32[128,768]{1,0:T(8,128)}, u32[]{:S(2)}) copy-start(f32[128,768]{1,0:T(8,128)} %get-tuple-element.264.refs_0_.refs_7_) | copy-start | bytes 1179652
  127.2 35.9 %copy-start.4 = (bf16[3,128,192]{2,1,0:T(8,128)(2,1)S(1)}, bf16[3,128,192]{2,1,0:T(8,128)(2,1)}, u32[]{:S(2)}) copy-start(bf16[3,128,192]{2,1,0:T(8,128)(2,1)} %get-tuple-element.270.refs_11_) | copy-start | bytes 442372
  127.2 35.9 %copy-start.5 = (f32[3,128,128]{2,1,0:T(8,128)S(1)}, f32[3,128,128]{2,1,0:T(8,128)}, u32[]{:S(2)}) copy-start(f32[3,128,128]{2,1,0:T(8,128)} %get-tuple-element.271.refs_12_) | copy-start | bytes 589828
  150.7 7.6 %collective-permute-start.18 = (bf16[136,768]{1,0:T(8,128)(2,1)S(1)}, bf16[136,768]{1,0:T(8,128)(2,1)S(1)}, u32[]{:S(2)}, u32[]{:S(2)}) collective-permute-start(bf16[136,768]{1,0:T(8,128)(2,1)S(1)} %get-tuple-element.269.refs_0_), channel_id=1, source_target_pairs={{0,1},{1,2},{2,3},{3,0},{4,5},{5,6},{6,7},{7,4},{8,9},{9,10},{10,1... | collective-permute-start | bytes 626696 | tf_op jit(solution)/shard_map/ppermute | solution.py:872
  151.6 11.6 %collective-permute-start.19 = (bf16[136,768]{1,0:T(8,128)(2,1)S(1)}, bf16[136,768]{1,0:T(8,128)(2,1)S(1)}, u32[]{:S(2)}, u32[]{:S(2)}) collective-permute-start(bf16[136,768]{1,0:T(8,128)(2,1)S(1)} %get-tuple-element.269.refs_0_), channel_id=1, source_target_pairs={{0,2},{1,3},{2,0},{3,1},{4,6},{5,7},{6,4},{7,5},{8,10},{9,11},{10,... | collective-permute-start | bytes 626696 | tf_op jit(solution)/shard_map/ppermute | solution.py:872
  153.8 9.4 %collective-permute-start.20 = (bf16[136,768]{1,0:T(8,128)(2,1)S(1)}, bf16[136,768]{1,0:T(8,128)(2,1)S(1)}, u32[]{:S(2)}, u32[]{:S(2)}) collective-permute-start(bf16[136,768]{1,0:T(8,128)(2,1)S(1)} %get-tuple-element.269.refs_0_), channel_id=1, source_target_pairs={{0,3},{1,0},{2,1},{3,2},{4,7},{5,4},{6,5},{7,6},{8,11},{9,8},{10,9... | collective-permute-start | bytes 626696 | tf_op jit(solution)/shard_map/ppermute | solution.py:872
  167.7 14.4 %collective-permute-start.21 = (bf16[128,768]{1,0:T(8,128)(2,1)S(1)}, bf16[128,768]{1,0:T(8,128)(2,1)S(1)}, u32[]{:S(2)}, u32[]{:S(2)}) collective-permute-start(bf16[128,768]{1,0:T(8,128)(2,1)S(1)} %get-tuple-element.617), channel_id=1, source_target_pairs={{0,1},{1,2},{2,3},{3,0},{4,5},{5,6},{6,7},{7,4},{8,9},{9,10},{10,1... | collective-permute-start | bytes 589832 | tf_op jit(solution)/shard_map/ppermute | solution.py:872
  169.6 12.5 %collective-permute-start.22 = (bf16[128,768]{1,0:T(8,128)(2,1)S(1)}, bf16[128,768]{1,0:T(8,128)(2,1)S(1)}, u32[]{:S(2)}, u32[]{:S(2)}) collective-permute-start(bf16[128,768]{1,0:T(8,128)(2,1)S(1)} %get-tuple-element.617), channel_id=1, source_target_pairs={{0,2},{1,3},{2,0},{3,1},{4,6},{5,7},{6,4},{7,5},{8,10},{9,11},{10,... | collective-permute-start | bytes 589832 | tf_op jit(solution)/shard_map/ppermute | solution.py:872
  172.3 9.8 %collective-permute-start.23 = (bf16[128,768]{1,0:T(8,128)(2,1)S(1)}, bf16[128,768]{1,0:T(8,128)(2,1)S(1)}, u32[]{:S(2)}, u32[]{:S(2)}) collective-permute-start(bf16[128,768]{1,0:T(8,128)(2,1)S(1)} %get-tuple-element.617), channel_id=1, source_target_pairs={{0,3},{1,0},{2,1},{3,2},{4,7},{5,4},{6,5},{7,6},{8,11},{9,8},{10,9... | collective-permute-start | bytes 589832 | tf_op jit(solution)/shard_map/ppermute | solution.py:872
  172.3 3.8 %copy-start.19 = (s32[255]{0:T(256)S(1)}, s32[255]{0:T(256)}, u32[]{:S(2)}) copy-start(s32[255]{0:T(256)} %param.17) | copy-start | bytes 3064
  183.3 3.2 %copy-start.15 = (bf16[128,768]{1,0:T(8,128)(2,1)}, bf16[128,768]{1,0:T(8,128)(2,1)S(1)}, u32[]{:S(2)}) copy-start(bf16[128,768]{1,0:T(8,128)(2,1)S(1)} %get-tuple-element.685.refs_3_) | copy-start | bytes 589828 | tf_op jit(solution)/shard_map/while
  183.3 3.2 %copy-start.17 = (bf16[128,768]{1,0:T(8,128)(2,1)}, bf16[128,768]{1,0:T(8,128)(2,1)S(1)}, u32[]{:S(2)}) copy-start(bf16[128,768]{1,0:T(8,128)(2,1)S(1)} %get-tuple-element.686.refs_4_) | copy-start | bytes 589828 | tf_op jit(solution)/shard_map/while
  183.3 25.8 %copy-start.11 = (bf16[128,768]{1,0:T(8,128)(2,1)}, bf16[128,768]{1,0:T(8,128)(2,1)S(1)}, u32[]{:S(2)}) copy-start(bf16[128,768]{1,0:T(8,128)(2,1)S(1)} %get-tuple-element.683.refs_1_) | copy-start | bytes 589828 | tf_op jit(solution)/shard_map/while
  183.3 25.8 %copy-start.13 = (bf16[128,768]{1,0:T(8,128)(2,1)}, bf16[128,768]{1,0:T(8,128)(2,1)S(1)}, u32[]{:S(2)}) copy-start(bf16[128,768]{1,0:T(8,128)(2,1)S(1)} %get-tuple-element.684.refs_2_) | copy-start | bytes 589828 | tf_op jit(solution)/shard_map/while
  226.9 12.7 %collective-permute-start = (bf16[136,768]{1,0:T(8,128)(2,1)S(1)}, bf16[136,768]{1,0:T(8,128)(2,1)S(1)}, u32[]{:S(2)}, u32[]{:S(2)}) collective-permute-start(bf16[136,768]{1,0:T(8,128)(2,1)S(1)} %combine_back.1.refs_0_), channel_id=1, source_target_pairs={{0,1},{1,2},{2,3},{3,0},{4,5},{5,6},{6,7},{7,4},{8,9},{9,10},{10,1... | collective-permute-start | bytes 626696 | tf_op jit(solution)/shard_map/while/body/ppermute | solution.py:872
  228.4 11.3 %collective-permute-start.1 = (bf16[136,768]{1,0:T(8,128)(2,1)S(1)}, bf16[136,768]{1,0:T(8,128)(2,1)S(1)}, u32[]{:S(2)}, u32[]{:S(2)}) collective-permute-start(bf16[136,768]{1,0:T(8,128)(2,1)S(1)} %combine_back.1.refs_0_), channel_id=1, source_target_pairs={{0,2},{1,3},{2,0},{3,1},{4,6},{5,7},{6,4},{7,5},{8,10},{9,11},{10,... | collective-permute-start | bytes 626696 | tf_op jit(solution)/shard_map/while/body/ppermute | solution.py:872
  228.4 11.7 %collective-permute-start.2 = (bf16[136,768]{1,0:T(8,128)(2,1)S(1)}, bf16[136,768]{1,0:T(8,128)(2,1)S(1)}, u32[]{:S(2)}, u32[]{:S(2)}) collective-permute-start(bf16[136,768]{1,0:T(8,128)(2,1)S(1)} %combine_back.1.refs_0_), channel_id=1, source_target_pairs={{0,3},{1,0},{2,1},{3,2},{4,7},{5,4},{6,5},{7,6},{8,11},{9,8},{10,9... | collective-permute-start | bytes 626696 | tf_op jit(solution)/shard_map/while/body/ppermute | solution.py:872
  230.8 9.2 %copy-start.10 = (f32[2,2,768]{2,1,0:T(2,128)S(1)}, f32[2,2,768]{2,1,0:T(2,128)}, u32[]{:S(2)}) copy-start(f32[2,2,768]{2,1,0:T(2,128)} %get-tuple-element.794) | copy-start | bytes 36868 | tf_op jit(solution)/shard_map/while
  246.7 17.1 %copy-start = (f32[128,768]{1,0:T(8,128)S(1)}, f32[128,768]{1,0:T(8,128)}, u32[]{:S(2)}) copy-start(f32[128,768]{1,0:T(8,128)} %get-tuple-element.606.refs_0_) | copy-start | bytes 1179652 | tf_op jit(solution)/shard_map/while
  246.7 26.0 %all-to-all-start.2 = ((bf16[32,24,896]{2,1,0:T(8,128)(2,1)}), bf16[32,24,896]{2,1,0:T(8,128)(2,1)S(1)}, u32[]{:S(2)}, u32[]{:S(2)}) async-start(bf16[32,24,896]{2,1,0:T(8,128)(2,1)} %bitcast.59), calls=%async_computation.2 | async-start | bytes 2752512 | tf_op jit(solution)/shard_map/while/body/all_to_all | solution.py:878
  251.3 7.4 %collective-permute-start.3 = (bf16[128,768]{1,0:T(8,128)(2,1)S(1)}, bf16[128,768]{1,0:T(8,128)(2,1)S(1)}, u32[]{:S(2)}, u32[]{:S(2)}) collective-permute-start(bf16[128,768]{1,0:T(8,128)(2,1)S(1)} %get-tuple-element.607.refs_1_), channel_id=1, source_target_pairs={{0,1},{1,2},{2,3},{3,0},{4,5},{5,6},{6,7},{7,4},{8,9},{9,10},{10,1... | collective-permute-start | bytes 589832 | tf_op jit(solution)/shard_map/while/body/ppermute | solution.py:872
  252.5 11.3 %collective-permute-start.4 = (bf16[128,768]{1,0:T(8,128)(2,1)S(1)}, bf16[128,768]{1,0:T(8,128)(2,1)S(1)}, u32[]{:S(2)}, u32[]{:S(2)}) collective-permute-start(bf16[128,768]{1,0:T(8,128)(2,1)S(1)} %get-tuple-element.607.refs_1_), channel_id=1, source_target_pairs={{0,2},{1,3},{2,0},{3,1},{4,6},{5,7},{6,4},{7,5},{8,10},{9,11},{10,... | collective-permute-start | bytes 589832 | tf_op jit(solution)/shard_map/while/body/ppermute | solution.py:872
  254.9 8.9 %collective-permute-start.5 = (bf16[128,768]{1,0:T(8,128)(2,1)S(1)}, bf16[128,768]{1,0:T(8,128)(2,1)S(1)}, u32[]{:S(2)}, u32[]{:S(2)}) collective-permute-start(bf16[128,768]{1,0:T(8,128)(2,1)S(1)} %get-tuple-element.607.refs_1_), channel_id=1, source_target_pairs={{0,3},{1,0},{2,1},{3,2},{4,7},{5,4},{6,5},{7,6},{8,11},{9,8},{10,9... | collective-permute-start | bytes 589832 | tf_op jit(solution)/shard_map/while/body/ppermute | solution.py:872
  264.8 9.8 %copy-start.12 = (bf16[128,768]{1,0:T(8,128)(2,1)S(1)}, bf16[128,768]{1,0:T(8,128)(2,1)}, u32[]{:S(2)}) copy-start(bf16[128,768]{1,0:T(8,128)(2,1)} %copy-done.11) | copy-start | bytes 589828 | tf_op jit(solution)/shard_map/while
  264.8 9.8 %copy-start.14 = (bf16[128,768]{1,0:T(8,128)(2,1)S(1)}, bf16[128,768]{1,0:T(8,128)(2,1)}, u32[]{:S(2)}) copy-start(bf16[128,768]{1,0:T(8,128)(2,1)} %copy-done.13) | copy-start | bytes 589828 | tf_op jit(solution)/shard_map/while
  264.9 9.8 %copy-start.16 = (bf16[128,768]{1,0:T(8,128)(2,1)S(1)}, bf16[128,768]{1,0:T(8,128)(2,1)}, u32[]{:S(2)}) copy-start(bf16[128,768]{1,0:T(8,128)(2,1)} %copy-done.15) | copy-start | bytes 589828 | tf_op jit(solution)/shard_map/while
  264.9 9.8 %copy-start.18 = (bf16[128,768]{1,0:T(8,128)(2,1)S(1)}, bf16[128,768]{1,0:T(8,128)(2,1)}, u32[]{:S(2)}) copy-start(bf16[128,768]{1,0:T(8,128)(2,1)} %copy-done.17) | copy-start | bytes 589828 | tf_op jit(solution)/shard_map/while
  274.7 27.2 %all-to-all-start.7 = ((bf16[32,24,896]{2,1,0:T(8,128)(2,1)}), bf16[32,24,896]{2,1,0:T(8,128)(2,1)S(1)}, u32[]{:S(2)}, u32[]{:S(2)}) async-start(bf16[32,24,896]{2,1,0:T(8,128)(2,1)} %bitcast.60), calls=%async_computation.7 | async-start | bytes 2752512 | tf_op jit(solution)/shard_map/all_to_all | solution.py:878
  279.1 7.7 %collective-permute-start.15 = (bf16[128,768]{1,0:T(8,128)(2,1)S(1)}, bf16[128,768]{1,0:T(8,128)(2,1)S(1)}, u32[]{:S(2)}, u32[]{:S(2)}) collective-permute-start(bf16[128,768]{1,0:T(8,128)(2,1)S(1)} %get-tuple-element.268.refs_1_), channel_id=1, source_target_pairs={{0,1},{1,2},{2,3},{3,0},{4,5},{5,6},{6,7},{7,4},{8,9},{9,10},{10,1... | collective-permute-start | bytes 589832 | tf_op jit(solution)/shard_map/ppermute | solution.py:872
  280.3 11.4 %collective-permute-start.16 = (bf16[128,768]{1,0:T(8,128)(2,1)S(1)}, bf16[128,768]{1,0:T(8,128)(2,1)S(1)}, u32[]{:S(2)}, u32[]{:S(2)}) collective-permute-start(bf16[128,768]{1,0:T(8,128)(2,1)S(1)} %get-tuple-element.268.refs_1_), channel_id=1, source_target_pairs={{0,2},{1,3},{2,0},{3,1},{4,6},{5,7},{6,4},{7,5},{8,10},{9,11},{10,... | collective-permute-start | bytes 589832 | tf_op jit(solution)/shard_map/ppermute | solution.py:872
  282.7 9.0 %collective-permute-start.17 = (bf16[128,768]{1,0:T(8,128)(2,1)S(1)}, bf16[128,768]{1,0:T(8,128)(2,1)S(1)}, u32[]{:S(2)}, u32[]{:S(2)}) collective-permute-start(bf16[128,768]{1,0:T(8,128)(2,1)S(1)} %get-tuple-element.268.refs_1_), channel_id=1, source_target_pairs={{0,3},{1,0},{2,1},{3,2},{4,7},{5,4},{6,5},{7,6},{8,11},{9,8},{10,9... | collective-permute-start | bytes 589832 | tf_op jit(solution)/shard_map/ppermute | solution.py:872
Sparse Core Ops, SparseCore 0:
  176.2 122.6 all-reduce.1

commit v4 on v3

--- a/solution.py
+++ b/solution.py
@@ -440,22 +440,23 @@
     return 0.5 * (1.0 + bent) + 0.5 * values * (1.0 - bent * bent) * inner
 
 
-def expert_forward(got_ref, in_ref, out_ref, rows_ref, before_ref, active_ref, back_ref):
+def expert_forward(got_ref, in_ref, out_ref, rows_ref, slope_ref, active_ref, back_ref):
     unpack(got_ref, 0, rows_ref)
+    go(rows_ref)
     before = dot(rows_ref[...], in_ref[...])
-    before_ref[...] = before
-    go(rows_ref, before_ref)
+    slope_ref[...] = gelu_slope(before).astype(bf16)
+    go(slope_ref)
     active = gelu(before).astype(bf16)
     active_ref[...] = active
     go(active_ref)
     pack(dot(active, out_ref[...]).astype(bf16), 0, back_ref)
 
 
-def expert_backward(got_ref, before_ref, in_ref, out_ref, grads_ref, down_ref, back_ref):
+def expert_backward(got_ref, out_ref, slope_ref, in_ref, grads_ref, down_ref, back_ref):
     unpack(got_ref, 0, grads_ref)
     go(grads_ref)
     grad_active = dot(grads_ref[...], out_ref[...], 1, 1)
-    grad_before = (grad_active * gelu_slope(before_ref[...])).astype(bf16)
+    grad_before = (grad_active * slope_ref[...].astype(f32)).astype(bf16)
     down_ref[...] = grad_before
     go(down_ref)
     pack(dot(grad_before, in_ref[...], 1, 1).astype(bf16), 0, back_ref)
@@ -941,9 +942,9 @@
         Layer(across, 0),
         Layer(down, 0),
     )
-    rows0, before0, active0, send = call(
+    rows0, slope0, active0, send = call(
         expert_forward,
-        [Kept(slots, bf16), Kept(slots, f32), Kept(slots, bf16), ((MAIN, SENT), bf16)],
+        [Kept(slots, bf16), Kept(slots, bf16), Kept(slots, bf16), ((MAIN, SENT), bf16)],
         across_experts(send),
         Layer(expert_in, 0),
         Layer(expert_out, 0),
@@ -1055,9 +1056,9 @@
             expert_backward,
             [Kept(slots, bf16), Kept(slots, bf16), ((MAIN, SENT), bf16)],
             across_experts(send),
-            Late(before0),
+            Late(Layer(expert_out, 0)),
+            Late(slope0),
             Late(Layer(expert_in, 0)),
-            Late(Layer(expert_out, 0)),
         )
         got = across_experts(send)
         in_grads, out_grads = call_stacked(

time: 313 us -> 312 us (level)
  transfers between devices with their start and end apart: 27 -> 27, of which waited for: 16 -> 17; matrix products, arithmetic and copies ran while one was open for 1% -> 1% of each run, Pallas kernels for 11% -> 11%
where the time goes in v4:
time: 312 us; the launch traced here: 309 us
  blocking collectives  118 us (38%)
  waiting for transfers between devices  68.2 us (22%)
  Pallas kernels  62.2 us (20%)
  starting transfers between devices  43.6 us (14%)
  between operations  15 us (5%)
    all_to_all x6, blocking collectives, across_experts(): return lax.all_to_all(values, 'expert', 0, 0, tiled=True)  118 us
    ppermute x24, waiting for transfers between devices, around(): lax.ppermute(values, 'tensor', [(i, (i + shift) % 4) for i in range(4)])  54.7 us
    pallas_call x18, Pallas kernels, call(): pl.pallas_call(kernel, out_shape=[pltpu.HBM(*o) if is_kept else jax.Shape...  47.3 us
    ppermute x24, starting transfers between devices, around(): lax.ppermute(values, 'tensor', [(i, (i + shift) % 4) for i in range(4)])  34.6 us
    pallas_call x2, Pallas kernels, call_stacked(): pl.pallas_call(body, grid=(1,), out_shape=[pltpu.HBM(stacked, f32)] * 2,...  9.59 us
    all_to_all x2, starting transfers between devices, across_experts(): return lax.all_to_all(values, 'expert', 0, 0, tiled=True)  8.94 us
    all_to_all x2, waiting for transfers between devices, across_experts(): return lax.all_to_all(values, 'expert', 0, 0, tiled=True)  7.91 us
  transfers between devices with their start and end apart: 27, of which 17 were waited for; matrix products, arithmetic and copies ran while one was open for 1% of the time, Pallas kernels for 11%

profile of v4, /device:TPU:1, one launch (start us, length us, event | category | flops | bytes accessed | tf_op | source)
XLA Modules:
  0.0 309.3 jit_solution(1023785632519582947)
XLA Ops:
  9.4 3.4 %attention_first.1 = (bf16[128,768]{1,0:T(8,128)(2,1)}, bf16[3,128,192]{2,1,0:T(8,128)(2,1)}, f32[3,128,128]{2,1,0:T(8,128)}, bf16[128,192]{1,0:T(8,128)(2,1)}, bf16[128,768]{1,0:T(8,128)(2,1)S(1)}) custom-call(bf16[128,768]{1,0:T(8,128)(2,1)} %refs_0_.3, f32[2,2,768]{2,1,0:T(2,128)} %refs_8_.3, bf16[2,3,192,768]{3,2,1,0:T(8,128)(2,1)} %bitcast.6.refs_2_.refs_6_.refs_13_, ...), custom_call_target="tpu_custom_call" | custom-call | tf_op jit(solution)/shard_map/attention_first/pallas_call | solution.py:132
  12.7 2.2 collective-permute-start.6
  14.9 2.6 collective-permute-start.7
  18.6 2.2 collective-permute-done.6.refs_2_
  20.9 5.2 %collective-permute-done.7.refs_3_ = bf16[128,768]{1,0:T(8,128)(2,1)S(1)} collective-permute-done((bf16[128,768]{1,0:T(8,128)(2,1)S(1)}, bf16[128,768]{1,0:T(8,128)(2,1)S(1)}, u32[]{:S(2)}, u32[]{:S(2)}) %collective-permute-start.7) | collective-permute-done | bytes 196640 | tf_op jit(solution)/shard_map/ppermute | solution.py:873
  28.1 21.5 %all_to_all.85 = bf16[32,8,1152]{2,1,0:T(8,128)(2,1)S(1)} all-to-all(bf16[32,8,1152]{2,1,0:T(8,128)(2,1)S(1)} %bitcast.51), channel_id=1, replica_groups=mesh['expert'=32,'tensor'=4] {'expert'}, dimensions={0} | all-to-all | bytes 1179648 | tf_op jit(solution)/shard_map/all_to_all | solution.py:879
  49.7 2.3 expert_forward.1
  52.0 15.8 %all_to_all.86 = bf16[32,8,1152]{2,1,0:T(8,128)(2,1)S(1)} all-to-all(bf16[32,8,1152]{2,1,0:T(8,128)(2,1)S(1)} %bitcast.52), channel_id=1, replica_groups=mesh['expert'=32,'tensor'=4] {'expert'}, dimensions={0} | all-to-all | bytes 1179648 | tf_op jit(solution)/shard_map/all_to_all | solution.py:879
  67.8 2.1 combine_first.1
  70.9 2.1 collective-permute-start.10
  74.3 3.5 %collective-permute-done.9.refs_2_ = bf16[128,768]{1,0:T(8,128)(2,1)S(1)} collective-permute-done((bf16[128,768]{1,0:T(8,128)(2,1)S(1)}, bf16[128,768]{1,0:T(8,128)(2,1)S(1)}, u32[]{:S(2)}, u32[]{:S(2)}) %collective-permute-start.9) | collective-permute-done | bytes 196640 | tf_op jit(solution)/shard_map/ppermute | solution.py:873
  77.8 4.6 %collective-permute-done.10.refs_3_ = bf16[128,768]{1,0:T(8,128)(2,1)S(1)} collective-permute-done((bf16[128,768]{1,0:T(8,128)(2,1)S(1)}, bf16[128,768]{1,0:T(8,128)(2,1)S(1)}, u32[]{:S(2)}, u32[]{:S(2)}) %collective-permute-start.10) | collective-permute-done | bytes 196640 | tf_op jit(solution)/shard_map/ppermute | solution.py:873
  82.5 3.4 %attention_next.1 = (f32[128,768]{1,0:T(8,128)}, bf16[128,768]{1,0:T(8,128)(2,1)}, bf16[3,128,192]{2,1,0:T(8,128)(2,1)}, f32[3,128,128]{2,1,0:T(8,128)}, bf16[12...) custom-call(f32[128,768]{1,0:T(8,128)} %get-tuple-element.633.refs_0_, bf16[128,768]{1,0:T(8,128)(2,1)S(1)} %get-tuple-element.261.refs_1_, ...), custom_call_target="tpu_custom_call" | custom-call | tf_op jit(solution)/shard_map/attention_next/pallas_call | solution.py:132
  87.5 2.3 collective-permute-start.13
  90.3 2.5 collective-permute-done.12.refs_2_
  92.8 5.8 %collective-permute-done.13.refs_3_ = bf16[128,768]{1,0:T(8,128)(2,1)S(1)} collective-permute-done((bf16[128,768]{1,0:T(8,128)(2,1)S(1)}, bf16[128,768]{1,0:T(8,128)(2,1)S(1)}, u32[]{:S(2)}, u32[]{:S(2)}) %collective-permute-start.13) | collective-permute-done | bytes 196640 | tf_op jit(solution)/shard_map/ppermute | solution.py:873
  98.6 2.2 route_next.1
  100.7 23.4 %all_to_all.87 = bf16[32,8,2304]{2,1,0:T(8,128)(2,1)S(1)} all-to-all(bf16[32,8,2304]{2,1,0:T(8,128)(2,1)S(1)} %bitcast.49), channel_id=1, replica_groups=mesh['expert'=32,'tensor'=4] {'expert'}, dimensions={0} | all-to-all | bytes 2359296 | tf_op jit(solution)/shard_map/all_to_all | solution.py:879
  124.2 3.3 %expert_both.1 = (bf16[384,768]{1,0:T(8,128)(2,1)}, bf16[384,768]{1,0:T(8,128)(2,1)}, bf16[384,768]{1,0:T(8,128)(2,1)}, bf16[384,768]{1,0:T(8,128)(2,1)}, bf16[256,2304]{1,0:T(8,128)(2,1)S(1)}) custom-call(bf16[256,2304]{1,0:T(8,128)(2,1)S(1)} %bitcast.46, bf16[2,768,768]{2,1,0:T(8,128)(2,1)S(1)} %bitcast.55, bf16[2,768,768]{2,1,0:T(8,128)(2,1)S(1)} %bitcast.58), custom_call_target="tpu_custom_call" | custom-call | tf_op jit(solution)/shard_map/expert_both/pallas_call | solution.py:132
  127.5 22.6 %all_to_all.88 = bf16[32,8,2304]{2,1,0:T(8,128)(2,1)S(1)} all-to-all(bf16[32,8,2304]{2,1,0:T(8,128)(2,1)S(1)} %bitcast.50), channel_id=1, replica_groups=mesh['expert'=32,'tensor'=4] {'expert'}, dimensions={0} | all-to-all | bytes 2359296 | tf_op jit(solution)/shard_map/all_to_all | solution.py:879
  151.8 2.2 collective-permute-start.19
  154.5 4.0 %collective-permute-done.18.refs_1_ = bf16[136,768]{1,0:T(8,128)(2,1)S(1)} collective-permute-done((bf16[136,768]{1,0:T(8,128)(2,1)S(1)}, bf16[136,768]{1,0:T(8,128)(2,1)S(1)}, u32[]{:S(2)}, u32[]{:S(2)}) %collective-permute-start.18) | collective-permute-done | bytes 208928 | tf_op jit(solution)/shard_map/ppermute | solution.py:873
  158.5 4.9 %collective-permute-done.19.refs_2_ = bf16[136,768]{1,0:T(8,128)(2,1)S(1)} collective-permute-done((bf16[136,768]{1,0:T(8,128)(2,1)S(1)}, bf16[136,768]{1,0:T(8,128)(2,1)S(1)}, u32[]{:S(2)}, u32[]{:S(2)}) %collective-permute-start.19) | collective-permute-done | bytes 208928 | tf_op jit(solution)/shard_map/ppermute | solution.py:873
  163.4 4.5 %attention_back.1 = (f32[128,768]{1,0:T(8,128)}, bf16[128,768]{1,0:T(8,128)(2,1)}, bf16[128,576]{1,0:T(8,128)(2,1)}, bf16[128,768]{1,0:T(8,128)(2,1)S(1)}, bf16[...) custom-call(bf16[136,768]{1,0:T(8,128)(2,1)S(1)} %get-tuple-element.269.refs_0_, ...), custom_call_target="tpu_custom_call" | custom-call | tf_op jit(solution)/shard_map/attention_back/pallas_call | solution.py:132
  169.8 2.7 collective-permute-start.22
  172.5 3.8 %weight_grads.1 = f32[768,896]{1,0:T(8,128)} custom-call(bf16[128,768]{1,0:T(8,128)(2,1)} %get-tuple-element.297.refs_0_, bf16[128,576]{1,0:T(8,128)(2,1)} %get-tuple-element.298.refs_1_, bf16[128,192]{1,0:T(8,128)(2,1)} %get-tuple-element.299.refs_2_, bf16[128,768]{1,0:T(8,128)(2,1)} %get-tuple-element.300.refs_3_, ...), custom_call_target="tpu_custom_call" | custom-call | tf_op jit(solution)/shard_map/weight_grads/pallas_call | solution.py:132
  177.5 4.8 %expert_grads_top.1 = (f32[2,1,768,768]{3,2,1,0:T(8,128)}, f32[2,1,768,768]{3,2,1,0:T(8,128)}) custom-call(bf16[384,768]{1,0:T(8,128)(2,1)} %get-tuple-element.274.rows_ref, bf16[384,768]{1,0:T(8,128)(2,1)} %get-tuple-element.275.active_ref, bf16[384,768]{1,0:T(8,128)(2,1)} %get-tuple-element.276.grads_ref, bf16[384,768]{1,0:T(8,128)(2,1)} %get-tuple-element.277.down_ref), custom_call_target="tpu_custom_call" | custom-call | tf_op jit(solution)/shard_map/expert_grads_top/pallas_call | solution.py:148
  183.5 89.9 %while.16 = (s32[]{:T(128)}, f32[2,1,768,768]{3,2,1,0:T(8,128)}, f32[2,1,768,768]{3,2,1,0:T(8,128)}, f32[128,768]{1,0:T(8,128)}, bf16[768,896]{1,0:T(8,128)(2,1)...) while((s32[]{:T(128)}, f32[2,1,768,768]{3,2,1,0:T(8,128)}, ...), condition=%wide.region_1.0_spmd, body=%wide.region_0.0_spmd.sunk | while | flops 2 | bytes 19268428 | solution.py:1115
  183.5 3.1 %start_back.1 = (f32[128,768]{1,0:T(8,128)}, f32[1,768]{1,0:T(1,128)}, bf16[8,128]{1,0:T(8,128)(2,1)S(1)}, bf16[256,1152]{1,0:T(8,128)(2,1)S(1)}) custom-call(f32[128,768]{1,0:T(8,128)} %get-tuple-element.647.refs_0_, bf16[128,768]{1,0:T(8,128)(2,1)S(1)} %get-tuple-element.683.refs_1_, bf16[128,768]{1,0:T(8,128)(2,1)S(1)} %get-tuple-element.684.refs_2_, ...), custom_call_target="tpu_custom_call" | custom-call | tf_op jit(solution)/shard_map/while/body/start_back/pallas_call | solution.py:132
  186.7 17.7 %all_to_all.89 = bf16[32,8,1152]{2,1,0:T(8,128)(2,1)S(1)} all-to-all(bf16[32,8,1152]{2,1,0:T(8,128)(2,1)S(1)} %bitcast.42), channel_id=1, replica_groups=mesh['expert'=32,'tensor'=4] {'expert'}, dimensions={0} | all-to-all | bytes 1179648 | tf_op jit(solution)/shard_map/while/body/all_to_all | solution.py:879
  204.5 3.5 %expert_backward.1 = (bf16[384,768]{1,0:T(8,128)(2,1)}, bf16[384,768]{1,0:T(8,128)(2,1)}, bf16[256,1152]{1,0:T(8,128)(2,1)S(1)}) custom-call(bf16[256,1152]{1,0:T(8,128)(2,1)S(1)} %bitcast.40, bf16[2,768,768]{2,1,0:T(8,128)(2,1)} %get-tuple-element.692.refs_1_, bf16[384,768]{1,0:T(8,128)(2,1)} %get-tuple-element.693.refs_2_, ...), custom_call_target="tpu_custom_call" | custom-call | tf_op jit(solution)/shard_map/while/body/expert_backward/pallas_call | solution.py:132
  208.0 17.4 %all_to_all.90 = bf16[32,8,1152]{2,1,0:T(8,128)(2,1)S(1)} all-to-all(bf16[32,8,1152]{2,1,0:T(8,128)(2,1)S(1)} %bitcast.43), channel_id=1, replica_groups=mesh['expert'=32,'tensor'=4] {'expert'}, dimensions={0} | all-to-all | bytes 1179648 | tf_op jit(solution)/shard_map/while/body/all_to_all | solution.py:879
  227.2 2.5 collective-permute-start.2
  229.7 4.8 %expert_grads_low.1 = (f32[2,1,768,768]{3,2,1,0:T(8,128)}, f32[2,1,768,768]{3,2,1,0:T(8,128)}) custom-call(bf16[384,768]{1,0:T(8,128)(2,1)} %get-tuple-element.696.rows_ref, bf16[384,768]{1,0:T(8,128)(2,1)} %get-tuple-element.697.active_ref, bf16[384,768]{1,0:T(8,128)(2,1)} %get-tuple-element.595.grads_ref, ...), custom_call_target="tpu_custom_call", output_to_operand_aliasing={{0}: (4, {}), {1}: (5, {})} | custom-call | tf_op jit(solution)/shard_map/while/body/expert_grads_low/pallas_call | solution.py:148
  234.5 4.2 %collective-permute-done.refs_1_ = bf16[136,768]{1,0:T(8,128)(2,1)S(1)} collective-permute-done((bf16[136,768]{1,0:T(8,128)(2,1)S(1)}, bf16[136,768]{1,0:T(8,128)(2,1)S(1)}, u32[]{:S(2)}, u32[]{:S(2)}) %collective-permute-start) | collective-permute-done | bytes 208928 | tf_op jit(solution)/shard_map/while/body/ppermute | solution.py:873
  239.1 6.7 %attention_back_low.1 = (f32[128,768]{1,0:T(8,128)}, bf16[128,768]{1,0:T(8,128)(2,1)S(1)}, bf16[768,896]{1,0:T(8,128)(2,1)}) custom-call(bf16[136,768]{1,0:T(8,128)(2,1)S(1)} %combine_back.1.refs_0_, bf16[136,768]{1,0:T(8,128)(2,1)S(1)} %collective-permute-done.refs_1_, bf16[136,768]{1,0:T(8,128)(2,1)S(1)} %collective-permute-done.1.refs_2_, ...), custom_call_target="tpu_custom_call" | custom-call | tf_op jit(solution)/shard_map/while/body/attention_back_low/pallas_call | solution.py:132
  245.8 4.4 %all-to-all-start.2 = ((bf16[32,24,896]{2,1,0:T(8,128)(2,1)}), bf16[32,24,896]{2,1,0:T(8,128)(2,1)S(1)}, u32[]{:S(2)}, u32[]{:S(2)}) async-start(bf16[32,24,896]{2,1,0:T(8,128)(2,1)} %bitcast.59), calls=%async_computation.2 | async-start | bytes 2752512 | tf_op jit(solution)/shard_map/while/body/all_to_all | solution.py:879
  251.4 2.4 collective-permute-start.4
  254.1 3.5 %collective-permute-done.3.refs_2_ = bf16[128,768]{1,0:T(8,128)(2,1)S(1)} collective-permute-done((bf16[128,768]{1,0:T(8,128)(2,1)S(1)}, bf16[128,768]{1,0:T(8,128)(2,1)S(1)}, u32[]{:S(2)}, u32[]{:S(2)}) %collective-permute-start.3) | collective-permute-done | bytes 196640 | tf_op jit(solution)/shard_map/while/body/ppermute | solution.py:873
  257.6 5.1 %collective-permute-done.4.refs_3_ = bf16[128,768]{1,0:T(8,128)(2,1)S(1)} collective-permute-done((bf16[128,768]{1,0:T(8,128)(2,1)S(1)}, bf16[128,768]{1,0:T(8,128)(2,1)S(1)}, u32[]{:S(2)}, u32[]{:S(2)}) %collective-permute-start.4) | collective-permute-done | bytes 196640 | tf_op jit(solution)/shard_map/while/body/ppermute | solution.py:873
  263.8 7.7 %all-to-all-done.2 = bf16[32,24,896]{2,1,0:T(8,128)(2,1)S(1)} async-done(((bf16[32,24,896]{2,1,0:T(8,128)(2,1)}), bf16[32,24,896]{2,1,0:T(8,128)(2,1)S(1)}, u32[]{:S(2)}, u32[]{:S(2)}) %all-to-all-start.2) | async-done | bytes 1376288 | tf_op jit(solution)/shard_map/while/body/all_to_all | solution.py:879
  273.4 4.5 %all-to-all-start.7 = ((bf16[32,24,896]{2,1,0:T(8,128)(2,1)}), bf16[32,24,896]{2,1,0:T(8,128)(2,1)S(1)}, u32[]{:S(2)}, u32[]{:S(2)}) async-start(bf16[32,24,896]{2,1,0:T(8,128)(2,1)} %bitcast.60), calls=%async_computation.7 | async-start | bytes 2752512 | tf_op jit(solution)/shard_map/all_to_all | solution.py:879
  279.2 2.4 collective-permute-start.16
  281.7 3.9 %collective-permute-done.15.refs_2_ = bf16[128,768]{1,0:T(8,128)(2,1)S(1)} collective-permute-done((bf16[128,768]{1,0:T(8,128)(2,1)S(1)}, bf16[128,768]{1,0:T(8,128)(2,1)S(1)}, u32[]{:S(2)}, u32[]{:S(2)}) %collective-permute-start.15) | collective-permute-done | bytes 196640 | tf_op jit(solution)/shard_map/ppermute | solution.py:873
  285.6 5.0 %collective-permute-done.16.refs_3_ = bf16[128,768]{1,0:T(8,128)(2,1)S(1)} collective-permute-done((bf16[128,768]{1,0:T(8,128)(2,1)S(1)}, bf16[128,768]{1,0:T(8,128)(2,1)S(1)}, u32[]{:S(2)}, u32[]{:S(2)}) %collective-permute-start.16) | collective-permute-done | bytes 196640 | tf_op jit(solution)/shard_map/ppermute | solution.py:873
  291.4 5.5 %all-reduce.2.cloned.1.call-done.grads_ref = f32[768,896]{1,0:T(8,128)} async-done(((f32[768,896]{1,0:T(8,128)}), f32[768,896]{1,0:T(8,128)}) %all-reduce.2.cloned.1.call-update) | async-done | bytes 2752528 | tf_op jit(solution)/shard_map/psum | solution.py:1039
  296.9 2.9 place_top.1
  300.0 2.4 place_low.1
  (78 shorter events, 24.6 us)
Async XLA Ops:
  7.2 18.9 %copy-start.8 = (bf16[128,768]{1,0:T(8,128)(2,1)S(1)}, bf16[128,768]{1,0:T(8,128)(2,1)}, u32[]{:S(2)}) copy-start(bf16[128,768]{1,0:T(8,128)(2,1)} %refs_0_.3) | copy-start | bytes 589828
  7.2 18.9 %copy-start.9 = (f32[2,2,768]{2,1,0:T(2,128)S(1)}, f32[2,2,768]{2,1,0:T(2,128)}, u32[]{:S(2)}) copy-start(f32[2,2,768]{2,1,0:T(2,128)} %refs_8_.3) | copy-start | bytes 36868
  7.2 289.7 %all-reduce.2.cloned.1.call-start = ((), (), s32[]{:S(2)}) async-start(), calls=%async_computation.8 | async-start | bytes 5505024 | tf_op jit(solution)/shard_map/psum | solution.py:1039
  9.3 40.3 %copy-start.3 = (f32[2,3,128,128]{3,2,1,0:T(8,128)}, f32[2,3,128,128]{3,2,1,0:T(8,128)S(1)}, u32[]{:S(2)}) copy-start(f32[2,3,128,128]{3,2,1,0:T(8,128)S(1)} %get-tuple-element.253.refs_3_.refs_7_) | copy-start | bytes 1179652
  9.3 40.3 %copy-start.6 = (bf16[2,1,768,768]{3,2,1,0:T(8,128)(2,1)S(1)}, bf16[2,1,768,768]{3,2,1,0:T(8,128)(2,1)}, u32[]{:S(2)}) copy-start(bf16[2,1,768,768]{3,2,1,0:T(8,128)(2,1)} %param.23) | copy-start | bytes 7077892
  9.3 40.3 %copy-start.7 = (bf16[2,1,768,768]{3,2,1,0:T(8,128)(2,1)S(1)}, bf16[2,1,768,768]{3,2,1,0:T(8,128)(2,1)}, u32[]{:S(2)}) copy-start(bf16[2,1,768,768]{3,2,1,0:T(8,128)(2,1)} %param.24) | copy-start | bytes 7077892
  12.7 8.1 %collective-permute-start.6 = (bf16[128,768]{1,0:T(8,128)(2,1)S(1)}, bf16[128,768]{1,0:T(8,128)(2,1)S(1)}, u32[]{:S(2)}, u32[]{:S(2)}) collective-permute-start(bf16[128,768]{1,0:T(8,128)(2,1)S(1)} %get-tuple-element.254.refs_1_), channel_id=1, source_target_pairs={{0,1},{1,2},{2,3},{3,0},{4,5},{5,6},{6,7},{7,4},{8,9},{9,10},{10,1... | collective-permute-start | bytes 589832 | tf_op jit(solution)/shard_map/ppermute | solution.py:873
  14.9 11.1 %collective-permute-start.7 = (bf16[128,768]{1,0:T(8,128)(2,1)S(1)}, bf16[128,768]{1,0:T(8,128)(2,1)S(1)}, u32[]{:S(2)}, u32[]{:S(2)}) collective-permute-start(bf16[128,768]{1,0:T(8,128)(2,1)S(1)} %get-tuple-element.254.refs_1_), channel_id=1, source_target_pairs={{0,2},{1,3},{2,0},{3,1},{4,6},{5,7},{6,4},{7,5},{8,10},{9,11},{10,... | collective-permute-start | bytes 589832 | tf_op jit(solution)/shard_map/ppermute | solution.py:873
  17.6 8.5 %collective-permute-start.8 = (bf16[128,768]{1,0:T(8,128)(2,1)S(1)}, bf16[128,768]{1,0:T(8,128)(2,1)S(1)}, u32[]{:S(2)}, u32[]{:S(2)}) collective-permute-start(bf16[128,768]{1,0:T(8,128)(2,1)S(1)} %get-tuple-element.254.refs_1_), channel_id=1, source_target_pairs={{0,3},{1,0},{2,1},{3,2},{4,7},{5,4},{6,5},{7,6},{8,11},{9,8},{10,9... | collective-permute-start | bytes 589832 | tf_op jit(solution)/shard_map/ppermute | solution.py:873
  67.8 30.8 %copy-start.1 = (bf16[128,768]{1,0:T(8,128)(2,1)S(1)}, bf16[128,768]{1,0:T(8,128)(2,1)}, u32[]{:S(2)}) copy-start(bf16[128,768]{1,0:T(8,128)(2,1)} %refs_9_.3) | copy-start | bytes 589828
  69.9 8.0 %collective-permute-start.9 = (bf16[128,768]{1,0:T(8,128)(2,1)S(1)}, bf16[128,768]{1,0:T(8,128)(2,1)S(1)}, u32[]{:S(2)}, u32[]{:S(2)}) collective-permute-start(bf16[128,768]{1,0:T(8,128)(2,1)S(1)} %get-tuple-element.261.refs_1_), channel_id=1, source_target_pairs={{0,1},{1,2},{2,3},{3,0},{4,5},{5,6},{6,7},{7,4},{8,9},{9,10},{10,1... | collective-permute-start | bytes 589832 | tf_op jit(solution)/shard_map/ppermute | solution.py:873
  70.9 11.5 %collective-permute-start.10 = (bf16[128,768]{1,0:T(8,128)(2,1)S(1)}, bf16[128,768]{1,0:T(8,128)(2,1)S(1)}, u32[]{:S(2)}, u32[]{:S(2)}) collective-permute-start(bf16[128,768]{1,0:T(8,128)(2,1)S(1)} %get-tuple-element.261.refs_1_), channel_id=1, source_target_pairs={{0,2},{1,3},{2,0},{3,1},{4,6},{5,7},{6,4},{7,5},{8,10},{9,11},{10,... | collective-permute-start | bytes 589832 | tf_op jit(solution)/shard_map/ppermute | solution.py:873
  73.0 9.5 %collective-permute-start.11 = (bf16[128,768]{1,0:T(8,128)(2,1)S(1)}, bf16[128,768]{1,0:T(8,128)(2,1)S(1)}, u32[]{:S(2)}, u32[]{:S(2)}) collective-permute-start(bf16[128,768]{1,0:T(8,128)(2,1)S(1)} %get-tuple-element.261.refs_1_), channel_id=1, source_target_pairs={{0,3},{1,0},{2,1},{3,2},{4,7},{5,4},{6,5},{7,6},{8,11},{9,8},{10,9... | collective-permute-start | bytes 589832 | tf_op jit(solution)/shard_map/ppermute | solution.py:873
  85.8 7.0 %collective-permute-start.12 = (bf16[128,768]{1,0:T(8,128)(2,1)S(1)}, bf16[128,768]{1,0:T(8,128)(2,1)S(1)}, u32[]{:S(2)}, u32[]{:S(2)}) collective-permute-start(bf16[128,768]{1,0:T(8,128)(2,1)S(1)} %get-tuple-element.263.refs_1_), channel_id=1, source_target_pairs={{0,1},{1,2},{2,3},{3,0},{4,5},{5,6},{6,7},{7,4},{8,9},{9,10},{10,1... | collective-permute-start | bytes 589832 | tf_op jit(solution)/shard_map/ppermute | solution.py:873
  87.5 11.1 %collective-permute-start.13 = (bf16[128,768]{1,0:T(8,128)(2,1)S(1)}, bf16[128,768]{1,0:T(8,128)(2,1)S(1)}, u32[]{:S(2)}, u32[]{:S(2)}) collective-permute-start(bf16[128,768]{1,0:T(8,128)(2,1)S(1)} %get-tuple-element.263.refs_1_), channel_id=1, source_target_pairs={{0,2},{1,3},{2,0},{3,1},{4,6},{5,7},{6,4},{7,5},{8,10},{9,11},{10,... | collective-permute-start | bytes 589832 | tf_op jit(solution)/shard_map/ppermute | solution.py:873
  89.8 8.8 %collective-permute-start.14 = (bf16[128,768]{1,0:T(8,128)(2,1)S(1)}, bf16[128,768]{1,0:T(8,128)(2,1)S(1)}, u32[]{:S(2)}, u32[]{:S(2)}) collective-permute-start(bf16[128,768]{1,0:T(8,128)(2,1)S(1)} %get-tuple-element.263.refs_1_), channel_id=1, source_target_pairs={{0,3},{1,0},{2,1},{3,2},{4,7},{5,4},{6,5},{7,6},{8,11},{9,8},{10,9... | collective-permute-start | bytes 589832 | tf_op jit(solution)/shard_map/ppermute | solution.py:873
  127.4 35.9 %copy-start.2 = (f32[128,768]{1,0:T(8,128)S(1)}, f32[128,768]{1,0:T(8,128)}, u32[]{:S(2)}) copy-start(f32[128,768]{1,0:T(8,128)} %get-tuple-element.264.refs_0_.refs_7_) | copy-start | bytes 1179652
  127.5 35.9 %copy-start.4 = (bf16[3,128,192]{2,1,0:T(8,128)(2,1)S(1)}, bf16[3,128,192]{2,1,0:T(8,128)(2,1)}, u32[]{:S(2)}) copy-start(bf16[3,128,192]{2,1,0:T(8,128)(2,1)} %get-tuple-element.270.refs_11_) | copy-start | bytes 442372
  127.5 35.9 %copy-start.5 = (f32[3,128,128]{2,1,0:T(8,128)S(1)}, f32[3,128,128]{2,1,0:T(8,128)}, u32[]{:S(2)}) copy-start(f32[3,128,128]{2,1,0:T(8,128)} %get-tuple-element.271.refs_12_) | copy-start | bytes 589828
  150.9 7.6 %collective-permute-start.18 = (bf16[136,768]{1,0:T(8,128)(2,1)S(1)}, bf16[136,768]{1,0:T(8,128)(2,1)S(1)}, u32[]{:S(2)}, u32[]{:S(2)}) collective-permute-start(bf16[136,768]{1,0:T(8,128)(2,1)S(1)} %get-tuple-element.269.refs_0_), channel_id=1, source_target_pairs={{0,1},{1,2},{2,3},{3,0},{4,5},{5,6},{6,7},{7,4},{8,9},{9,10},{10,1... | collective-permute-start | bytes 626696 | tf_op jit(solution)/shard_map/ppermute | solution.py:873
  151.8 11.6 %collective-permute-start.19 = (bf16[136,768]{1,0:T(8,128)(2,1)S(1)}, bf16[136,768]{1,0:T(8,128)(2,1)S(1)}, u32[]{:S(2)}, u32[]{:S(2)}) collective-permute-start(bf16[136,768]{1,0:T(8,128)(2,1)S(1)} %get-tuple-element.269.refs_0_), channel_id=1, source_target_pairs={{0,2},{1,3},{2,0},{3,1},{4,6},{5,7},{6,4},{7,5},{8,10},{9,11},{10,... | collective-permute-start | bytes 626696 | tf_op jit(solution)/shard_map/ppermute | solution.py:873
  154.0 9.4 %collective-permute-start.20 = (bf16[136,768]{1,0:T(8,128)(2,1)S(1)}, bf16[136,768]{1,0:T(8,128)(2,1)S(1)}, u32[]{:S(2)}, u32[]{:S(2)}) collective-permute-start(bf16[136,768]{1,0:T(8,128)(2,1)S(1)} %get-tuple-element.269.refs_0_), channel_id=1, source_target_pairs={{0,3},{1,0},{2,1},{3,2},{4,7},{5,4},{6,5},{7,6},{8,11},{9,8},{10,9... | collective-permute-start | bytes 626696 | tf_op jit(solution)/shard_map/ppermute | solution.py:873
  167.9 14.4 %collective-permute-start.21 = (bf16[128,768]{1,0:T(8,128)(2,1)S(1)}, bf16[128,768]{1,0:T(8,128)(2,1)S(1)}, u32[]{:S(2)}, u32[]{:S(2)}) collective-permute-start(bf16[128,768]{1,0:T(8,128)(2,1)S(1)} %get-tuple-element.617), channel_id=1, source_target_pairs={{0,1},{1,2},{2,3},{3,0},{4,5},{5,6},{6,7},{7,4},{8,9},{9,10},{10,1... | collective-permute-start | bytes 589832 | tf_op jit(solution)/shard_map/ppermute | solution.py:873
  169.8 12.5 %collective-permute-start.22 = (bf16[128,768]{1,0:T(8,128)(2,1)S(1)}, bf16[128,768]{1,0:T(8,128)(2,1)S(1)}, u32[]{:S(2)}, u32[]{:S(2)}) collective-permute-start(bf16[128,768]{1,0:T(8,128)(2,1)S(1)} %get-tuple-element.617), channel_id=1, source_target_pairs={{0,2},{1,3},{2,0},{3,1},{4,6},{5,7},{6,4},{7,5},{8,10},{9,11},{10,... | collective-permute-start | bytes 589832 | tf_op jit(solution)/shard_map/ppermute | solution.py:873
  172.5 9.8 %collective-permute-start.23 = (bf16[128,768]{1,0:T(8,128)(2,1)S(1)}, bf16[128,768]{1,0:T(8,128)(2,1)S(1)}, u32[]{:S(2)}, u32[]{:S(2)}) collective-permute-start(bf16[128,768]{1,0:T(8,128)(2,1)S(1)} %get-tuple-element.617), channel_id=1, source_target_pairs={{0,3},{1,0},{2,1},{3,2},{4,7},{5,4},{6,5},{7,6},{8,11},{9,8},{10,9... | collective-permute-start | bytes 589832 | tf_op jit(solution)/shard_map/ppermute | solution.py:873
  172.5 3.8 %copy-start.19 = (s32[255]{0:T(256)S(1)}, s32[255]{0:T(256)}, u32[]{:S(2)}) copy-start(s32[255]{0:T(256)} %param.17) | copy-start | bytes 3064
  183.5 3.2 %copy-start.15 = (bf16[128,768]{1,0:T(8,128)(2,1)}, bf16[128,768]{1,0:T(8,128)(2,1)S(1)}, u32[]{:S(2)}) copy-start(bf16[128,768]{1,0:T(8,128)(2,1)S(1)} %get-tuple-element.685.refs_3_) | copy-start | bytes 589828 | tf_op jit(solution)/shard_map/while
  183.5 3.2 %copy-start.17 = (bf16[128,768]{1,0:T(8,128)(2,1)}, bf16[128,768]{1,0:T(8,128)(2,1)S(1)}, u32[]{:S(2)}) copy-start(bf16[128,768]{1,0:T(8,128)(2,1)S(1)} %get-tuple-element.686.refs_4_) | copy-start | bytes 589828 | tf_op jit(solution)/shard_map/while
  183.5 24.4 %copy-start.11 = (bf16[128,768]{1,0:T(8,128)(2,1)}, bf16[128,768]{1,0:T(8,128)(2,1)S(1)}, u32[]{:S(2)}) copy-start(bf16[128,768]{1,0:T(8,128)(2,1)S(1)} %get-tuple-element.683.refs_1_) | copy-start | bytes 589828 | tf_op jit(solution)/shard_map/while
  183.5 24.4 %copy-start.13 = (bf16[128,768]{1,0:T(8,128)(2,1)}, bf16[128,768]{1,0:T(8,128)(2,1)S(1)}, u32[]{:S(2)}) copy-start(bf16[128,768]{1,0:T(8,128)(2,1)S(1)} %get-tuple-element.684.refs_2_) | copy-start | bytes 589828 | tf_op jit(solution)/shard_map/while
  225.8 12.9 %collective-permute-start = (bf16[136,768]{1,0:T(8,128)(2,1)S(1)}, bf16[136,768]{1,0:T(8,128)(2,1)S(1)}, u32[]{:S(2)}, u32[]{:S(2)}) collective-permute-start(bf16[136,768]{1,0:T(8,128)(2,1)S(1)} %combine_back.1.refs_0_), channel_id=1, source_target_pairs={{0,1},{1,2},{2,3},{3,0},{4,5},{5,6},{6,7},{7,4},{8,9},{9,10},{10,1... | collective-permute-start | bytes 626696 | tf_op jit(solution)/shard_map/while/body/ppermute | solution.py:873
  227.2 11.5 %collective-permute-start.1 = (bf16[136,768]{1,0:T(8,128)(2,1)S(1)}, bf16[136,768]{1,0:T(8,128)(2,1)S(1)}, u32[]{:S(2)}, u32[]{:S(2)}) collective-permute-start(bf16[136,768]{1,0:T(8,128)(2,1)S(1)} %combine_back.1.refs_0_), channel_id=1, source_target_pairs={{0,2},{1,3},{2,0},{3,1},{4,6},{5,7},{6,4},{7,5},{8,10},{9,11},{10,... | collective-permute-start | bytes 626696 | tf_op jit(solution)/shard_map/while/body/ppermute | solution.py:873
  227.2 11.8 %collective-permute-start.2 = (bf16[136,768]{1,0:T(8,128)(2,1)S(1)}, bf16[136,768]{1,0:T(8,128)(2,1)S(1)}, u32[]{:S(2)}, u32[]{:S(2)}) collective-permute-start(bf16[136,768]{1,0:T(8,128)(2,1)S(1)} %combine_back.1.refs_0_), channel_id=1, source_target_pairs={{0,3},{1,0},{2,1},{3,2},{4,7},{5,4},{6,5},{7,6},{8,11},{9,8},{10,9... | collective-permute-start | bytes 626696 | tf_op jit(solution)/shard_map/while/body/ppermute | solution.py:873
  229.7 9.4 %copy-start.10 = (f32[2,2,768]{2,1,0:T(2,128)S(1)}, f32[2,2,768]{2,1,0:T(2,128)}, u32[]{:S(2)}) copy-start(f32[2,2,768]{2,1,0:T(2,128)} %get-tuple-element.794) | copy-start | bytes 36868 | tf_op jit(solution)/shard_map/while
  245.7 17.0 %copy-start = (f32[128,768]{1,0:T(8,128)S(1)}, f32[128,768]{1,0:T(8,128)}, u32[]{:S(2)}) copy-start(f32[128,768]{1,0:T(8,128)} %get-tuple-element.606.refs_0_) | copy-start | bytes 1179652 | tf_op jit(solution)/shard_map/while
  245.8 25.7 %all-to-all-start.2 = ((bf16[32,24,896]{2,1,0:T(8,128)(2,1)}), bf16[32,24,896]{2,1,0:T(8,128)(2,1)S(1)}, u32[]{:S(2)}, u32[]{:S(2)}) async-start(bf16[32,24,896]{2,1,0:T(8,128)(2,1)} %bitcast.59), calls=%async_computation.2 | async-start | bytes 2752512 | tf_op jit(solution)/shard_map/while/body/all_to_all | solution.py:879
  250.2 7.4 %collective-permute-start.3 = (bf16[128,768]{1,0:T(8,128)(2,1)S(1)}, bf16[128,768]{1,0:T(8,128)(2,1)S(1)}, u32[]{:S(2)}, u32[]{:S(2)}) collective-permute-start(bf16[128,768]{1,0:T(8,128)(2,1)S(1)} %get-tuple-element.607.refs_1_), channel_id=1, source_target_pairs={{0,1},{1,2},{2,3},{3,0},{4,5},{5,6},{6,7},{7,4},{8,9},{9,10},{10,1... | collective-permute-start | bytes 589832 | tf_op jit(solution)/shard_map/while/body/ppermute | solution.py:873
  251.4 11.3 %collective-permute-start.4 = (bf16[128,768]{1,0:T(8,128)(2,1)S(1)}, bf16[128,768]{1,0:T(8,128)(2,1)S(1)}, u32[]{:S(2)}, u32[]{:S(2)}) collective-permute-start(bf16[128,768]{1,0:T(8,128)(2,1)S(1)} %get-tuple-element.607.refs_1_), channel_id=1, source_target_pairs={{0,2},{1,3},{2,0},{3,1},{4,6},{5,7},{6,4},{7,5},{8,10},{9,11},{10,... | collective-permute-start | bytes 589832 | tf_op jit(solution)/shard_map/while/body/ppermute | solution.py:873
  253.8 8.9 %collective-permute-start.5 = (bf16[128,768]{1,0:T(8,128)(2,1)S(1)}, bf16[128,768]{1,0:T(8,128)(2,1)S(1)}, u32[]{:S(2)}, u32[]{:S(2)}) collective-permute-start(bf16[128,768]{1,0:T(8,128)(2,1)S(1)} %get-tuple-element.607.refs_1_), channel_id=1, source_target_pairs={{0,3},{1,0},{2,1},{3,2},{4,7},{5,4},{6,5},{7,6},{8,11},{9,8},{10,9... | collective-permute-start | bytes 589832 | tf_op jit(solution)/shard_map/while/body/ppermute | solution.py:873
  263.7 9.6 %copy-start.12 = (bf16[128,768]{1,0:T(8,128)(2,1)S(1)}, bf16[128,768]{1,0:T(8,128)(2,1)}, u32[]{:S(2)}) copy-start(bf16[128,768]{1,0:T(8,128)(2,1)} %copy-done.11) | copy-start | bytes 589828 | tf_op jit(solution)/shard_map/while
  263.8 9.6 %copy-start.14 = (bf16[128,768]{1,0:T(8,128)(2,1)S(1)}, bf16[128,768]{1,0:T(8,128)(2,1)}, u32[]{:S(2)}) copy-start(bf16[128,768]{1,0:T(8,128)(2,1)} %copy-done.13) | copy-start | bytes 589828 | tf_op jit(solution)/shard_map/while
  263.8 9.6 %copy-start.16 = (bf16[128,768]{1,0:T(8,128)(2,1)S(1)}, bf16[128,768]{1,0:T(8,128)(2,1)}, u32[]{:S(2)}) copy-start(bf16[128,768]{1,0:T(8,128)(2,1)} %copy-done.15) | copy-start | bytes 589828 | tf_op jit(solution)/shard_map/while
  263.8 9.6 %copy-start.18 = (bf16[128,768]{1,0:T(8,128)(2,1)S(1)}, bf16[128,768]{1,0:T(8,128)(2,1)}, u32[]{:S(2)}) copy-start(bf16[128,768]{1,0:T(8,128)(2,1)} %copy-done.17) | copy-start | bytes 589828 | tf_op jit(solution)/shard_map/while
  273.4 26.6 %all-to-all-start.7 = ((bf16[32,24,896]{2,1,0:T(8,128)(2,1)}), bf16[32,24,896]{2,1,0:T(8,128)(2,1)S(1)}, u32[]{:S(2)}, u32[]{:S(2)}) async-start(bf16[32,24,896]{2,1,0:T(8,128)(2,1)} %bitcast.60), calls=%async_computation.7 | async-start | bytes 2752512 | tf_op jit(solution)/shard_map/all_to_all | solution.py:879
  277.9 7.7 %collective-permute-start.15 = (bf16[128,768]{1,0:T(8,128)(2,1)S(1)}, bf16[128,768]{1,0:T(8,128)(2,1)S(1)}, u32[]{:S(2)}, u32[]{:S(2)}) collective-permute-start(bf16[128,768]{1,0:T(8,128)(2,1)S(1)} %get-tuple-element.268.refs_1_), channel_id=1, source_target_pairs={{0,1},{1,2},{2,3},{3,0},{4,5},{5,6},{6,7},{7,4},{8,9},{9,10},{10,1... | collective-permute-start | bytes 589832 | tf_op jit(solution)/shard_map/ppermute | solution.py:873
  279.2 11.4 %collective-permute-start.16 = (bf16[128,768]{1,0:T(8,128)(2,1)S(1)}, bf16[128,768]{1,0:T(8,128)(2,1)S(1)}, u32[]{:S(2)}, u32[]{:S(2)}) collective-permute-start(bf16[128,768]{1,0:T(8,128)(2,1)S(1)} %get-tuple-element.268.refs_1_), channel_id=1, source_target_pairs={{0,2},{1,3},{2,0},{3,1},{4,6},{5,7},{6,4},{7,5},{8,10},{9,11},{10,... | collective-permute-start | bytes 589832 | tf_op jit(solution)/shard_map/ppermute | solution.py:873
  281.6 9.0 %collective-permute-start.17 = (bf16[128,768]{1,0:T(8,128)(2,1)S(1)}, bf16[128,768]{1,0:T(8,128)(2,1)S(1)}, u32[]{:S(2)}, u32[]{:S(2)}) collective-permute-start(bf16[128,768]{1,0:T(8,128)(2,1)S(1)} %get-tuple-element.268.refs_1_), channel_id=1, source_target_pairs={{0,3},{1,0},{2,1},{3,2},{4,7},{5,4},{6,5},{7,6},{8,11},{9,8},{10,9... | collective-permute-start | bytes 589832 | tf_op jit(solution)/shard_map/ppermute | solution.py:873
Sparse Core Ops, SparseCore 0:
  176.5 120.3 all-reduce.1

commit v5 on v4

--- a/solution.py
+++ b/solution.py
@@ -59,8 +59,14 @@
 
 
 class Leaving:
-    def __init__(self, held, target, done):
-        self.held, self.copy, self.gone = held, pltpu.make_async_copy(held, target, done), False
+    def __init__(self, held, target, done, first, parts):
+        self.held, self.gone = held, [False] * len(parts)
+        self.copies = [
+            pltpu.make_async_copy(held.at[a:b], target.at[a:b], done.at[first + n])
+            if len(parts) > 1
+            else pltpu.make_async_copy(held, target, done.at[first])
+            for n, (a, b) in enumerate(parts)
+        ]
 
     @property
     def dtype(self):
@@ -72,10 +78,11 @@
     def __setitem__(self, index, value):
         self.held[index] = value
 
-    def go(self):
-        if not self.gone:
-            self.copy.start()
-            self.gone = True
+    def go(self, part=None):
+        for n, copy in enumerate(self.copies):
+            if part in (None, n) and not self.gone[n]:
+                copy.start()
+                self.gone[n] = True
 
 
 def go(*refs):
@@ -98,7 +105,9 @@
     shapes = [(o.shape, o.dtype) if isinstance(o, Kept) else o for o in outs]
     scratch = [pltpu.VMEM(p, a.dtype) for p, a, is_late in zip(parts, arrays, late) if is_late]
     scratch += [pltpu.VMEM(*o) for o, is_kept in zip(shapes, kept) if is_kept]
-    copies = len(scratch)
+    payload = (WIDTH, SUMMED)
+    cuts = [((0, 384), (384, 576), (576, 768)) if o[0] == payload else ((0, 0),) for o in shapes]
+    copies = sum(late) + sum(len(c) for c, is_kept in zip(cuts, kept) if is_kept)
     scratch += [pltpu.VMEM(*h) for h in held]
     if copies:
         scratch.append(pltpu.SemaphoreType.DMA((copies,)))
@@ -115,16 +124,19 @@
                 used += 1
             given.append(view)
         taken, leaving = [], []
-        for ref, is_kept in zip(refs[len(operands) : count], kept):
+        place = used
+        for ref, is_kept, parts_here in zip(refs[len(operands) : count], kept, cuts):
             if is_kept:
-                ref = Leaving(spare[used], ref, done.at[used])
+                ref = Leaving(spare[used], ref, done, place, parts_here)
                 leaving.append(ref)
                 used += 1
+                place += len(parts_here)
             taken.append(ref)
         body(*given, *taken, *spare[used:])
         go(*leaving)
         for ref in leaving:
-            ref.copy.wait()
+            for copy in ref.copies:
+                copy.wait()
         for view in given:
             if isinstance(view, Arriving):
                 view.wait()
@@ -648,8 +660,6 @@
 def fill_grads(low, back_triple, mixture, after, low_two, logits, gains, table, grads_ref):
     kind = grads_ref.dtype
     qkv_rows = 3 * QUARTER
-    grads_ref[:qkv_rows, :WIDTH] = dot(back_triple, low, 0).astype(kind)
-    grads_ref[qkv_rows:, :WIDTH] = dot(mixture, after, 0).astype(kind)
     both = dot(logits, low_two, 0)
     total = both[:EXPERTS] + both[EXPERTS : 2 * EXPERTS]
     parts = jnp.concatenate([total[:, r * 128 : (r + 1) * 128] for r in range(GROUPS)], axis=0)
@@ -662,6 +672,12 @@
         grads_ref[start : start + 8, WIDTH:] = folded(gain).astype(kind)
     start = 2 * SHARE + 8
     grads_ref[start : start + 8, WIDTH : WIDTH + EXPERTS] = table.astype(kind)
+    grads_ref[qkv_rows:, :WIDTH] = dot(mixture, after, 0).astype(kind)
+    grads_ref.go(2)
+    grads_ref[:384, :WIDTH] = dot(back_triple[:, :384], low, 0).astype(kind)
+    grads_ref.go(0)
+    grads_ref[384:qkv_rows, :WIDTH] = dot(back_triple[:, 384:], low, 0).astype(kind)
+    grads_ref.go(1)
 
 
 def weight_grads(

time: 312 us -> 311 us (level)
  transfers between devices with their start and end apart: 27 -> 27, of which waited for: 17 -> 16; matrix products, arithmetic and copies ran while one was open for 1% -> 1% of each run, Pallas kernels for 11% -> 11%
where the time goes in v5:
time: 311 us; the launch traced here: 309 us
  blocking collectives  118 us (38%)
  waiting for transfers between devices  68.1 us (22%)
  Pallas kernels  62 us (20%)
  starting transfers between devices  43.6 us (14%)
  between operations  15 us (5%)
    all_to_all x6, blocking collectives, across_experts(): return lax.all_to_all(values, 'expert', 0, 0, tiled=True)  118 us
    ppermute x24, waiting for transfers between devices, around(): lax.ppermute(values, 'tensor', [(i, (i + shift) % 4) for i in range(4)])  54.8 us
    pallas_call x18, Pallas kernels, call(): pl.pallas_call(kernel, out_shape=[pltpu.HBM(*o) if is_kept else jax.Shape...  47.1 us
    ppermute x24, starting transfers between devices, around(): lax.ppermute(values, 'tensor', [(i, (i + shift) % 4) for i in range(4)])  34.6 us
    pallas_call x2, Pallas kernels, call_stacked(): pl.pallas_call(body, grid=(1,), out_shape=[pltpu.HBM(stacked, f32)] * 2,...  9.59 us
    all_to_all x2, starting transfers between devices, across_experts(): return lax.all_to_all(values, 'expert', 0, 0, tiled=True)  8.97 us
    all_to_all x2, waiting for transfers between devices, across_experts(): return lax.all_to_all(values, 'expert', 0, 0, tiled=True)  7.65 us
  transfers between devices with their start and end apart: 27, of which 16 were waited for; matrix products, arithmetic and copies ran while one was open for 1% of the time, Pallas kernels for 11%

profile of v5, /device:TPU:1, one launch (start us, length us, event | category | flops | bytes accessed | tf_op | source)
XLA Modules:
  0.0 309.0 jit_solution(4955303722479008998)
XLA Ops:
  9.4 3.4 %attention_first.1 = (bf16[128,768]{1,0:T(8,128)(2,1)}, bf16[3,128,192]{2,1,0:T(8,128)(2,1)}, f32[3,128,128]{2,1,0:T(8,128)}, bf16[128,192]{1,0:T(8,128)(2,1)}, bf16[128,768]{1,0:T(8,128)(2,1)S(1)}) custom-call(bf16[128,768]{1,0:T(8,128)(2,1)} %refs_0_.3, f32[2,2,768]{2,1,0:T(2,128)} %refs_8_.3, bf16[2,3,192,768]{3,2,1,0:T(8,128)(2,1)} %bitcast.6.refs_2_.refs_6_.refs_13_, ...), custom_call_target="tpu_custom_call" | custom-call | tf_op jit(solution)/shard_map/attention_first/pallas_call | solution.py:144
  12.7 2.2 collective-permute-start.6
  14.9 2.6 collective-permute-start.7
  18.6 2.2 collective-permute-done.6.refs_2_
  20.9 5.2 %collective-permute-done.7.refs_3_ = bf16[128,768]{1,0:T(8,128)(2,1)S(1)} collective-permute-done((bf16[128,768]{1,0:T(8,128)(2,1)S(1)}, bf16[128,768]{1,0:T(8,128)(2,1)S(1)}, u32[]{:S(2)}, u32[]{:S(2)}) %collective-permute-start.7) | collective-permute-done | bytes 196640 | tf_op jit(solution)/shard_map/ppermute | solution.py:889
  28.1 21.5 %all_to_all.85 = bf16[32,8,1152]{2,1,0:T(8,128)(2,1)S(1)} all-to-all(bf16[32,8,1152]{2,1,0:T(8,128)(2,1)S(1)} %bitcast.51), channel_id=1, replica_groups=mesh['expert'=32,'tensor'=4] {'expert'}, dimensions={0} | all-to-all | bytes 1179648 | tf_op jit(solution)/shard_map/all_to_all | solution.py:895
  49.7 2.3 expert_forward.1
  52.0 15.8 %all_to_all.86 = bf16[32,8,1152]{2,1,0:T(8,128)(2,1)S(1)} all-to-all(bf16[32,8,1152]{2,1,0:T(8,128)(2,1)S(1)} %bitcast.52), channel_id=1, replica_groups=mesh['expert'=32,'tensor'=4] {'expert'}, dimensions={0} | all-to-all | bytes 1179648 | tf_op jit(solution)/shard_map/all_to_all | solution.py:895
  67.8 2.1 combine_first.1
  70.9 2.1 collective-permute-start.10
  74.3 3.5 %collective-permute-done.9.refs_2_ = bf16[128,768]{1,0:T(8,128)(2,1)S(1)} collective-permute-done((bf16[128,768]{1,0:T(8,128)(2,1)S(1)}, bf16[128,768]{1,0:T(8,128)(2,1)S(1)}, u32[]{:S(2)}, u32[]{:S(2)}) %collective-permute-start.9) | collective-permute-done | bytes 196640 | tf_op jit(solution)/shard_map/ppermute | solution.py:889
  77.8 4.6 %collective-permute-done.10.refs_3_ = bf16[128,768]{1,0:T(8,128)(2,1)S(1)} collective-permute-done((bf16[128,768]{1,0:T(8,128)(2,1)S(1)}, bf16[128,768]{1,0:T(8,128)(2,1)S(1)}, u32[]{:S(2)}, u32[]{:S(2)}) %collective-permute-start.10) | collective-permute-done | bytes 196640 | tf_op jit(solution)/shard_map/ppermute | solution.py:889
  82.5 3.4 %attention_next.1 = (f32[128,768]{1,0:T(8,128)}, bf16[128,768]{1,0:T(8,128)(2,1)}, bf16[3,128,192]{2,1,0:T(8,128)(2,1)}, f32[3,128,128]{2,1,0:T(8,128)}, bf16[12...) custom-call(f32[128,768]{1,0:T(8,128)} %get-tuple-element.633.refs_0_, bf16[128,768]{1,0:T(8,128)(2,1)S(1)} %get-tuple-element.261.refs_1_, ...), custom_call_target="tpu_custom_call" | custom-call | tf_op jit(solution)/shard_map/attention_next/pallas_call | solution.py:144
  87.5 2.3 collective-permute-start.13
  90.3 2.5 collective-permute-done.12.refs_2_
  92.8 5.8 %collective-permute-done.13.refs_3_ = bf16[128,768]{1,0:T(8,128)(2,1)S(1)} collective-permute-done((bf16[128,768]{1,0:T(8,128)(2,1)S(1)}, bf16[128,768]{1,0:T(8,128)(2,1)S(1)}, u32[]{:S(2)}, u32[]{:S(2)}) %collective-permute-start.13) | collective-permute-done | bytes 196640 | tf_op jit(solution)/shard_map/ppermute | solution.py:889
  98.6 2.2 route_next.1
  100.7 23.4 %all_to_all.87 = bf16[32,8,2304]{2,1,0:T(8,128)(2,1)S(1)} all-to-all(bf16[32,8,2304]{2,1,0:T(8,128)(2,1)S(1)} %bitcast.49), channel_id=1, replica_groups=mesh['expert'=32,'tensor'=4] {'expert'}, dimensions={0} | all-to-all | bytes 2359296 | tf_op jit(solution)/shard_map/all_to_all | solution.py:895
  124.2 3.3 %expert_both.1 = (bf16[384,768]{1,0:T(8,128)(2,1)}, bf16[384,768]{1,0:T(8,128)(2,1)}, bf16[384,768]{1,0:T(8,128)(2,1)}, bf16[384,768]{1,0:T(8,128)(2,1)}, bf16[256,2304]{1,0:T(8,128)(2,1)S(1)}) custom-call(bf16[256,2304]{1,0:T(8,128)(2,1)S(1)} %bitcast.46, bf16[2,768,768]{2,1,0:T(8,128)(2,1)S(1)} %bitcast.55, bf16[2,768,768]{2,1,0:T(8,128)(2,1)S(1)} %bitcast.58), custom_call_target="tpu_custom_call" | custom-call | tf_op jit(solution)/shard_map/expert_both/pallas_call | solution.py:144
  127.5 22.6 %all_to_all.88 = bf16[32,8,2304]{2,1,0:T(8,128)(2,1)S(1)} all-to-all(bf16[32,8,2304]{2,1,0:T(8,128)(2,1)S(1)} %bitcast.50), channel_id=1, replica_groups=mesh['expert'=32,'tensor'=4] {'expert'}, dimensions={0} | all-to-all | bytes 2359296 | tf_op jit(solution)/shard_map/all_to_all | solution.py:895
  151.8 2.2 collective-permute-start.19
  154.5 4.0 %collective-permute-done.18.refs_1_ = bf16[136,768]{1,0:T(8,128)(2,1)S(1)} collective-permute-done((bf16[136,768]{1,0:T(8,128)(2,1)S(1)}, bf16[136,768]{1,0:T(8,128)(2,1)S(1)}, u32[]{:S(2)}, u32[]{:S(2)}) %collective-permute-start.18) | collective-permute-done | bytes 208928 | tf_op jit(solution)/shard_map/ppermute | solution.py:889
  158.5 4.9 %collective-permute-done.19.refs_2_ = bf16[136,768]{1,0:T(8,128)(2,1)S(1)} collective-permute-done((bf16[136,768]{1,0:T(8,128)(2,1)S(1)}, bf16[136,768]{1,0:T(8,128)(2,1)S(1)}, u32[]{:S(2)}, u32[]{:S(2)}) %collective-permute-start.19) | collective-permute-done | bytes 208928 | tf_op jit(solution)/shard_map/ppermute | solution.py:889
  163.4 4.5 %attention_back.1 = (f32[128,768]{1,0:T(8,128)}, bf16[128,768]{1,0:T(8,128)(2,1)}, bf16[128,576]{1,0:T(8,128)(2,1)}, bf16[128,768]{1,0:T(8,128)(2,1)S(1)}, bf16[...) custom-call(bf16[136,768]{1,0:T(8,128)(2,1)S(1)} %get-tuple-element.269.refs_0_, ...), custom_call_target="tpu_custom_call" | custom-call | tf_op jit(solution)/shard_map/attention_back/pallas_call | solution.py:144
  169.8 2.7 collective-permute-start.22
  172.5 3.7 %weight_grads.1 = f32[768,896]{1,0:T(8,128)} custom-call(bf16[128,768]{1,0:T(8,128)(2,1)} %get-tuple-element.297.refs_0_, bf16[128,576]{1,0:T(8,128)(2,1)} %get-tuple-element.298.refs_1_, bf16[128,192]{1,0:T(8,128)(2,1)} %get-tuple-element.299.refs_2_, bf16[128,768]{1,0:T(8,128)(2,1)} %get-tuple-element.300.refs_3_, ...), custom_call_target="tpu_custom_call" | custom-call | tf_op jit(solution)/shard_map/weight_grads/pallas_call | solution.py:144
  177.4 4.8 %expert_grads_top.1 = (f32[2,1,768,768]{3,2,1,0:T(8,128)}, f32[2,1,768,768]{3,2,1,0:T(8,128)}) custom-call(bf16[384,768]{1,0:T(8,128)(2,1)} %get-tuple-element.274.rows_ref, bf16[384,768]{1,0:T(8,128)(2,1)} %get-tuple-element.275.active_ref, bf16[384,768]{1,0:T(8,128)(2,1)} %get-tuple-element.276.grads_ref, bf16[384,768]{1,0:T(8,128)(2,1)} %get-tuple-element.277.down_ref), custom_call_target="tpu_custom_call" | custom-call | tf_op jit(solution)/shard_map/expert_grads_top/pallas_call | solution.py:160
  183.4 89.8 %while.16 = (s32[]{:T(128)}, f32[2,1,768,768]{3,2,1,0:T(8,128)}, f32[2,1,768,768]{3,2,1,0:T(8,128)}, f32[128,768]{1,0:T(8,128)}, bf16[768,896]{1,0:T(8,128)(2,1)...) while((s32[]{:T(128)}, f32[2,1,768,768]{3,2,1,0:T(8,128)}, ...), condition=%wide.region_1.0_spmd, body=%wide.region_0.0_spmd.sunk | while | flops 2 | bytes 19268428 | solution.py:1131
  183.4 3.1 %start_back.1 = (f32[128,768]{1,0:T(8,128)}, f32[1,768]{1,0:T(1,128)}, bf16[8,128]{1,0:T(8,128)(2,1)S(1)}, bf16[256,1152]{1,0:T(8,128)(2,1)S(1)}) custom-call(f32[128,768]{1,0:T(8,128)} %get-tuple-element.647.refs_0_, bf16[128,768]{1,0:T(8,128)(2,1)S(1)} %get-tuple-element.683.refs_1_, bf16[128,768]{1,0:T(8,128)(2,1)S(1)} %get-tuple-element.684.refs_2_, ...), custom_call_target="tpu_custom_call" | custom-call | tf_op jit(solution)/shard_map/while/body/start_back/pallas_call | solution.py:144
  186.6 17.8 %all_to_all.89 = bf16[32,8,1152]{2,1,0:T(8,128)(2,1)S(1)} all-to-all(bf16[32,8,1152]{2,1,0:T(8,128)(2,1)S(1)} %bitcast.42), channel_id=1, replica_groups=mesh['expert'=32,'tensor'=4] {'expert'}, dimensions={0} | all-to-all | bytes 1179648 | tf_op jit(solution)/shard_map/while/body/all_to_all | solution.py:895
  204.4 3.5 %expert_backward.1 = (bf16[384,768]{1,0:T(8,128)(2,1)}, bf16[384,768]{1,0:T(8,128)(2,1)}, bf16[256,1152]{1,0:T(8,128)(2,1)S(1)}) custom-call(bf16[256,1152]{1,0:T(8,128)(2,1)S(1)} %bitcast.40, bf16[2,768,768]{2,1,0:T(8,128)(2,1)} %get-tuple-element.692.refs_1_, bf16[384,768]{1,0:T(8,128)(2,1)} %get-tuple-element.693.refs_2_, ...), custom_call_target="tpu_custom_call" | custom-call | tf_op jit(solution)/shard_map/while/body/expert_backward/pallas_call | solution.py:144
  207.9 17.3 %all_to_all.90 = bf16[32,8,1152]{2,1,0:T(8,128)(2,1)S(1)} all-to-all(bf16[32,8,1152]{2,1,0:T(8,128)(2,1)S(1)} %bitcast.43), channel_id=1, replica_groups=mesh['expert'=32,'tensor'=4] {'expert'}, dimensions={0} | all-to-all | bytes 1179648 | tf_op jit(solution)/shard_map/while/body/all_to_all | solution.py:895
  227.1 2.5 collective-permute-start.2
  229.6 4.8 %expert_grads_low.1 = (f32[2,1,768,768]{3,2,1,0:T(8,128)}, f32[2,1,768,768]{3,2,1,0:T(8,128)}) custom-call(bf16[384,768]{1,0:T(8,128)(2,1)} %get-tuple-element.696.rows_ref, bf16[384,768]{1,0:T(8,128)(2,1)} %get-tuple-element.697.active_ref, bf16[384,768]{1,0:T(8,128)(2,1)} %get-tuple-element.595.grads_ref, ...), custom_call_target="tpu_custom_call", output_to_operand_aliasing={{0}: (4, {}), {1}: (5, {})} | custom-call | tf_op jit(solution)/shard_map/while/body/expert_grads_low/pallas_call | solution.py:160
  234.4 4.2 %collective-permute-done.refs_1_ = bf16[136,768]{1,0:T(8,128)(2,1)S(1)} collective-permute-done((bf16[136,768]{1,0:T(8,128)(2,1)S(1)}, bf16[136,768]{1,0:T(8,128)(2,1)S(1)}, u32[]{:S(2)}, u32[]{:S(2)}) %collective-permute-start) | collective-permute-done | bytes 208928 | tf_op jit(solution)/shard_map/while/body/ppermute | solution.py:889
  238.9 6.6 %attention_back_low.1 = (f32[128,768]{1,0:T(8,128)}, bf16[128,768]{1,0:T(8,128)(2,1)S(1)}, bf16[768,896]{1,0:T(8,128)(2,1)}) custom-call(bf16[136,768]{1,0:T(8,128)(2,1)S(1)} %combine_back.1.refs_0_, bf16[136,768]{1,0:T(8,128)(2,1)S(1)} %collective-permute-done.refs_1_, bf16[136,768]{1,0:T(8,128)(2,1)S(1)} %collective-permute-done.1.refs_2_, ...), custom_call_target="tpu_custom_call" | custom-call | tf_op jit(solution)/shard_map/while/body/attention_back_low/pallas_call | solution.py:144
  245.5 4.4 %all-to-all-start.2 = ((bf16[32,24,896]{2,1,0:T(8,128)(2,1)}), bf16[32,24,896]{2,1,0:T(8,128)(2,1)S(1)}, u32[]{:S(2)}, u32[]{:S(2)}) async-start(bf16[32,24,896]{2,1,0:T(8,128)(2,1)} %bitcast.59), calls=%async_computation.2 | async-start | bytes 2752512 | tf_op jit(solution)/shard_map/while/body/all_to_all | solution.py:895
  251.2 2.4 collective-permute-start.4
  253.9 3.5 %collective-permute-done.3.refs_2_ = bf16[128,768]{1,0:T(8,128)(2,1)S(1)} collective-permute-done((bf16[128,768]{1,0:T(8,128)(2,1)S(1)}, bf16[128,768]{1,0:T(8,128)(2,1)S(1)}, u32[]{:S(2)}, u32[]{:S(2)}) %collective-permute-start.3) | collective-permute-done | bytes 196640 | tf_op jit(solution)/shard_map/while/body/ppermute | solution.py:889
  257.4 5.1 %collective-permute-done.4.refs_3_ = bf16[128,768]{1,0:T(8,128)(2,1)S(1)} collective-permute-done((bf16[128,768]{1,0:T(8,128)(2,1)S(1)}, bf16[128,768]{1,0:T(8,128)(2,1)S(1)}, u32[]{:S(2)}, u32[]{:S(2)}) %collective-permute-start.4) | collective-permute-done | bytes 196640 | tf_op jit(solution)/shard_map/while/body/ppermute | solution.py:889
  263.6 7.6 %all-to-all-done.2 = bf16[32,24,896]{2,1,0:T(8,128)(2,1)S(1)} async-done(((bf16[32,24,896]{2,1,0:T(8,128)(2,1)}), bf16[32,24,896]{2,1,0:T(8,128)(2,1)S(1)}, u32[]{:S(2)}, u32[]{:S(2)}) %all-to-all-start.2) | async-done | bytes 1376288 | tf_op jit(solution)/shard_map/while/body/all_to_all | solution.py:895
  273.2 4.5 %all-to-all-start.7 = ((bf16[32,24,896]{2,1,0:T(8,128)(2,1)}), bf16[32,24,896]{2,1,0:T(8,128)(2,1)S(1)}, u32[]{:S(2)}, u32[]{:S(2)}) async-start(bf16[32,24,896]{2,1,0:T(8,128)(2,1)} %bitcast.60), calls=%async_computation.7 | async-start | bytes 2752512 | tf_op jit(solution)/shard_map/all_to_all | solution.py:895
  279.0 2.4 collective-permute-start.16
  281.5 3.9 %collective-permute-done.15.refs_2_ = bf16[128,768]{1,0:T(8,128)(2,1)S(1)} collective-permute-done((bf16[128,768]{1,0:T(8,128)(2,1)S(1)}, bf16[128,768]{1,0:T(8,128)(2,1)S(1)}, u32[]{:S(2)}, u32[]{:S(2)}) %collective-permute-start.15) | collective-permute-done | bytes 196640 | tf_op jit(solution)/shard_map/ppermute | solution.py:889
  285.4 5.0 %collective-permute-done.16.refs_3_ = bf16[128,768]{1,0:T(8,128)(2,1)S(1)} collective-permute-done((bf16[128,768]{1,0:T(8,128)(2,1)S(1)}, bf16[128,768]{1,0:T(8,128)(2,1)S(1)}, u32[]{:S(2)}, u32[]{:S(2)}) %collective-permute-start.16) | collective-permute-done | bytes 196640 | tf_op jit(solution)/shard_map/ppermute | solution.py:889
  291.2 5.6 %all-reduce.2.cloned.1.call-done.grads_ref = f32[768,896]{1,0:T(8,128)} async-done(((f32[768,896]{1,0:T(8,128)}), f32[768,896]{1,0:T(8,128)}) %all-reduce.2.cloned.1.call-update) | async-done | bytes 2752528 | tf_op jit(solution)/shard_map/psum | solution.py:1055
  296.8 2.9 place_top.1
  299.7 2.4 place_low.1
  (78 shorter events, 24.4 us)
Async XLA Ops:
  7.2 18.9 %copy-start.8 = (bf16[128,768]{1,0:T(8,128)(2,1)S(1)}, bf16[128,768]{1,0:T(8,128)(2,1)}, u32[]{:S(2)}) copy-start(bf16[128,768]{1,0:T(8,128)(2,1)} %refs_0_.3) | copy-start | bytes 589828
  7.2 18.9 %copy-start.9 = (f32[2,2,768]{2,1,0:T(2,128)S(1)}, f32[2,2,768]{2,1,0:T(2,128)}, u32[]{:S(2)}) copy-start(f32[2,2,768]{2,1,0:T(2,128)} %refs_8_.3) | copy-start | bytes 36868
  7.2 289.6 %all-reduce.2.cloned.1.call-start = ((), (), s32[]{:S(2)}) async-start(), calls=%async_computation.8 | async-start | bytes 5505024 | tf_op jit(solution)/shard_map/psum | solution.py:1055
  9.3 40.3 %copy-start.3 = (f32[2,3,128,128]{3,2,1,0:T(8,128)}, f32[2,3,128,128]{3,2,1,0:T(8,128)S(1)}, u32[]{:S(2)}) copy-start(f32[2,3,128,128]{3,2,1,0:T(8,128)S(1)} %get-tuple-element.253.refs_3_.refs_7_) | copy-start | bytes 1179652
  9.3 40.3 %copy-start.6 = (bf16[2,1,768,768]{3,2,1,0:T(8,128)(2,1)S(1)}, bf16[2,1,768,768]{3,2,1,0:T(8,128)(2,1)}, u32[]{:S(2)}) copy-start(bf16[2,1,768,768]{3,2,1,0:T(8,128)(2,1)} %param.23) | copy-start | bytes 7077892
  9.3 40.3 %copy-start.7 = (bf16[2,1,768,768]{3,2,1,0:T(8,128)(2,1)S(1)}, bf16[2,1,768,768]{3,2,1,0:T(8,128)(2,1)}, u32[]{:S(2)}) copy-start(bf16[2,1,768,768]{3,2,1,0:T(8,128)(2,1)} %param.24) | copy-start | bytes 7077892
  12.7 8.1 %collective-permute-start.6 = (bf16[128,768]{1,0:T(8,128)(2,1)S(1)}, bf16[128,768]{1,0:T(8,128)(2,1)S(1)}, u32[]{:S(2)}, u32[]{:S(2)}) collective-permute-start(bf16[128,768]{1,0:T(8,128)(2,1)S(1)} %get-tuple-element.254.refs_1_), channel_id=1, source_target_pairs={{0,1},{1,2},{2,3},{3,0},{4,5},{5,6},{6,7},{7,4},{8,9},{9,10},{10,1... | collective-permute-start | bytes 589832 | tf_op jit(solution)/shard_map/ppermute | solution.py:889
  14.9 11.1 %collective-permute-start.7 = (bf16[128,768]{1,0:T(8,128)(2,1)S(1)}, bf16[128,768]{1,0:T(8,128)(2,1)S(1)}, u32[]{:S(2)}, u32[]{:S(2)}) collective-permute-start(bf16[128,768]{1,0:T(8,128)(2,1)S(1)} %get-tuple-element.254.refs_1_), channel_id=1, source_target_pairs={{0,2},{1,3},{2,0},{3,1},{4,6},{5,7},{6,4},{7,5},{8,10},{9,11},{10,... | collective-permute-start | bytes 589832 | tf_op jit(solution)/shard_map/ppermute | solution.py:889
  17.6 8.5 %collective-permute-start.8 = (bf16[128,768]{1,0:T(8,128)(2,1)S(1)}, bf16[128,768]{1,0:T(8,128)(2,1)S(1)}, u32[]{:S(2)}, u32[]{:S(2)}) collective-permute-start(bf16[128,768]{1,0:T(8,128)(2,1)S(1)} %get-tuple-element.254.refs_1_), channel_id=1, source_target_pairs={{0,3},{1,0},{2,1},{3,2},{4,7},{5,4},{6,5},{7,6},{8,11},{9,8},{10,9... | collective-permute-start | bytes 589832 | tf_op jit(solution)/shard_map/ppermute | solution.py:889
  67.8 30.8 %copy-start.1 = (bf16[128,768]{1,0:T(8,128)(2,1)S(1)}, bf16[128,768]{1,0:T(8,128)(2,1)}, u32[]{:S(2)}) copy-start(bf16[128,768]{1,0:T(8,128)(2,1)} %refs_9_.3) | copy-start | bytes 589828
  69.9 8.0 %collective-permute-start.9 = (bf16[128,768]{1,0:T(8,128)(2,1)S(1)}, bf16[128,768]{1,0:T(8,128)(2,1)S(1)}, u32[]{:S(2)}, u32[]{:S(2)}) collective-permute-start(bf16[128,768]{1,0:T(8,128)(2,1)S(1)} %get-tuple-element.261.refs_1_), channel_id=1, source_target_pairs={{0,1},{1,2},{2,3},{3,0},{4,5},{5,6},{6,7},{7,4},{8,9},{9,10},{10,1... | collective-permute-start | bytes 589832 | tf_op jit(solution)/shard_map/ppermute | solution.py:889
  70.9 11.5 %collective-permute-start.10 = (bf16[128,768]{1,0:T(8,128)(2,1)S(1)}, bf16[128,768]{1,0:T(8,128)(2,1)S(1)}, u32[]{:S(2)}, u32[]{:S(2)}) collective-permute-start(bf16[128,768]{1,0:T(8,128)(2,1)S(1)} %get-tuple-element.261.refs_1_), channel_id=1, source_target_pairs={{0,2},{1,3},{2,0},{3,1},{4,6},{5,7},{6,4},{7,5},{8,10},{9,11},{10,... | collective-permute-start | bytes 589832 | tf_op jit(solution)/shard_map/ppermute | solution.py:889
  73.0 9.5 %collective-permute-start.11 = (bf16[128,768]{1,0:T(8,128)(2,1)S(1)}, bf16[128,768]{1,0:T(8,128)(2,1)S(1)}, u32[]{:S(2)}, u32[]{:S(2)}) collective-permute-start(bf16[128,768]{1,0:T(8,128)(2,1)S(1)} %get-tuple-element.261.refs_1_), channel_id=1, source_target_pairs={{0,3},{1,0},{2,1},{3,2},{4,7},{5,4},{6,5},{7,6},{8,11},{9,8},{10,9... | collective-permute-start | bytes 589832 | tf_op jit(solution)/shard_map/ppermute | solution.py:889
  85.8 7.0 %collective-permute-start.12 = (bf16[128,768]{1,0:T(8,128)(2,1)S(1)}, bf16[128,768]{1,0:T(8,128)(2,1)S(1)}, u32[]{:S(2)}, u32[]{:S(2)}) collective-permute-start(bf16[128,768]{1,0:T(8,128)(2,1)S(1)} %get-tuple-element.263.refs_1_), channel_id=1, source_target_pairs={{0,1},{1,2},{2,3},{3,0},{4,5},{5,6},{6,7},{7,4},{8,9},{9,10},{10,1... | collective-permute-start | bytes 589832 | tf_op jit(solution)/shard_map/ppermute | solution.py:889
  87.5 11.1 %collective-permute-start.13 = (bf16[128,768]{1,0:T(8,128)(2,1)S(1)}, bf16[128,768]{1,0:T(8,128)(2,1)S(1)}, u32[]{:S(2)}, u32[]{:S(2)}) collective-permute-start(bf16[128,768]{1,0:T(8,128)(2,1)S(1)} %get-tuple-element.263.refs_1_), channel_id=1, source_target_pairs={{0,2},{1,3},{2,0},{3,1},{4,6},{5,7},{6,4},{7,5},{8,10},{9,11},{10,... | collective-permute-start | bytes 589832 | tf_op jit(solution)/shard_map/ppermute | solution.py:889
  89.8 8.8 %collective-permute-start.14 = (bf16[128,768]{1,0:T(8,128)(2,1)S(1)}, bf16[128,768]{1,0:T(8,128)(2,1)S(1)}, u32[]{:S(2)}, u32[]{:S(2)}) collective-permute-start(bf16[128,768]{1,0:T(8,128)(2,1)S(1)} %get-tuple-element.263.refs_1_), channel_id=1, source_target_pairs={{0,3},{1,0},{2,1},{3,2},{4,7},{5,4},{6,5},{7,6},{8,11},{9,8},{10,9... | collective-permute-start | bytes 589832 | tf_op jit(solution)/shard_map/ppermute | solution.py:889
  127.4 35.9 %copy-start.2 = (f32[128,768]{1,0:T(8,128)S(1)}, f32[128,768]{1,0:T(8,128)}, u32[]{:S(2)}) copy-start(f32[128,768]{1,0:T(8,128)} %get-tuple-element.264.refs_0_.refs_7_) | copy-start | bytes 1179652
  127.5 35.9 %copy-start.4 = (bf16[3,128,192]{2,1,0:T(8,128)(2,1)S(1)}, bf16[3,128,192]{2,1,0:T(8,128)(2,1)}, u32[]{:S(2)}) copy-start(bf16[3,128,192]{2,1,0:T(8,128)(2,1)} %get-tuple-element.270.refs_11_) | copy-start | bytes 442372
  127.5 35.9 %copy-start.5 = (f32[3,128,128]{2,1,0:T(8,128)S(1)}, f32[3,128,128]{2,1,0:T(8,128)}, u32[]{:S(2)}) copy-start(f32[3,128,128]{2,1,0:T(8,128)} %get-tuple-element.271.refs_12_) | copy-start | bytes 589828
  150.9 7.6 %collective-permute-start.18 = (bf16[136,768]{1,0:T(8,128)(2,1)S(1)}, bf16[136,768]{1,0:T(8,128)(2,1)S(1)}, u32[]{:S(2)}, u32[]{:S(2)}) collective-permute-start(bf16[136,768]{1,0:T(8,128)(2,1)S(1)} %get-tuple-element.269.refs_0_), channel_id=1, source_target_pairs={{0,1},{1,2},{2,3},{3,0},{4,5},{5,6},{6,7},{7,4},{8,9},{9,10},{10,1... | collective-permute-start | bytes 626696 | tf_op jit(solution)/shard_map/ppermute | solution.py:889
  151.8 11.6 %collective-permute-start.19 = (bf16[136,768]{1,0:T(8,128)(2,1)S(1)}, bf16[136,768]{1,0:T(8,128)(2,1)S(1)}, u32[]{:S(2)}, u32[]{:S(2)}) collective-permute-start(bf16[136,768]{1,0:T(8,128)(2,1)S(1)} %get-tuple-element.269.refs_0_), channel_id=1, source_target_pairs={{0,2},{1,3},{2,0},{3,1},{4,6},{5,7},{6,4},{7,5},{8,10},{9,11},{10,... | collective-permute-start | bytes 626696 | tf_op jit(solution)/shard_map/ppermute | solution.py:889
  154.0 9.4 %collective-permute-start.20 = (bf16[136,768]{1,0:T(8,128)(2,1)S(1)}, bf16[136,768]{1,0:T(8,128)(2,1)S(1)}, u32[]{:S(2)}, u32[]{:S(2)}) collective-permute-start(bf16[136,768]{1,0:T(8,128)(2,1)S(1)} %get-tuple-element.269.refs_0_), channel_id=1, source_target_pairs={{0,3},{1,0},{2,1},{3,2},{4,7},{5,4},{6,5},{7,6},{8,11},{9,8},{10,9... | collective-permute-start | bytes 626696 | tf_op jit(solution)/shard_map/ppermute | solution.py:889
  167.9 14.2 %collective-permute-start.21 = (bf16[128,768]{1,0:T(8,128)(2,1)S(1)}, bf16[128,768]{1,0:T(8,128)(2,1)S(1)}, u32[]{:S(2)}, u32[]{:S(2)}) collective-permute-start(bf16[128,768]{1,0:T(8,128)(2,1)S(1)} %get-tuple-element.617), channel_id=1, source_target_pairs={{0,1},{1,2},{2,3},{3,0},{4,5},{5,6},{6,7},{7,4},{8,9},{9,10},{10,1... | collective-permute-start | bytes 589832 | tf_op jit(solution)/shard_map/ppermute | solution.py:889
  169.8 12.4 %collective-permute-start.22 = (bf16[128,768]{1,0:T(8,128)(2,1)S(1)}, bf16[128,768]{1,0:T(8,128)(2,1)S(1)}, u32[]{:S(2)}, u32[]{:S(2)}) collective-permute-start(bf16[128,768]{1,0:T(8,128)(2,1)S(1)} %get-tuple-element.617), channel_id=1, source_target_pairs={{0,2},{1,3},{2,0},{3,1},{4,6},{5,7},{6,4},{7,5},{8,10},{9,11},{10,... | collective-permute-start | bytes 589832 | tf_op jit(solution)/shard_map/ppermute | solution.py:889
  172.5 9.7 %collective-permute-start.23 = (bf16[128,768]{1,0:T(8,128)(2,1)S(1)}, bf16[128,768]{1,0:T(8,128)(2,1)S(1)}, u32[]{:S(2)}, u32[]{:S(2)}) collective-permute-start(bf16[128,768]{1,0:T(8,128)(2,1)S(1)} %get-tuple-element.617), channel_id=1, source_target_pairs={{0,3},{1,0},{2,1},{3,2},{4,7},{5,4},{6,5},{7,6},{8,11},{9,8},{10,9... | collective-permute-start | bytes 589832 | tf_op jit(solution)/shard_map/ppermute | solution.py:889
  172.5 3.7 %copy-start.19 = (s32[255]{0:T(256)S(1)}, s32[255]{0:T(256)}, u32[]{:S(2)}) copy-start(s32[255]{0:T(256)} %param.17) | copy-start | bytes 3064
  183.4 3.2 %copy-start.15 = (bf16[128,768]{1,0:T(8,128)(2,1)}, bf16[128,768]{1,0:T(8,128)(2,1)S(1)}, u32[]{:S(2)}) copy-start(bf16[128,768]{1,0:T(8,128)(2,1)S(1)} %get-tuple-element.685.refs_3_) | copy-start | bytes 589828 | tf_op jit(solution)/shard_map/while
  183.4 3.2 %copy-start.17 = (bf16[128,768]{1,0:T(8,128)(2,1)}, bf16[128,768]{1,0:T(8,128)(2,1)S(1)}, u32[]{:S(2)}) copy-start(bf16[128,768]{1,0:T(8,128)(2,1)S(1)} %get-tuple-element.686.refs_4_) | copy-start | bytes 589828 | tf_op jit(solution)/shard_map/while
  183.4 24.5 %copy-start.11 = (bf16[128,768]{1,0:T(8,128)(2,1)}, bf16[128,768]{1,0:T(8,128)(2,1)S(1)}, u32[]{:S(2)}) copy-start(bf16[128,768]{1,0:T(8,128)(2,1)S(1)} %get-tuple-element.683.refs_1_) | copy-start | bytes 589828 | tf_op jit(solution)/shard_map/while
  183.4 24.5 %copy-start.13 = (bf16[128,768]{1,0:T(8,128)(2,1)}, bf16[128,768]{1,0:T(8,128)(2,1)S(1)}, u32[]{:S(2)}) copy-start(bf16[128,768]{1,0:T(8,128)(2,1)S(1)} %get-tuple-element.684.refs_2_) | copy-start | bytes 589828 | tf_op jit(solution)/shard_map/while
  225.7 12.9 %collective-permute-start = (bf16[136,768]{1,0:T(8,128)(2,1)S(1)}, bf16[136,768]{1,0:T(8,128)(2,1)S(1)}, u32[]{:S(2)}, u32[]{:S(2)}) collective-permute-start(bf16[136,768]{1,0:T(8,128)(2,1)S(1)} %combine_back.1.refs_0_), channel_id=1, source_target_pairs={{0,1},{1,2},{2,3},{3,0},{4,5},{5,6},{6,7},{7,4},{8,9},{9,10},{10,1... | collective-permute-start | bytes 626696 | tf_op jit(solution)/shard_map/while/body/ppermute | solution.py:889
  227.1 11.5 %collective-permute-start.1 = (bf16[136,768]{1,0:T(8,128)(2,1)S(1)}, bf16[136,768]{1,0:T(8,128)(2,1)S(1)}, u32[]{:S(2)}, u32[]{:S(2)}) collective-permute-start(bf16[136,768]{1,0:T(8,128)(2,1)S(1)} %combine_back.1.refs_0_), channel_id=1, source_target_pairs={{0,2},{1,3},{2,0},{3,1},{4,6},{5,7},{6,4},{7,5},{8,10},{9,11},{10,... | collective-permute-start | bytes 626696 | tf_op jit(solution)/shard_map/while/body/ppermute | solution.py:889
  227.1 11.8 %collective-permute-start.2 = (bf16[136,768]{1,0:T(8,128)(2,1)S(1)}, bf16[136,768]{1,0:T(8,128)(2,1)S(1)}, u32[]{:S(2)}, u32[]{:S(2)}) collective-permute-start(bf16[136,768]{1,0:T(8,128)(2,1)S(1)} %combine_back.1.refs_0_), channel_id=1, source_target_pairs={{0,3},{1,0},{2,1},{3,2},{4,7},{5,4},{6,5},{7,6},{8,11},{9,8},{10,9... | collective-permute-start | bytes 626696 | tf_op jit(solution)/shard_map/while/body/ppermute | solution.py:889
  229.6 9.4 %copy-start.10 = (f32[2,2,768]{2,1,0:T(2,128)S(1)}, f32[2,2,768]{2,1,0:T(2,128)}, u32[]{:S(2)}) copy-start(f32[2,2,768]{2,1,0:T(2,128)} %get-tuple-element.794) | copy-start | bytes 36868 | tf_op jit(solution)/shard_map/while
  245.5 17.0 %copy-start = (f32[128,768]{1,0:T(8,128)S(1)}, f32[128,768]{1,0:T(8,128)}, u32[]{:S(2)}) copy-start(f32[128,768]{1,0:T(8,128)} %get-tuple-element.606.refs_0_) | copy-start | bytes 1179652 | tf_op jit(solution)/shard_map/while
  245.5 25.7 %all-to-all-start.2 = ((bf16[32,24,896]{2,1,0:T(8,128)(2,1)}), bf16[32,24,896]{2,1,0:T(8,128)(2,1)S(1)}, u32[]{:S(2)}, u32[]{:S(2)}) async-start(bf16[32,24,896]{2,1,0:T(8,128)(2,1)} %bitcast.59), calls=%async_computation.2 | async-start | bytes 2752512 | tf_op jit(solution)/shard_map/while/body/all_to_all | solution.py:895
  250.0 7.4 %collective-permute-start.3 = (bf16[128,768]{1,0:T(8,128)(2,1)S(1)}, bf16[128,768]{1,0:T(8,128)(2,1)S(1)}, u32[]{:S(2)}, u32[]{:S(2)}) collective-permute-start(bf16[128,768]{1,0:T(8,128)(2,1)S(1)} %get-tuple-element.607.refs_1_), channel_id=1, source_target_pairs={{0,1},{1,2},{2,3},{3,0},{4,5},{5,6},{6,7},{7,4},{8,9},{9,10},{10,1... | collective-permute-start | bytes 589832 | tf_op jit(solution)/shard_map/while/body/ppermute | solution.py:889
  251.2 11.3 %collective-permute-start.4 = (bf16[128,768]{1,0:T(8,128)(2,1)S(1)}, bf16[128,768]{1,0:T(8,128)(2,1)S(1)}, u32[]{:S(2)}, u32[]{:S(2)}) collective-permute-start(bf16[128,768]{1,0:T(8,128)(2,1)S(1)} %get-tuple-element.607.refs_1_), channel_id=1, source_target_pairs={{0,2},{1,3},{2,0},{3,1},{4,6},{5,7},{6,4},{7,5},{8,10},{9,11},{10,... | collective-permute-start | bytes 589832 | tf_op jit(solution)/shard_map/while/body/ppermute | solution.py:889
  253.6 8.9 %collective-permute-start.5 = (bf16[128,768]{1,0:T(8,128)(2,1)S(1)}, bf16[128,768]{1,0:T(8,128)(2,1)S(1)}, u32[]{:S(2)}, u32[]{:S(2)}) collective-permute-start(bf16[128,768]{1,0:T(8,128)(2,1)S(1)} %get-tuple-element.607.refs_1_), channel_id=1, source_target_pairs={{0,3},{1,0},{2,1},{3,2},{4,7},{5,4},{6,5},{7,6},{8,11},{9,8},{10,9... | collective-permute-start | bytes 589832 | tf_op jit(solution)/shard_map/while/body/ppermute | solution.py:889
  263.5 9.6 %copy-start.12 = (bf16[128,768]{1,0:T(8,128)(2,1)S(1)}, bf16[128,768]{1,0:T(8,128)(2,1)}, u32[]{:S(2)}) copy-start(bf16[128,768]{1,0:T(8,128)(2,1)} %copy-done.11) | copy-start | bytes 589828 | tf_op jit(solution)/shard_map/while
  263.5 9.6 %copy-start.14 = (bf16[128,768]{1,0:T(8,128)(2,1)S(1)}, bf16[128,768]{1,0:T(8,128)(2,1)}, u32[]{:S(2)}) copy-start(bf16[128,768]{1,0:T(8,128)(2,1)} %copy-done.13) | copy-start | bytes 589828 | tf_op jit(solution)/shard_map/while
  263.5 9.6 %copy-start.16 = (bf16[128,768]{1,0:T(8,128)(2,1)S(1)}, bf16[128,768]{1,0:T(8,128)(2,1)}, u32[]{:S(2)}) copy-start(bf16[128,768]{1,0:T(8,128)(2,1)} %copy-done.15) | copy-start | bytes 589828 | tf_op jit(solution)/shard_map/while
  263.5 9.6 %copy-start.18 = (bf16[128,768]{1,0:T(8,128)(2,1)S(1)}, bf16[128,768]{1,0:T(8,128)(2,1)}, u32[]{:S(2)}) copy-start(bf16[128,768]{1,0:T(8,128)(2,1)} %copy-done.17) | copy-start | bytes 589828 | tf_op jit(solution)/shard_map/while
  273.2 26.5 %all-to-all-start.7 = ((bf16[32,24,896]{2,1,0:T(8,128)(2,1)}), bf16[32,24,896]{2,1,0:T(8,128)(2,1)S(1)}, u32[]{:S(2)}, u32[]{:S(2)}) async-start(bf16[32,24,896]{2,1,0:T(8,128)(2,1)} %bitcast.60), calls=%async_computation.7 | async-start | bytes 2752512 | tf_op jit(solution)/shard_map/all_to_all | solution.py:895
  277.7 7.7 %collective-permute-start.15 = (bf16[128,768]{1,0:T(8,128)(2,1)S(1)}, bf16[128,768]{1,0:T(8,128)(2,1)S(1)}, u32[]{:S(2)}, u32[]{:S(2)}) collective-permute-start(bf16[128,768]{1,0:T(8,128)(2,1)S(1)} %get-tuple-element.268.refs_1_), channel_id=1, source_target_pairs={{0,1},{1,2},{2,3},{3,0},{4,5},{5,6},{6,7},{7,4},{8,9},{9,10},{10,1... | collective-permute-start | bytes 589832 | tf_op jit(solution)/shard_map/ppermute | solution.py:889
  279.0 11.4 %collective-permute-start.16 = (bf16[128,768]{1,0:T(8,128)(2,1)S(1)}, bf16[128,768]{1,0:T(8,128)(2,1)S(1)}, u32[]{:S(2)}, u32[]{:S(2)}) collective-permute-start(bf16[128,768]{1,0:T(8,128)(2,1)S(1)} %get-tuple-element.268.refs_1_), channel_id=1, source_target_pairs={{0,2},{1,3},{2,0},{3,1},{4,6},{5,7},{6,4},{7,5},{8,10},{9,11},{10,... | collective-permute-start | bytes 589832 | tf_op jit(solution)/shard_map/ppermute | solution.py:889
  281.4 9.0 %collective-permute-start.17 = (bf16[128,768]{1,0:T(8,128)(2,1)S(1)}, bf16[128,768]{1,0:T(8,128)(2,1)S(1)}, u32[]{:S(2)}, u32[]{:S(2)}) collective-permute-start(bf16[128,768]{1,0:T(8,128)(2,1)S(1)} %get-tuple-element.268.refs_1_), channel_id=1, source_target_pairs={{0,3},{1,0},{2,1},{3,2},{4,7},{5,4},{6,5},{7,6},{8,11},{9,8},{10,9... | collective-permute-start | bytes 589832 | tf_op jit(solution)/shard_map/ppermute | solution.py:889
Sparse Core Ops, SparseCore 0:
  176.3 120.4 all-reduce.1
